TPU v7x, 512 devices: a whole 4x4x16 slice. The times are simulated.
512 devices in a mesh: gr: 16 (over y, z_hi, core), gc: 32 (over z_lo, x).
Axes of the slice: x: 4, y: 4, z: 16 (z_hi: 2, z_lo: 8; z = z_hi * 8 + z_lo), core: 2. Of those that a mesh axis runs over, the one named last changes fastest.
Arguments:
- grad: bfloat16 [640, 16384], P('gc', 'gr'), may hold values from -6 to 6
- basis: bfloat16 [16384, 16384], P('gr', 'gc'), may hold values from -0.046875 to 0.046875
- first_moment: float32 [640, 16384], P('gr', 'gc'), may hold values from -3 to 3
- second_moment: float32 [640, 16384], P('gr', 'gc'), may hold values from 0.001 to 0.1
Outputs:
- update: bfloat16 [640, 16384], P('gc', 'gr')
- new_first: float32 [640, 16384], P('gr', 'gc')
- new_second: float32 [640, 16384], P('gr', 'gc')
All inputs are finite; a program needn't handle non-finite values.
Results may differ from a plain program's by a relative error of at most 0.0049.
Values may be sent and summed in bfloat16 or wider, within the bound.
No kernel may reach another device: no remote copies, remote signals or barrier semaphores. Data moves between devices by JAX's collectives and lax.ppermute only.
A program may use at most 64 MiB of HBM per device.

v0:
```python
import jax
import jax.numpy as jnp
from jax import lax
from jax.sharding import PartitionSpec as P

STEP = 10


BETA_ONE = 0.9
BETA_TWO = 0.999
EPSILON = 1e-08


def adam_step(rotated, first_moment, second_moment):
    new_first = BETA_ONE * first_moment + (1.0 - BETA_ONE) * rotated
    new_second = BETA_TWO * second_moment + (1.0 - BETA_TWO) * rotated * rotated
    corr_one = 1.0 - BETA_ONE**STEP
    corr_two = 1.0 - BETA_TWO**STEP
    direction = (new_first / corr_one / (jnp.sqrt(new_second / corr_two) + EPSILON)).astype(
        jnp.bfloat16
    )
    return (direction, new_first, new_second)


def shards(grad, basis, first_moment, second_moment):
    all_rows = lax.all_gather(grad, "gc", axis=0, tiled=True)
    picked = all_rows
    rotated = lax.psum_scatter(
        jnp.dot(picked, basis, preferred_element_type=jnp.float32),
        "gr",
        scatter_dimension=0,
        tiled=True,
    )
    shares, new_first, new_second = adam_step(rotated, first_moment, second_moment)
    direction = lax.all_gather(shares, "gr", axis=0, tiled=True)
    picked = direction
    summed = lax.psum_scatter(
        lax.dot_general(
            picked, basis, (((1,), (1,)), ((), ())), preferred_element_type=jnp.float32
        ),
        "gc",
        scatter_dimension=0,
        tiled=True,
    )
    return (summed.astype(jnp.bfloat16), new_first, new_second)


def solution(mesh):
    in_specs = (P("gc", "gr"), P("gr", "gc"), P("gr", "gc"), P("gr", "gc"))
    out_specs = (P("gc", "gr"), P("gr", "gc"), P("gr", "gc"))
    return jax.shard_map(shards, mesh=mesh, in_specs=in_specs, out_specs=out_specs, check_vma=False)
```

profile of v0, /device:TPU:128, one launch (start us, length us, event | category | flops | bytes accessed | tf_op | source)
XLA Modules:
  0.0 561.9 jit_solution(6504536593139793854)
XLA Ops:
  7.2 0.0 copy-start
  7.2 0.0 all-gather.3.cloned.1.call-start
  7.2 0.7 all-gather.3.cloned.1.call-update
  7.9 0.0 reduce-scatter.4.cloned.1.call-start
  8.0 177.3 %all-gather.3.cloned.1.call-done = bf16[32,20,1024]{2,1,0:T(8,128)(2,1)} async-done(((bf16[1,20,1024]{2,1,0:T(8,128)(2,1)}), bf16[32,20,1024]{2,1,0:T(8,128)(2,1)}) %all-gather.3.cloned.1.call-update) | async-done | bytes 1310736 | tf_op jit(solution)/shard_map/all_gather | solution.py:26
  185.3 2.3 reshape.7
  187.6 0.0 copy-done
  187.6 0.0 copy-start.1
  187.6 0.0 copy-start.2
  187.6 1.9 fusion.4
  189.5 0.0 reduce-scatter.4.cloned.1.call-update
  189.6 153.8 %reduce-scatter.4.cloned.1.call-done = f32[40,512]{1,0:T(8,128)} async-done(((f32[640,512]{1,0:T(8,128)}), f32[40,512]{1,0:T(8,128)}) %reduce-scatter.4.cloned.1.call-update) | async-done | bytes 81936 | tf_op jit(solution)/shard_map/reduce_scatter | solution.py:28
  343.3 0.0 copy-done.2
  343.4 1.6 divide_convert_fusion
  344.9 45.7 %all_gather.7 = bf16[640,512]{1,0:T(8,128)(2,1)S(1)} all-gather(bf16[40,512]{1,0:T(8,128)(2,1)S(1)} %get-tuple-element.3), channel_id=1, replica_groups=mesh['gr'=16,'gc'=32] {'gr'}, dimensions={0}, use_global_device_ids=true | all-gather | bytes 696320 | tf_op jit(solution)/shard_map/all_gather | solution.py:35
  390.6 2.4 fusion.5
  393.0 94.9 %fusion = f32[24,1024]{1,0:T(8,128)S(1)} fusion(f32[640,1024]{1,0:T(8,128)} %fusion.5), kind=kCustom, calls=%all-reduce-scatter | all-reduce-scatter fusion | flops 786433 | bytes 2721792
  488.0 6.4 %collective-permute-start.5 = (bf16[4,1024]{1,0:T(4,128)(2,1)S(1)}, bf16[4,1024]{1,0:T(4,128)(2,1)S(1)}, u32[]{:S(2)}, u32[]{:S(2)}) collective-permute-start(bf16[4,1024]{1,0:T(4,128)(2,1)S(1)} %slice), channel_id=1, source_target_pairs={{0,6},{1,7},{2,8},{3,9},{4,10},{5,11},{6,12},{7,13},{8,14},{9,15},... | collective-permute-start | bytes 24584
  494.5 5.0 collective-permute-start
  499.4 12.9 %collective-permute-start.1 = (bf16[24,1024]{1,0:T(8,128)(2,1)S(1)}, bf16[24,1024]{1,0:T(8,128)(2,1)S(1)}, u32[]{:S(2)}, u32[]{:S(2)}) collective-permute-start(bf16[24,1024]{1,0:T(8,128)(2,1)S(1)} %convert.10), channel_id=1, source_target_pairs={{0,2},{1,3},{2,4},{3,5},{4,6},{5,7},{6,8},{7,9},{8,10},{9,11},{10,... | collective-permute-start | bytes 147464
  512.3 16.9 %collective-permute-start.2 = (bf16[24,1024]{1,0:T(8,128)(2,1)S(1)}, bf16[24,1024]{1,0:T(8,128)(2,1)S(1)}, u32[]{:S(2)}, u32[]{:S(2)}) collective-permute-start(bf16[24,1024]{1,0:T(8,128)(2,1)S(1)} %convert.10), channel_id=1, source_target_pairs={{0,3},{1,4},{2,5},{3,6},{4,7},{5,8},{6,9},{7,10},{8,11},{9,12},{10... | collective-permute-start | bytes 147464
  529.2 13.9 %collective-permute-start.3 = (bf16[24,1024]{1,0:T(8,128)(2,1)S(1)}, bf16[24,1024]{1,0:T(8,128)(2,1)S(1)}, u32[]{:S(2)}, u32[]{:S(2)}) collective-permute-start(bf16[24,1024]{1,0:T(8,128)(2,1)S(1)} %convert.10), channel_id=1, source_target_pairs={{0,4},{1,5},{2,6},{3,7},{4,8},{5,9},{6,10},{7,11},{8,12},{9,13},{1... | collective-permute-start | bytes 147464
  543.2 0.0 collective-permute-done.5
  543.2 1.9 collective-permute-start.4
  545.1 1.3 dynamic-slice.4
  547.0 0.0 collective-permute-done
  547.0 0.0 collective-permute-done.1
  547.1 0.0 collective-permute-done.2
  547.1 0.0 collective-permute-done.3
  547.1 6.3 %collective-permute-done.4 = bf16[24,1024]{1,0:T(8,128)(2,1)S(1)} collective-permute-done((bf16[24,1024]{1,0:T(8,128)(2,1)S(1)}, bf16[24,1024]{1,0:T(8,128)(2,1)S(1)}, u32[]{:S(2)}, u32[]{:S(2)}) %collective-permute-start.4) | collective-permute-done | bytes 49184
  553.4 1.0 concatenate
  554.4 0.6 dynamic-slice_convert_fusion
  (3 shorter events, 0.0 us)
Async XLA Ops:
  7.2 180.4 %copy-start = (bf16[1024,512]{1,0:T(8,128)(2,1)S(1)}, bf16[1024,512]{1,0:T(8,128)(2,1)}, u32[]{:S(2)}) copy-start(bf16[1024,512]{1,0:T(8,128)(2,1)} %param.5) | copy-start | bytes 3145732
  7.2 178.1 %all-gather.3.cloned.1.call-start = ((), (), s32[]{:S(2)}) async-start(), calls=%async_computation.2 | async-start | bytes 1622016 | tf_op jit(solution)/shard_map/all_gather | solution.py:26
  7.9 335.4 %reduce-scatter.4.cloned.1.call-start = ((), (), s32[]{:S(2)}) async-start(), calls=%async_computation.1 | async-start | bytes 1392640 | tf_op jit(solution)/shard_map/reduce_scatter | solution.py:28
  187.6 155.8 %copy-start.1 = (f32[40,512]{1,0:T(8,128)S(1)}, f32[40,512]{1,0:T(8,128)}, u32[]{:S(2)}) copy-start(f32[40,512]{1,0:T(8,128)} %param.6) | copy-start | bytes 245764
  187.6 155.8 %copy-start.2 = (f32[40,512]{1,0:T(8,128)S(1)}, f32[40,512]{1,0:T(8,128)}, u32[]{:S(2)}) copy-start(f32[40,512]{1,0:T(8,128)} %param.7) | copy-start | bytes 245764
  488.0 55.2 %collective-permute-start.5 = (bf16[4,1024]{1,0:T(4,128)(2,1)S(1)}, bf16[4,1024]{1,0:T(4,128)(2,1)S(1)}, u32[]{:S(2)}, u32[]{:S(2)}) collective-permute-start(bf16[4,1024]{1,0:T(4,128)(2,1)S(1)} %slice), channel_id=1, source_target_pairs={{0,6},{1,7},{2,8},{3,9},{4,10},{5,11},{6,12},{7,13},{8,14},{9,15},... | collective-permute-start | bytes 24584
  494.5 52.6 %collective-permute-start = (bf16[24,1024]{1,0:T(8,128)(2,1)S(1)}, bf16[24,1024]{1,0:T(8,128)(2,1)S(1)}, u32[]{:S(2)}, u32[]{:S(2)}) collective-permute-start(bf16[24,1024]{1,0:T(8,128)(2,1)S(1)} %convert.10), channel_id=1, source_target_pairs={{0,1},{1,2},{2,3},{3,4},{4,5},{5,6},{6,7},{7,8},{8,9},{9,10},{10,1... | collective-permute-start | bytes 147464
  499.4 47.6 %collective-permute-start.1 = (bf16[24,1024]{1,0:T(8,128)(2,1)S(1)}, bf16[24,1024]{1,0:T(8,128)(2,1)S(1)}, u32[]{:S(2)}, u32[]{:S(2)}) collective-permute-start(bf16[24,1024]{1,0:T(8,128)(2,1)S(1)} %convert.10), channel_id=1, source_target_pairs={{0,2},{1,3},{2,4},{3,5},{4,6},{5,7},{6,8},{7,9},{8,10},{9,11},{10,... | collective-permute-start | bytes 147464
  512.3 34.7 %collective-permute-start.2 = (bf16[24,1024]{1,0:T(8,128)(2,1)S(1)}, bf16[24,1024]{1,0:T(8,128)(2,1)S(1)}, u32[]{:S(2)}, u32[]{:S(2)}) collective-permute-start(bf16[24,1024]{1,0:T(8,128)(2,1)S(1)} %convert.10), channel_id=1, source_target_pairs={{0,3},{1,4},{2,5},{3,6},{4,7},{5,8},{6,9},{7,10},{8,11},{9,12},{10... | collective-permute-start | bytes 147464
  529.2 17.8 %collective-permute-start.3 = (bf16[24,1024]{1,0:T(8,128)(2,1)S(1)}, bf16[24,1024]{1,0:T(8,128)(2,1)S(1)}, u32[]{:S(2)}, u32[]{:S(2)}) collective-permute-start(bf16[24,1024]{1,0:T(8,128)(2,1)S(1)} %convert.10), channel_id=1, source_target_pairs={{0,4},{1,5},{2,6},{3,7},{4,8},{5,9},{6,10},{7,11},{8,12},{9,13},{1... | collective-permute-start | bytes 147464
  543.2 10.2 %collective-permute-start.4 = (bf16[24,1024]{1,0:T(8,128)(2,1)S(1)}, bf16[24,1024]{1,0:T(8,128)(2,1)S(1)}, u32[]{:S(2)}, u32[]{:S(2)}) collective-permute-start(bf16[24,1024]{1,0:T(8,128)(2,1)S(1)} %convert.10), channel_id=1, source_target_pairs={{0,5},{1,6},{2,7},{3,8},{4,9},{5,10},{6,11},{7,12},{8,13},{9,14},{... | collective-permute-start | bytes 147464
Sparse Core Ops, SparseCore 0:
  10.1 175.1 all-gather.2
  190.0 153.3 reduce-scatter.3
where the time goes:
time: 562 us
  waiting for transfers between devices  338 us (60%)
  blocking collectives  141 us (25%)
  starting transfers between devices  57.1 us (10%)
  between operations  14.9 us (3%)
    all_gather x1, waiting for transfers between devices, shards(): all_rows = lax.all_gather(grad, 'gc', axis=0, tiled=True)  177 us
    reduce_scatter x1, waiting for transfers between devices, shards(): lax.psum_scatter(jnp.dot(picked, basis, preferred_element_type=jnp.float3...  154 us
    unnamed x1, blocking collectives  94.9 us
    unnamed x6, starting transfers between devices  57.1 us
    all_gather x1, blocking collectives, shards(): direction = lax.all_gather(shares, 'gr', axis=0, tiled=True)  45.7 us
  transfers between devices with their start and end apart: 8, of which 3 were waited for; matrix products, arithmetic and copies ran while one was open for 0% of the time, Pallas kernels for 0%

commit v1 on v0

v1 whole, which is shorter than its diff:
```python
import jax
import jax.numpy as jnp
from jax import lax
from jax.sharding import Mesh
from jax.sharding import PartitionSpec as P

STEP = 10


BETA_ONE = 0.9
BETA_TWO = 0.999
EPSILON = 1e-08

F32, BF16 = jnp.float32, jnp.bfloat16
LANES = 128
SIZES = {"y": 4, "zh": 2, "core": 2, "zf": 4, "zn": 2, "x": 4}
GR = ("y", "zh", "core")
GC = ("zf", "zn", "x")


def adam_step(rotated, first_moment, second_moment):
    new_first = BETA_ONE * first_moment + (1.0 - BETA_ONE) * rotated
    new_second = BETA_TWO * second_moment + (1.0 - BETA_TWO) * rotated * rotated
    corr_one = 1.0 - BETA_ONE**STEP
    corr_two = 1.0 - BETA_TWO**STEP
    direction = (new_first / corr_one / (jnp.sqrt(new_second / corr_two) + EPSILON)).astype(BF16)
    return (direction, new_first, new_second)


def spread(block, axes, n):
    return lax.all_to_all(jnp.broadcast_to(block[None], (n,) + block.shape), axes, 0, 0, tiled=True)


def swap(value, axis):
    return lax.ppermute(value, axis, [(0, 1), (1, 0)])


def shards(grad, basis, first_moment, second_moment):
    zh = lax.axis_index("zh")
    rows, cols = grad.shape
    first_other = swap(first_moment, "zh")
    second_other = swap(second_moment, "zh")

    block = grad.reshape(rows, cols // LANES, LANES)
    block = spread(block, "zf", 4)
    block = spread(block, ("zn", "x"), 8)
    block = block.reshape(2, 2, 2, 4, rows, cols // LANES, LANES)
    picked = block.transpose(3, 1, 0, 2, 4, 5, 6).reshape(32 * rows, cols)

    partial = jnp.dot(picked, basis, preferred_element_type=F32).astype(BF16)
    parts = lax.all_to_all(partial.reshape(8, 80, -1), ("y", "core"), 0, 0, tiled=True)
    parts, first_other, second_other = lax.optimization_barrier((parts, first_other, second_other))
    part = jnp.sum(parts.astype(F32), axis=0)
    rotated = part + swap(part.astype(BF16), "zh").astype(F32)
    low, high = rotated[:40], rotated[40:]
    first = zh == 0
    mine, other = jnp.where(first, low, high), jnp.where(first, high, low)
    share, new_first, new_second = adam_step(mine, first_moment, second_moment)
    share_other, _, _ = adam_step(other, first_other, second_other)
    pair = jnp.concatenate(
        [jnp.where(first, share, share_other), jnp.where(first, share_other, share)], axis=0
    )
    direction = lax.all_gather(pair, ("y", "core"), axis=0, tiled=True)

    total = lax.dot_general(
        direction, basis, (((1,), (1,)), ((), ())), preferred_element_type=F32
    ).astype(BF16)
    total = total.reshape(4, 2, 2, 2, rows, cols // LANES, LANES)
    total = total.transpose(2, 1, 3, 0, 4, 5, 6).reshape(8, 4, rows, cols // LANES, LANES)
    total = lax.all_to_all(total, ("zn", "x"), 0, 0, tiled=True)
    total = jnp.sum(total.astype(F32), axis=0).astype(BF16)
    total = lax.all_to_all(total, "zf", 0, 0, tiled=True)
    update = jnp.sum(total.astype(F32), axis=0).astype(BF16).reshape(rows, cols)
    return (update, new_first, new_second)


def solution(mesh):
    fine = Mesh(mesh.devices.reshape(tuple(SIZES.values())), tuple(SIZES))
    in_specs = (P(GC, GR), P(GR, GC), P(GR, GC), P(GR, GC))
    out_specs = (P(GC, GR), P(GR, GC), P(GR, GC))
    return jax.shard_map(shards, mesh=fine, in_specs=in_specs, out_specs=out_specs, check_vma=False)
```

time: 562 us -> 155 us (0.28)
  the two profiles are of different devices: /device:TPU:128 before, /device:TPU:2 now
where the time goes in v1:
time: 155 us
  blocking collectives  102 us (66%)
  starting transfers between devices  25.8 us (17%)
  waiting for transfers between devices  20 us (13%)
  matrix products  2.56 us (2%)
  local copies, waits for them, and re-layouts  2.38 us (2%)
    all_to_all x2, blocking collectives, spread(): lax.all_to_all(jnp.broadcast_to(block[None], (n,) + block.shape), axes, 0...  43.9 us
    all_to_all x1, blocking collectives, shards(): total = lax.all_to_all(total, ('zn', 'x'), 0, 0, tiled=True)  27.6 us
    ppermute x3, starting transfers between devices, swap(): return lax.ppermute(value, axis, [(0, 1), (1, 0)])  21.2 us
    ppermute x3, waiting for transfers between devices, swap(): return lax.ppermute(value, axis, [(0, 1), (1, 0)])  20 us
    all_to_all x1, blocking collectives, shards(): total = lax.all_to_all(total, 'zf', 0, 0, tiled=True)  17.4 us
    all_gather x1, blocking collectives, shards(): direction = lax.all_gather(pair, ('y', 'core'), axis=0, tiled=True)  13.4 us
    all_to_all x1, starting transfers between devices, shards(): lax.all_to_all(partial.reshape(8, 80, -1), ('y', 'core'), 0, 0, tiled=True)  4.6 us
  transfers between devices with their start and end apart: 4, of which 3 were waited for; matrix products, arithmetic and copies ran while one was open for 0% of the time, Pallas kernels for 0%

profile of v1, /device:TPU:2, one launch (start us, length us, event | category | flops | bytes accessed | tf_op | source)
XLA Modules:
  0.0 155.0 jit_solution(16198231264869824141)
XLA Ops:
  0.6 0.0 copy-start
  0.6 0.9 copy.12
  1.6 24.2 %all_to_all.25 = bf16[4,20,8,128]{3,2,1,0:T(8,128)(2,1)S(1)} all-to-all(bf16[4,20,8,128]{3,2,1,0:T(8,128)(2,1)S(1)} %broadcast_in_dim.14), channel_id=1, replica_groups=mesh['y'=4,'zh'=2,'core'=2,'zf'=4,'zn'=2,'x'=4] {'zf'}, dimensions={0} | all-to-all | bytes 327680 | tf_op jit(solution)/shard_map/all_to_all | solution.py:31
  25.8 0.2 broadcast_in_dim.15
  26.0 19.7 %all_to_all.26 = bf16[8,4,20,8,128]{4,3,2,1,0:T(8,128)(2,1)S(1)} all-to-all(bf16[8,4,20,8,128]{4,3,2,1,0:T(8,128)(2,1)S(1)} %broadcast_in_dim.15), channel_id=1, replica_groups=mesh['y'=4,'zh'=2,'core'=2,'zf'=4,'zn'=2,'x'=4] {'zn','x'}, dimensions={0} | all-to-all | bytes 2621440 | tf_op jit(solution)/shard_map/all_to_all | solution.py:31
  45.7 0.1 copy.10
  45.9 0.0 copy-done
  45.9 1.7 %convolution_convert_fusion.1 = bf16[640,512]{1,0:T(8,128)(2,1)} fusion(bf16[1024,512]{1,0:T(8,128)(2,1)S(1)} %copy-done, bf16[80,8,8,128]{3,2,1,0:T(8,128)(2,1)S(1)} %bitcast.28), kind=kOutput, calls=%fused_computation.2 | convolution fusion | flops 671416320 | bytes 3014656 | tf_op jit(solution)/shard_map/dot_general | solution.py:50
  47.6 0.0 copy-start.1
  47.6 0.0 copy-start.2
  47.6 4.6 %all-to-all-start.2 = ((bf16[8,80,512]{2,1,0:T(8,128)(2,1)}), bf16[8,80,512]{2,1,0:T(8,128)(2,1)S(1)}, u32[]{:S(2)}, u32[]{:S(2)}) async-start(bf16[8,80,512]{2,1,0:T(8,128)(2,1)} %bitcast.2), calls=%async_computation.2 | async-start | bytes 1310720 | tf_op jit(solution)/shard_map/all_to_all | solution.py:51
  52.2 0.0 copy-done.1
  52.2 9.8 %collective-permute-start = (f32[40,512]{1,0:T(8,128)S(1)}, f32[40,512]{1,0:T(8,128)S(1)}, u32[]{:S(2)}, u32[]{:S(2)}) collective-permute-start(f32[40,512]{1,0:T(8,128)S(1)} %copy-done.1), channel_id=1, source_target_pairs={{0,64},{64,0},{1,65},{65,1},{2,66},{66,2},{3,67},{67,3},{4,68},{68... | collective-permute-start | bytes 245768 | tf_op jit(solution)/shard_map/ppermute | solution.py:35
  62.0 0.0 copy-done.2
  62.0 4.8 %collective-permute-start.1 = (f32[40,512]{1,0:T(8,128)S(1)}, f32[40,512]{1,0:T(8,128)S(1)}, u32[]{:S(2)}, u32[]{:S(2)}) collective-permute-start(f32[40,512]{1,0:T(8,128)S(1)} %copy-done.2), channel_id=1, source_target_pairs={{0,64},{64,0},{1,65},{65,1},{2,66},{66,2},{3,67},{67,3},{4,68},{68... | collective-permute-start | bytes 245768 | tf_op jit(solution)/shard_map/ppermute | solution.py:35
  66.8 1.0 collective-permute-done
  67.7 10.0 %collective-permute-done.1 = f32[40,512]{1,0:T(8,128)S(1)} collective-permute-done((f32[40,512]{1,0:T(8,128)S(1)}, f32[40,512]{1,0:T(8,128)S(1)}, u32[]{:S(2)}, u32[]{:S(2)}) %collective-permute-start.1) | collective-permute-done | bytes 81952 | tf_op jit(solution)/shard_map/ppermute | solution.py:35
  77.7 0.0 all-to-all-done.2
  77.8 0.1 convert_reduce_fusion
  77.9 6.7 %collective-permute-start.2 = (bf16[80,512]{1,0:T(8,128)(2,1)S(1)}, bf16[80,512]{1,0:T(8,128)(2,1)S(1)}, u32[]{:S(2)}, u32[]{:S(2)}) collective-permute-start(bf16[80,512]{1,0:T(8,128)(2,1)S(1)} %convert_element_type.27), channel_id=1, source_target_pairs={{0,64},{64,0},{1,65},{65,1},{2,66},{66,2},{3,67},{67,3},{4,68},{68... | collective-permute-start | bytes 245768 | tf_op jit(solution)/shard_map/ppermute | solution.py:35
  84.6 9.0 %collective-permute-done.2 = bf16[80,512]{1,0:T(8,128)(2,1)S(1)} collective-permute-done((bf16[80,512]{1,0:T(8,128)(2,1)S(1)}, bf16[80,512]{1,0:T(8,128)(2,1)S(1)}, u32[]{:S(2)}, u32[]{:S(2)}) %collective-permute-start.2) | collective-permute-done | bytes 81952 | tf_op jit(solution)/shard_map/ppermute | solution.py:35
  93.6 0.8 broadcast_select_fusion.1
  94.4 13.4 %all_gather.3 = bf16[640,512]{1,0:T(8,128)(2,1)S(1)} all-gather(bf16[80,512]{1,0:T(8,128)(2,1)S(1)} %pad_maximum_fusion), channel_id=1, replica_groups=mesh['y'=4,'zh'=2,'core'=2,'zf'=4,'zn'=2,'x'=4] {'y','core'}, dimensions={0}, use_global_device_ids=true | all-gather | bytes 737280 | tf_op jit(solution)/shard_map/all_gather | solution.py:63
  107.8 0.9 fusion
  108.7 0.4 copy.14
  109.0 0.1 copy.11
  109.2 27.6 %all_to_all.27 = bf16[8,4,20,8,128]{4,3,2,1,0:T(8,128)(2,1)S(1)} all-to-all(bf16[8,4,20,8,128]{4,3,2,1,0:T(8,128)(2,1)S(1)} %bitcast.27), channel_id=1, replica_groups=mesh['y'=4,'zh'=2,'core'=2,'zf'=4,'zn'=2,'x'=4] {'zn','x'}, dimensions={0} | all-to-all | bytes 2621440 | tf_op jit(solution)/shard_map/all_to_all | solution.py:70
  136.7 0.2 reduce_sum.34
  136.9 17.4 %all_to_all.28 = bf16[4,20,8,128]{3,2,1,0:T(8,128)(2,1)S(1)} all-to-all(bf16[4,20,8,128]{3,2,1,0:T(8,128)(2,1)S(1)} %reduce_sum.34), channel_id=1, replica_groups=mesh['y'=4,'zh'=2,'core'=2,'zf'=4,'zn'=2,'x'=4] {'zf'}, dimensions={0} | all-to-all | bytes 327680 | tf_op jit(solution)/shard_map/all_to_all | solution.py:72
  154.3 0.6 copy.15
  (8 shorter events, 0.1 us)
Async XLA Ops:
  0.6 45.2 %copy-start = (bf16[1024,512]{1,0:T(8,128)(2,1)S(1)}, bf16[1024,512]{1,0:T(8,128)(2,1)}, u32[]{:S(2)}) copy-start(bf16[1024,512]{1,0:T(8,128)(2,1)} %param.5) | copy-start | bytes 3145732
  47.6 4.6 %copy-start.1 = (f32[40,512]{1,0:T(8,128)S(1)}, f32[40,512]{1,0:T(8,128)}, u32[]{:S(2)}) copy-start(f32[40,512]{1,0:T(8,128)} %param.6) | copy-start | bytes 245764
  47.6 14.4 %copy-start.2 = (f32[40,512]{1,0:T(8,128)S(1)}, f32[40,512]{1,0:T(8,128)}, u32[]{:S(2)}) copy-start(f32[40,512]{1,0:T(8,128)} %param.7) | copy-start | bytes 245764
  47.6 30.2 %all-to-all-start.2 = ((bf16[8,80,512]{2,1,0:T(8,128)(2,1)}), bf16[8,80,512]{2,1,0:T(8,128)(2,1)S(1)}, u32[]{:S(2)}, u32[]{:S(2)}) async-start(bf16[8,80,512]{2,1,0:T(8,128)(2,1)} %bitcast.2), calls=%async_computation.2 | async-start | bytes 1310720 | tf_op jit(solution)/shard_map/all_to_all | solution.py:51
  52.2 15.5 %collective-permute-start = (f32[40,512]{1,0:T(8,128)S(1)}, f32[40,512]{1,0:T(8,128)S(1)}, u32[]{:S(2)}, u32[]{:S(2)}) collective-permute-start(f32[40,512]{1,0:T(8,128)S(1)} %copy-done.1), channel_id=1, source_target_pairs={{0,64},{64,0},{1,65},{65,1},{2,66},{66,2},{3,67},{67,3},{4,68},{68... | collective-permute-start | bytes 245768 | tf_op jit(solution)/shard_map/ppermute | solution.py:35
  62.0 15.8 %collective-permute-start.1 = (f32[40,512]{1,0:T(8,128)S(1)}, f32[40,512]{1,0:T(8,128)S(1)}, u32[]{:S(2)}, u32[]{:S(2)}) collective-permute-start(f32[40,512]{1,0:T(8,128)S(1)} %copy-done.2), channel_id=1, source_target_pairs={{0,64},{64,0},{1,65},{65,1},{2,66},{66,2},{3,67},{67,3},{4,68},{68... | collective-permute-start | bytes 245768 | tf_op jit(solution)/shard_map/ppermute | solution.py:35
  77.9 15.7 %collective-permute-start.2 = (bf16[80,512]{1,0:T(8,128)(2,1)S(1)}, bf16[80,512]{1,0:T(8,128)(2,1)S(1)}, u32[]{:S(2)}, u32[]{:S(2)}) collective-permute-start(bf16[80,512]{1,0:T(8,128)(2,1)S(1)} %convert_element_type.27), channel_id=1, source_target_pairs={{0,64},{64,0},{1,65},{65,1},{2,66},{66,2},{3,67},{67,3},{4,68},{68... | collective-permute-start | bytes 245768 | tf_op jit(solution)/shard_map/ppermute | solution.py:35

commit v2 on v1

--- a/solution.py
+++ b/solution.py
@@ -38,18 +38,18 @@
 def shards(grad, basis, first_moment, second_moment):
     zh = lax.axis_index("zh")
     rows, cols = grad.shape
-    first_other = swap(first_moment, "zh")
-    second_other = swap(second_moment, "zh")
-
     block = grad.reshape(rows, cols // LANES, LANES)
     block = spread(block, "zf", 4)
+    moments = jnp.stack([first_moment, second_moment])
+    moments, block = lax.optimization_barrier((moments, block))
+    slots = jnp.stack([jnp.where(zh == 0, 0.0, moments), jnp.where(zh == 0, moments, 0.0)])
+    first_other, second_other = lax.psum_scatter(slots, "zh", scatter_dimension=0)
     block = spread(block, ("zn", "x"), 8)
     block = block.reshape(2, 2, 2, 4, rows, cols // LANES, LANES)
     picked = block.transpose(3, 1, 0, 2, 4, 5, 6).reshape(32 * rows, cols)
 
     partial = jnp.dot(picked, basis, preferred_element_type=F32).astype(BF16)
     parts = lax.all_to_all(partial.reshape(8, 80, -1), ("y", "core"), 0, 0, tiled=True)
-    parts, first_other, second_other = lax.optimization_barrier((parts, first_other, second_other))
     part = jnp.sum(parts.astype(F32), axis=0)
     rotated = part + swap(part.astype(BF16), "zh").astype(F32)
     low, high = rotated[:40], rotated[40:]

time: 155 us -> 171 us (1.10)
  waiting for transfers between devices: 20 us -> 39.3 us
  blocking collectives: 102 us -> 82.8 us
  between operations: 0.78 us -> 14.2 us
  other arithmetic: 1.14 us -> 3.78 us
    all_to_all x2 -> x1, blocking collectives: 43.9 us -> 19.9 us  [spread(): lax.all_to_all(jnp.broadcast_to(block[None], (n,) + block.shape), axes, 0...]
    ppermute x3 -> x1, waiting for transfers between devices: 20 us -> 7.83 us  [swap(): return lax.ppermute(value, axis, [(0, 1), (1, 0)])]
    all_to_all x0 -> x1, waiting for transfers between devices: none -> 12 us  [spread(): lax.all_to_all(jnp.broadcast_to(block[None], (n,) + block.shape), axes, 0...]
    ppermute x3 -> x1, starting transfers between devices: 21.2 us -> 9.35 us  [swap(): return lax.ppermute(value, axis, [(0, 1), (1, 0)])]
    all_to_all x0 -> x1, starting transfers between devices: none -> 11.2 us  [spread(): lax.all_to_all(jnp.broadcast_to(block[None], (n,) + block.shape), axes, 0...]
    all_to_all x1, waiting for transfers between devices: 0.01 us -> 10.9 us  [shards(): lax.all_to_all(partial.reshape(8, 80, -1), ('y', 'core'), 0, 0, tiled=True)]
    reduce_scatter x0 -> x1, waiting for transfers between devices: none -> 8.63 us  [shards(): lax.psum_scatter(slots, 'zh', scatter_dimension=0)]
    all_gather x1, blocking collectives: 13.4 us -> 19.7 us  [shards(): direction = lax.all_gather(pair, ('y', 'core'), axis=0, tiled=True)]
  transfers between devices with their start and end apart: 4 -> 4, of which waited for: 3 -> 4; matrix products, arithmetic and copies ran while one was open for 0% -> 1% of each run, Pallas kernels for 0% -> 0%
where the time goes in v2:
time: 171 us
  blocking collectives  82.8 us (48%)
  waiting for transfers between devices  39.3 us (23%)
  starting transfers between devices  25 us (15%)
  between operations  14.2 us (8%)
  other arithmetic  3.78 us (2%)
  local copies, waits for them, and re-layouts  3.04 us (2%)
  matrix products  2.56 us (1%)
    all_to_all x1, blocking collectives, shards(): total = lax.all_to_all(total, ('zn', 'x'), 0, 0, tiled=True)  21.7 us
    all_to_all x1, blocking collectives, shards(): total = lax.all_to_all(total, 'zf', 0, 0, tiled=True)  21.5 us
    all_to_all x1, blocking collectives, spread(): lax.all_to_all(jnp.broadcast_to(block[None], (n,) + block.shape), axes, 0...  19.9 us
    all_gather x1, blocking collectives, shards(): direction = lax.all_gather(pair, ('y', 'core'), axis=0, tiled=True)  19.7 us
    all_to_all x1, waiting for transfers between devices, spread(): lax.all_to_all(jnp.broadcast_to(block[None], (n,) + block.shape), axes, 0...  12 us
    all_to_all x1, starting transfers between devices, spread(): lax.all_to_all(jnp.broadcast_to(block[None], (n,) + block.shape), axes, 0...  11.2 us
    all_to_all x1, waiting for transfers between devices, shards(): lax.all_to_all(partial.reshape(8, 80, -1), ('y', 'core'), 0, 0, tiled=True)  10.9 us
    ppermute x1, starting transfers between devices, swap(): return lax.ppermute(value, axis, [(0, 1), (1, 0)])  9.35 us
  transfers between devices with their start and end apart: 4, of which 4 were waited for; matrix products, arithmetic and copies ran while one was open for 1% of the time, Pallas kernels for 0%

profile of v2, /device:TPU:2, one launch (start us, length us, event | category | flops | bytes accessed | tf_op | source)
XLA Modules:
  0.0 170.7 jit_solution(4775068252983618891)
XLA Ops:
  7.2 0.0 copy-start
  7.2 0.9 copy.12
  8.1 0.7 broadcast_in_dim.20
  8.8 11.2 %all-to-all-start = ((bf16[4,20,8,128]{3,2,1,0:T(8,128)(2,1)}), bf16[4,20,8,128]{3,2,1,0:T(8,128)(2,1)S(1)}, u32[]{:S(2)}, u32[]{:S(2)}) async-start(bf16[4,20,8,128]{3,2,1,0:T(8,128)(2,1)} %broadcast_in_dim.20), calls=%async_computation | async-start | bytes 327680 | tf_op jit(solution)/shard_map/all_to_all | solution.py:31
  19.9 0.9 pad_maximum_fusion.1
  20.9 12.0 %all-to-all-done = bf16[4,20,8,128]{3,2,1,0:T(8,128)(2,1)S(1)} async-done(((bf16[4,20,8,128]{3,2,1,0:T(8,128)(2,1)}), bf16[4,20,8,128]{3,2,1,0:T(8,128)(2,1)S(1)}, u32[]{:S(2)}, u32[]{:S(2)}) %all-to-all-start) | async-done | bytes 163872 | tf_op jit(solution)/shard_map/all_to_all | solution.py:31
  32.9 0.2 broadcast_in_dim.21
  33.1 19.9 %all_to_all.25 = bf16[8,4,20,8,128]{4,3,2,1,0:T(8,128)(2,1)S(1)} all-to-all(bf16[8,4,20,8,128]{4,3,2,1,0:T(8,128)(2,1)S(1)} %broadcast_in_dim.21), channel_id=1, replica_groups=mesh['y'=4,'zh'=2,'core'=2,'zf'=4,'zn'=2,'x'=4] {'zn','x'}, dimensions={0} | all-to-all | bytes 2621440 | tf_op jit(solution)/shard_map/all_to_all | solution.py:31
  53.0 0.1 copy.10
  53.1 0.0 copy-done
  53.1 1.7 convolution_convert_fusion.1
  54.8 4.5 %all-to-all-start.2 = ((bf16[8,80,512]{2,1,0:T(8,128)(2,1)}), bf16[8,80,512]{2,1,0:T(8,128)(2,1)S(1)}, u32[]{:S(2)}, u32[]{:S(2)}) async-start(bf16[8,80,512]{2,1,0:T(8,128)(2,1)} %bitcast.4), calls=%async_computation.2 | async-start | bytes 1310720 | tf_op jit(solution)/shard_map/all_to_all | solution.py:52
  59.3 0.0 reduce-scatter.2.cloned.1.call-start
  59.3 0.0 copy-start.1
  59.4 0.0 copy-start.2
  59.4 0.8 pad_maximum_fusion
  60.1 0.0 reduce-scatter.2.cloned.1.call-update
  60.1 10.9 %all-to-all-done.2 = bf16[8,80,512]{2,1,0:T(8,128)(2,1)S(1)} async-done(((bf16[8,80,512]{2,1,0:T(8,128)(2,1)}), bf16[8,80,512]{2,1,0:T(8,128)(2,1)S(1)}, u32[]{:S(2)}, u32[]{:S(2)}) %all-to-all-start.2) | async-done | bytes 655392 | tf_op jit(solution)/shard_map/all_to_all | solution.py:52
  71.0 0.1 convert_reduce_fusion
  71.1 9.3 %collective-permute-start = (bf16[80,512]{1,0:T(8,128)(2,1)S(1)}, bf16[80,512]{1,0:T(8,128)(2,1)S(1)}, u32[]{:S(2)}, u32[]{:S(2)}) collective-permute-start(bf16[80,512]{1,0:T(8,128)(2,1)S(1)} %convert_element_type.27), channel_id=1, source_target_pairs={{0,64},{64,0},{1,65},{65,1},{2,66},{66,2},{3,67},{67,3},{4,68},{68... | collective-permute-start | bytes 245768 | tf_op jit(solution)/shard_map/ppermute | solution.py:35
  80.5 7.8 %collective-permute-done = bf16[80,512]{1,0:T(8,128)(2,1)S(1)} collective-permute-done((bf16[80,512]{1,0:T(8,128)(2,1)S(1)}, bf16[80,512]{1,0:T(8,128)(2,1)S(1)}, u32[]{:S(2)}, u32[]{:S(2)}) %collective-permute-start) | collective-permute-done | bytes 81952 | tf_op jit(solution)/shard_map/ppermute | solution.py:35
  88.3 8.6 %reduce-scatter.2.cloned.1.call-done = f32[1,2,40,512]{3,2,1,0:T(8,128)} async-done(((f32[2,2,40,512]{3,2,1,0:T(8,128)}), f32[1,2,40,512]{3,2,1,0:T(8,128)}) %reduce-scatter.2.cloned.1.call-update) | async-done | bytes 163856 | tf_op jit(solution)/shard_map/reduce_scatter | solution.py:46
  97.0 0.0 copy-done.1
  97.0 1.7 broadcast_select_fusion.1
  98.7 19.7 %all_gather.3 = bf16[640,512]{1,0:T(8,128)(2,1)S(1)} all-gather(bf16[80,512]{1,0:T(8,128)(2,1)S(1)} %pad_maximum_fusion.2), channel_id=1, replica_groups=mesh['y'=4,'zh'=2,'core'=2,'zf'=4,'zn'=2,'x'=4] {'y','core'}, dimensions={0}, use_global_device_ids=true | all-gather | bytes 737280 | tf_op jit(solution)/shard_map/all_gather | solution.py:63
  118.4 0.9 fusion
  119.3 0.4 copy.14
  119.7 0.1 copy.11
  119.8 21.7 %all_to_all.26 = bf16[8,4,20,8,128]{4,3,2,1,0:T(8,128)(2,1)S(1)} all-to-all(bf16[8,4,20,8,128]{4,3,2,1,0:T(8,128)(2,1)S(1)} %bitcast.51), channel_id=1, replica_groups=mesh['y'=4,'zh'=2,'core'=2,'zf'=4,'zn'=2,'x'=4] {'zn','x'}, dimensions={0} | all-to-all | bytes 2621440 | tf_op jit(solution)/shard_map/all_to_all | solution.py:70
  141.5 0.2 reduce_sum.34
  141.7 21.5 %all_to_all.27 = bf16[4,20,8,128]{3,2,1,0:T(8,128)(2,1)S(1)} all-to-all(bf16[4,20,8,128]{3,2,1,0:T(8,128)(2,1)S(1)} %reduce_sum.34), channel_id=1, replica_groups=mesh['y'=4,'zh'=2,'core'=2,'zf'=4,'zn'=2,'x'=4] {'zf'}, dimensions={0} | all-to-all | bytes 327680 | tf_op jit(solution)/shard_map/all_to_all | solution.py:72
  163.3 0.6 copy.15
  (9 shorter events, 0.1 us)
Async XLA Ops:
  7.2 45.9 %copy-start = (bf16[1024,512]{1,0:T(8,128)(2,1)S(1)}, bf16[1024,512]{1,0:T(8,128)(2,1)}, u32[]{:S(2)}) copy-start(bf16[1024,512]{1,0:T(8,128)(2,1)} %param.5) | copy-start | bytes 3145732
  8.8 24.1 %all-to-all-start = ((bf16[4,20,8,128]{3,2,1,0:T(8,128)(2,1)}), bf16[4,20,8,128]{3,2,1,0:T(8,128)(2,1)S(1)}, u32[]{:S(2)}, u32[]{:S(2)}) async-start(bf16[4,20,8,128]{3,2,1,0:T(8,128)(2,1)} %broadcast_in_dim.20), calls=%async_computation | async-start | bytes 327680 | tf_op jit(solution)/shard_map/all_to_all | solution.py:31
  54.8 16.2 %all-to-all-start.2 = ((bf16[8,80,512]{2,1,0:T(8,128)(2,1)}), bf16[8,80,512]{2,1,0:T(8,128)(2,1)S(1)}, u32[]{:S(2)}, u32[]{:S(2)}) async-start(bf16[8,80,512]{2,1,0:T(8,128)(2,1)} %bitcast.4), calls=%async_computation.2 | async-start | bytes 1310720 | tf_op jit(solution)/shard_map/all_to_all | solution.py:52
  59.3 37.7 %reduce-scatter.2.cloned.1.call-start = ((), (), s32[]{:S(2)}) async-start(), calls=%async_computation.6 | async-start | bytes 491520 | tf_op jit(solution)/shard_map/reduce_scatter | solution.py:46
  59.3 37.6 %copy-start.1 = (f32[40,512]{1,0:T(8,128)S(1)}, f32[40,512]{1,0:T(8,128)}, u32[]{:S(2)}) copy-start(f32[40,512]{1,0:T(8,128)} %param.6) | copy-start | bytes 245764
  59.4 37.6 %copy-start.2 = (f32[40,512]{1,0:T(8,128)S(1)}, f32[40,512]{1,0:T(8,128)}, u32[]{:S(2)}) copy-start(f32[40,512]{1,0:T(8,128)} %param.7) | copy-start | bytes 245764
  71.1 17.2 %collective-permute-start = (bf16[80,512]{1,0:T(8,128)(2,1)S(1)}, bf16[80,512]{1,0:T(8,128)(2,1)S(1)}, u32[]{:S(2)}, u32[]{:S(2)}) collective-permute-start(bf16[80,512]{1,0:T(8,128)(2,1)S(1)} %convert_element_type.27), channel_id=1, source_target_pairs={{0,64},{64,0},{1,65},{65,1},{2,66},{66,2},{3,67},{67,3},{4,68},{68... | collective-permute-start | bytes 245768 | tf_op jit(solution)/shard_map/ppermute | solution.py:35
Sparse Core Ops, SparseCore 0:
  62.9 34.0 reduce-scatter.1

commit v3 on v1

--- a/solution.py
+++ b/solution.py
@@ -35,21 +35,28 @@
     return lax.ppermute(value, axis, [(0, 1), (1, 0)])
 
 
+def swap_cores(value, core):
+    return lax.dynamic_index_in_dim(lax.all_gather(value, "core"), 1 - core, keepdims=False)
+
+
 def shards(grad, basis, first_moment, second_moment):
-    zh = lax.axis_index("zh")
+    zh, core = lax.axis_index("zh"), lax.axis_index("core")
     rows, cols = grad.shape
-    first_other = swap(first_moment, "zh")
-    second_other = swap(second_moment, "zh")
+    moments = swap(jnp.stack([first_moment, second_moment]).astype(BF16), "zh")
 
     block = grad.reshape(rows, cols // LANES, LANES)
     block = spread(block, "zf", 4)
+    block, moments = lax.optimization_barrier((block, moments))
+    first_other, second_other = moments[0].astype(F32), moments[1].astype(F32)
     block = spread(block, ("zn", "x"), 8)
     block = block.reshape(2, 2, 2, 4, rows, cols // LANES, LANES)
-    picked = block.transpose(3, 1, 0, 2, 4, 5, 6).reshape(32 * rows, cols)
+    picked = block.transpose(1, 3, 0, 2, 4, 5, 6).reshape(32 * rows, cols)
 
-    partial = jnp.dot(picked, basis, preferred_element_type=F32).astype(BF16)
-    parts = lax.all_to_all(partial.reshape(8, 80, -1), ("y", "core"), 0, 0, tiled=True)
-    parts, first_other, second_other = lax.optimization_barrier((parts, first_other, second_other))
+    partial = jnp.dot(picked, basis, preferred_element_type=F32).reshape(2, 320, -1)
+    away = lax.dynamic_index_in_dim(partial, 1 - core, keepdims=False).astype(BF16)
+    kept = lax.dynamic_index_in_dim(partial, core, keepdims=False)
+    chip = (kept + swap_cores(away, core).astype(F32)).astype(BF16)
+    parts = lax.all_to_all(chip.reshape(4, 80, -1), "y", 0, 0, tiled=True)
     part = jnp.sum(parts.astype(F32), axis=0)
     rotated = part + swap(part.astype(BF16), "zh").astype(F32)
     low, high = rotated[:40], rotated[40:]
@@ -60,13 +67,14 @@
     pair = jnp.concatenate(
         [jnp.where(first, share, share_other), jnp.where(first, share_other, share)], axis=0
     )
-    direction = lax.all_gather(pair, ("y", "core"), axis=0, tiled=True)
+    direction = spread(pair, "y", 4).reshape(320, -1)
+    direction = lax.all_gather(direction, "core", axis=0, tiled=True)
 
     total = lax.dot_general(
         direction, basis, (((1,), (1,)), ((), ())), preferred_element_type=F32
     ).astype(BF16)
-    total = total.reshape(4, 2, 2, 2, rows, cols // LANES, LANES)
-    total = total.transpose(2, 1, 3, 0, 4, 5, 6).reshape(8, 4, rows, cols // LANES, LANES)
+    total = total.reshape(2, 4, 2, 2, rows, cols // LANES, LANES)
+    total = total.transpose(2, 0, 3, 1, 4, 5, 6).reshape(8, 4, rows, cols // LANES, LANES)
     total = lax.all_to_all(total, ("zn", "x"), 0, 0, tiled=True)
     total = jnp.sum(total.astype(F32), axis=0).astype(BF16)
     total = lax.all_to_all(total, "zf", 0, 0, tiled=True)

time: 155 us -> 151 us (0.974)
  blocking collectives: 102 us -> 75.5 us
  starting transfers between devices: 25.8 us -> 34.5 us
  waiting for transfers between devices: 20 us -> 28.2 us
  local copies, waits for them, and re-layouts: 2.38 us -> 7.62 us
    all_to_all x2 -> x1, blocking collectives: 43.9 us -> 9.4 us  [spread(): lax.all_to_all(jnp.broadcast_to(block[None], (n,) + block.shape), axes, 0...]
    all_to_all x1 -> x2, waiting for transfers between devices: 0.01 us -> 15.1 us  [spread(): lax.all_to_all(jnp.broadcast_to(block[None], (n,) + block.shape), axes, 0...]
    all_to_all x1 -> x2, starting transfers between devices: 4.6 us -> 17.3 us  [spread(): lax.all_to_all(jnp.broadcast_to(block[None], (n,) + block.shape), axes, 0...]
    all_to_all x0 -> x1, blocking collectives: none -> 11.9 us  [shards(): parts = lax.all_to_all(chip.reshape(4, 80, -1), 'y', 0, 0, tiled=True)]
    all_to_all x1, blocking collectives: 17.4 us -> 28 us  [shards(): total = lax.all_to_all(total, 'zf', 0, 0, tiled=True)]
    all_gather x1 -> x2, blocking collectives: 13.4 us -> 4.54 us  [the longest x1 2.28 us: swap_cores(): lax.all_gather(value, 'core')]
    ppermute x3 -> x2, waiting for transfers between devices: 20 us -> 13 us  [swap(): return lax.ppermute(value, axis, [(0, 1), (1, 0)])]
    all_to_all x1, blocking collectives: 27.6 us -> 21.6 us  [shards(): total = lax.all_to_all(total, ('zn', 'x'), 0, 0, tiled=True)]
  transfers between devices with their start and end apart: 4 -> 4, of which waited for: 3 -> 3; matrix products, arithmetic and copies ran while one was open for 0% -> 1% of each run, Pallas kernels for 0% -> 0%
where the time goes in v3:
time: 151 us; the launch traced here: 150 us
  blocking collectives  75.5 us (50%)
  starting transfers between devices  34.5 us (23%)
  waiting for transfers between devices  28.2 us (19%)
  local copies, waits for them, and re-layouts  7.62 us (5%)
  other arithmetic  2.14 us (1%)
  matrix products  1.72 us (1%)
    all_to_all x1, blocking collectives, shards(): total = lax.all_to_all(total, 'zf', 0, 0, tiled=True)  28 us
    all_to_all x1, blocking collectives, shards(): total = lax.all_to_all(total, ('zn', 'x'), 0, 0, tiled=True)  21.6 us
    all_to_all x2, starting transfers between devices, spread(): lax.all_to_all(jnp.broadcast_to(block[None], (n,) + block.shape), axes, 0...  17.3 us
    ppermute x2, starting transfers between devices, swap(): return lax.ppermute(value, axis, [(0, 1), (1, 0)])  17.2 us
    all_to_all x2, waiting for transfers between devices, spread(): lax.all_to_all(jnp.broadcast_to(block[None], (n,) + block.shape), axes, 0...  15.1 us
    ppermute x2, waiting for transfers between devices, swap(): return lax.ppermute(value, axis, [(0, 1), (1, 0)])  13 us
    all_to_all x1, blocking collectives, shards(): parts = lax.all_to_all(chip.reshape(4, 80, -1), 'y', 0, 0, tiled=True)  11.9 us
    all_to_all x1, blocking collectives, spread(): lax.all_to_all(jnp.broadcast_to(block[None], (n,) + block.shape), axes, 0...  9.4 us
  transfers between devices with their start and end apart: 4, of which 3 were waited for; matrix products, arithmetic and copies ran while one was open for 1% of the time, Pallas kernels for 0%

profile of v3, /device:TPU:2, one launch (start us, length us, event | category | flops | bytes accessed | tf_op | source)
XLA Modules:
  0.0 150.4 jit_solution(8601262594663718419)
XLA Ops:
  0.6 0.0 copy-start
  0.6 0.9 copy.13
  1.5 0.7 broadcast_in_dim.9
  2.2 11.2 %all-to-all-start = ((bf16[4,20,8,128]{3,2,1,0:T(8,128)(2,1)}), bf16[4,20,8,128]{3,2,1,0:T(8,128)(2,1)S(1)}, u32[]{:S(2)}, u32[]{:S(2)}) async-start(bf16[4,20,8,128]{3,2,1,0:T(8,128)(2,1)} %broadcast_in_dim.9), calls=%async_computation | async-start | bytes 327680 | tf_op jit(solution)/shard_map/all_to_all | solution.py:31
  13.4 0.9 convert_bitcast_fusion
  14.4 9.1 %collective-permute-start = (bf16[2,40,512]{2,1,0:T(8,128)(2,1)S(1)}, bf16[2,40,512]{2,1,0:T(8,128)(2,1)S(1)}, u32[]{:S(2)}, u32[]{:S(2)}) collective-permute-start(bf16[2,40,512]{2,1,0:T(8,128)(2,1)S(1)} %pad_maximum_fusion), channel_id=1, source_target_pairs={{0,64},{64,0},{1,65},{65,1},{2,66},{66,2},{3,67},{67,3},{4,68},{68... | collective-permute-start | bytes 245768 | tf_op jit(solution)/shard_map/ppermute | solution.py:35
  23.5 6.1 %collective-permute-done = bf16[2,40,512]{2,1,0:T(8,128)(2,1)S(1)} collective-permute-done((bf16[2,40,512]{2,1,0:T(8,128)(2,1)S(1)}, bf16[2,40,512]{2,1,0:T(8,128)(2,1)S(1)}, u32[]{:S(2)}, u32[]{:S(2)}) %collective-permute-start) | collective-permute-done | bytes 81952 | tf_op jit(solution)/shard_map/ppermute | solution.py:35
  29.6 0.0 all-to-all-done
  29.6 1.3 broadcast_in_dim.10
  30.9 6.1 %all-to-all-start.1 = ((bf16[8,4,20,8,128]{4,3,2,1,0:T(8,128)(2,1)}), bf16[8,4,20,8,128]{4,3,2,1,0:T(8,128)(2,1)S(1)}, u32[]{:S(2)}, u32[]{:S(2)}) async-start(bf16[8,4,20,8,128]{4,3,2,1,0:T(8,128)(2,1)} %broadcast_in_dim.10), calls=%async_computation.1 | async-start | bytes 2621440 | tf_op jit(solution)/shard_map/all_to_all | solution.py:31
  37.0 15.1 %all-to-all-done.1 = bf16[8,4,20,8,128]{4,3,2,1,0:T(8,128)(2,1)S(1)} async-done(((bf16[8,4,20,8,128]{4,3,2,1,0:T(8,128)(2,1)}), bf16[8,4,20,8,128]{4,3,2,1,0:T(8,128)(2,1)S(1)}, u32[]{:S(2)}, u32[]{:S(2)}) %all-to-all-start.1) | async-done | bytes 1310752 | tf_op jit(solution)/shard_map/all_to_all | solution.py:31
  52.1 1.2 copy.11
  53.3 2.4 %dot_general.8 = bf16[2,320,1024]{2,1,0:T(8,128)(2,1)S(1)} reshape(bf16[2,4,2,2,20,8,128]{6,5,4,3,2,1,0:T(8,128)(2,1)} %copy.11) | data formatting | bytes 2621440 | tf_op jit(solution)/shard_map/dot_general | solution.py:55
  55.7 0.8 fusion.1
  56.5 0.1 dynamic-slice_convert_fusion
  56.6 2.3 %all_gather.7 = bf16[2,320,512]{2,1,0:T(8,128)(2,1)S(1)} all-gather(bf16[1,320,512]{2,1,0:T(8,128)(2,1)S(1)} %dynamic-slice_convert_fusion), channel_id=1, replica_groups=mesh['y'=4,'zh'=2,'core'=2,'zf'=4,'zn'=2,'x'=4] {'core'}, dimensions={0}, use_global_device_ids=true | all-gather | bytes 983040 | tf_op jit(solution)/shard_map/all_gather | solution.py:39
  58.9 0.1 add_convert_fusion
  59.0 11.9 %all_to_all.30 = bf16[4,80,512]{2,1,0:T(8,128)(2,1)S(1)} all-to-all(bf16[4,80,512]{2,1,0:T(8,128)(2,1)S(1)} %bitcast.47), channel_id=1, replica_groups=mesh['y'=4,'zh'=2,'core'=2,'zf'=4,'zn'=2,'x'=4] {'y'}, dimensions={0} | all-to-all | bytes 655360 | tf_op jit(solution)/shard_map/all_to_all | solution.py:59
  71.0 8.1 %collective-permute-start.1 = (bf16[80,512]{1,0:T(8,128)(2,1)S(1)}, bf16[80,512]{1,0:T(8,128)(2,1)S(1)}, u32[]{:S(2)}, u32[]{:S(2)}) collective-permute-start(bf16[80,512]{1,0:T(8,128)(2,1)S(1)} %convert_element_type.52), channel_id=1, source_target_pairs={{0,64},{64,0},{1,65},{65,1},{2,66},{66,2},{3,67},{67,3},{4,68},{68... | collective-permute-start | bytes 245768 | tf_op jit(solution)/shard_map/ppermute | solution.py:35
  79.1 6.9 %collective-permute-done.1 = bf16[80,512]{1,0:T(8,128)(2,1)S(1)} collective-permute-done((bf16[80,512]{1,0:T(8,128)(2,1)S(1)}, bf16[80,512]{1,0:T(8,128)(2,1)S(1)}, u32[]{:S(2)}, u32[]{:S(2)}) %collective-permute-start.1) | collective-permute-done | bytes 81952 | tf_op jit(solution)/shard_map/ppermute | solution.py:35
  86.0 0.0 copy-done.1
  86.0 0.0 copy-done.2
  86.1 0.8 broadcast_select_fusion.1
  86.9 9.4 %all_to_all.31 = bf16[4,80,512]{2,1,0:T(8,128)(2,1)S(1)} all-to-all(bf16[4,80,512]{2,1,0:T(8,128)(2,1)S(1)} %broadcast_in_dim.22), channel_id=1, replica_groups=mesh['y'=4,'zh'=2,'core'=2,'zf'=4,'zn'=2,'x'=4] {'y'}, dimensions={0} | all-to-all | bytes 655360 | tf_op jit(solution)/shard_map/all_to_all | solution.py:31
  96.3 2.3 %all_gather.8 = bf16[640,512]{1,0:T(8,128)(2,1)S(1)} all-gather(bf16[320,512]{1,0:T(8,128)(2,1)S(1)} %bitcast.48), channel_id=1, replica_groups=mesh['y'=4,'zh'=2,'core'=2,'zf'=4,'zn'=2,'x'=4] {'core'}, dimensions={0}, use_global_device_ids=true | all-gather | bytes 983040 | tf_op jit(solution)/shard_map/all_gather | solution.py:71
  98.5 0.9 fusion
  99.4 0.4 copy.14
  99.8 0.1 copy.12
  99.9 21.6 %all_to_all.32 = bf16[8,4,20,8,128]{4,3,2,1,0:T(8,128)(2,1)S(1)} all-to-all(bf16[8,4,20,8,128]{4,3,2,1,0:T(8,128)(2,1)S(1)} %bitcast.46), channel_id=1, replica_groups=mesh['y'=4,'zh'=2,'core'=2,'zf'=4,'zn'=2,'x'=4] {'zn','x'}, dimensions={0} | all-to-all | bytes 2621440 | tf_op jit(solution)/shard_map/all_to_all | solution.py:78
  121.6 0.2 reduce_sum.34
  121.8 28.0 %all_to_all.33 = bf16[4,20,8,128]{3,2,1,0:T(8,128)(2,1)S(1)} all-to-all(bf16[4,20,8,128]{3,2,1,0:T(8,128)(2,1)S(1)} %reduce_sum.34), channel_id=1, replica_groups=mesh['y'=4,'zh'=2,'core'=2,'zf'=4,'zn'=2,'x'=4] {'zf'}, dimensions={0} | all-to-all | bytes 327680 | tf_op jit(solution)/shard_map/all_to_all | solution.py:80
  149.8 0.6 copy.15
  (13 shorter events, 0.2 us)
Async XLA Ops:
  0.6 55.0 %copy-start = (bf16[1024,512]{1,0:T(8,128)(2,1)S(1)}, bf16[1024,512]{1,0:T(8,128)(2,1)}, u32[]{:S(2)}) copy-start(bf16[1024,512]{1,0:T(8,128)(2,1)} %param.5) | copy-start | bytes 3145732
  2.2 27.4 %all-to-all-start = ((bf16[4,20,8,128]{3,2,1,0:T(8,128)(2,1)}), bf16[4,20,8,128]{3,2,1,0:T(8,128)(2,1)S(1)}, u32[]{:S(2)}, u32[]{:S(2)}) async-start(bf16[4,20,8,128]{3,2,1,0:T(8,128)(2,1)} %broadcast_in_dim.9), calls=%async_computation | async-start | bytes 327680 | tf_op jit(solution)/shard_map/all_to_all | solution.py:31
  14.4 15.3 %collective-permute-start = (bf16[2,40,512]{2,1,0:T(8,128)(2,1)S(1)}, bf16[2,40,512]{2,1,0:T(8,128)(2,1)S(1)}, u32[]{:S(2)}, u32[]{:S(2)}) collective-permute-start(bf16[2,40,512]{2,1,0:T(8,128)(2,1)S(1)} %pad_maximum_fusion), channel_id=1, source_target_pairs={{0,64},{64,0},{1,65},{65,1},{2,66},{66,2},{3,67},{67,3},{4,68},{68... | collective-permute-start | bytes 245768 | tf_op jit(solution)/shard_map/ppermute | solution.py:35
  30.9 21.2 %all-to-all-start.1 = ((bf16[8,4,20,8,128]{4,3,2,1,0:T(8,128)(2,1)}), bf16[8,4,20,8,128]{4,3,2,1,0:T(8,128)(2,1)S(1)}, u32[]{:S(2)}, u32[]{:S(2)}) async-start(bf16[8,4,20,8,128]{4,3,2,1,0:T(8,128)(2,1)} %broadcast_in_dim.10), calls=%async_computation.1 | async-start | bytes 2621440 | tf_op jit(solution)/shard_map/all_to_all | solution.py:31
  58.9 27.2 %copy-start.1 = (f32[40,512]{1,0:T(8,128)S(1)}, f32[40,512]{1,0:T(8,128)}, u32[]{:S(2)}) copy-start(f32[40,512]{1,0:T(8,128)} %param.6) | copy-start | bytes 245764
  58.9 27.2 %copy-start.2 = (f32[40,512]{1,0:T(8,128)S(1)}, f32[40,512]{1,0:T(8,128)}, u32[]{:S(2)}) copy-start(f32[40,512]{1,0:T(8,128)} %param.7) | copy-start | bytes 245764
  71.0 15.0 %collective-permute-start.1 = (bf16[80,512]{1,0:T(8,128)(2,1)S(1)}, bf16[80,512]{1,0:T(8,128)(2,1)S(1)}, u32[]{:S(2)}, u32[]{:S(2)}) collective-permute-start(bf16[80,512]{1,0:T(8,128)(2,1)S(1)} %convert_element_type.52), channel_id=1, source_target_pairs={{0,64},{64,0},{1,65},{65,1},{2,66},{66,2},{3,67},{67,3},{4,68},{68... | collective-permute-start | bytes 245768 | tf_op jit(solution)/shard_map/ppermute | solution.py:35

commit v4 on v3

--- a/solution.py
+++ b/solution.py
@@ -42,19 +42,20 @@
 def shards(grad, basis, first_moment, second_moment):
     zh, core = lax.axis_index("zh"), lax.axis_index("core")
     rows, cols = grad.shape
-    moments = swap(jnp.stack([first_moment, second_moment]).astype(BF16), "zh")
-
+    moments = jnp.stack([first_moment, second_moment]).astype(BF16)
     block = grad.reshape(rows, cols // LANES, LANES)
     block = spread(block, "zf", 4)
     block, moments = lax.optimization_barrier((block, moments))
+    moments = swap(moments, "zh")
+    block = spread(block, ("zn", "x"), 8)
+    block, moments = lax.optimization_barrier((block, moments))
     first_other, second_other = moments[0].astype(F32), moments[1].astype(F32)
-    block = spread(block, ("zn", "x"), 8)
     block = block.reshape(2, 2, 2, 4, rows, cols // LANES, LANES)
     picked = block.transpose(1, 3, 0, 2, 4, 5, 6).reshape(32 * rows, cols)
 
-    partial = jnp.dot(picked, basis, preferred_element_type=F32).reshape(2, 320, -1)
-    away = lax.dynamic_index_in_dim(partial, 1 - core, keepdims=False).astype(BF16)
-    kept = lax.dynamic_index_in_dim(partial, core, keepdims=False)
+    partial = jnp.dot(picked, basis, preferred_element_type=F32)
+    away = lax.dynamic_slice_in_dim(partial, 320 * (1 - core), 320).astype(BF16)
+    kept = lax.dynamic_slice_in_dim(partial, 320 * core, 320)
     chip = (kept + swap_cores(away, core).astype(F32)).astype(BF16)
     parts = lax.all_to_all(chip.reshape(4, 80, -1), "y", 0, 0, tiled=True)
     part = jnp.sum(parts.astype(F32), axis=0)

time: 151 us -> 147 us (0.974)
  waiting for transfers between devices: 28.2 us -> 41.8 us
  blocking collectives: 75.5 us -> 68 us
  starting transfers between devices: 34.5 us -> 27.3 us
  local copies, waits for them, and re-layouts: 7.62 us -> 4.17 us
    ppermute x2, waiting for transfers between devices: 13 us -> 29.8 us  [swap(): return lax.ppermute(value, axis, [(0, 1), (1, 0)])]
    all_to_all x1, blocking collectives: 28 us -> 19.1 us  [shards(): total = lax.all_to_all(total, 'zf', 0, 0, tiled=True)]
    ppermute x2, starting transfers between devices: 17.2 us -> 10.5 us  [swap(): return lax.ppermute(value, axis, [(0, 1), (1, 0)])]
    all_to_all x2, waiting for transfers between devices: 15.1 us -> 12 us  [spread(): lax.all_to_all(jnp.broadcast_to(block[None], (n,) + block.shape), axes, 0...]
    dot_general x1 -> x0, local copies, waits for them, and re-layouts: 2.36 us -> none  [shards(): jnp.dot(picked, basis, preferred_element_type=F32).reshape(2, 320, -1)]
    all_to_all x1, blocking collectives: 9.4 us -> 11.2 us  [spread(): lax.all_to_all(jnp.broadcast_to(block[None], (n,) + block.shape), axes, 0...]
where the time goes in v4:
time: 147 us; the launch traced here: 146 us
  blocking collectives  68 us (46%)
  waiting for transfers between devices  41.8 us (28%)
  starting transfers between devices  27.3 us (19%)
  local copies, waits for them, and re-layouts  4.17 us (3%)
  other arithmetic  2.14 us (1%)
  matrix products  1.71 us (1%)
    ppermute x2, waiting for transfers between devices, swap(): return lax.ppermute(value, axis, [(0, 1), (1, 0)])  29.8 us
    all_to_all x1, blocking collectives, shards(): total = lax.all_to_all(total, ('zn', 'x'), 0, 0, tiled=True)  21.1 us
    all_to_all x1, blocking collectives, shards(): total = lax.all_to_all(total, 'zf', 0, 0, tiled=True)  19.1 us
    all_to_all x2, starting transfers between devices, spread(): lax.all_to_all(jnp.broadcast_to(block[None], (n,) + block.shape), axes, 0...  16.8 us
    all_to_all x2, waiting for transfers between devices, spread(): lax.all_to_all(jnp.broadcast_to(block[None], (n,) + block.shape), axes, 0...  12 us
    all_to_all x1, blocking collectives, shards(): parts = lax.all_to_all(chip.reshape(4, 80, -1), 'y', 0, 0, tiled=True)  11.9 us
    all_to_all x1, blocking collectives, spread(): lax.all_to_all(jnp.broadcast_to(block[None], (n,) + block.shape), axes, 0...  11.2 us
    ppermute x2, starting transfers between devices, swap(): return lax.ppermute(value, axis, [(0, 1), (1, 0)])  10.5 us
  transfers between devices with their start and end apart: 4, of which 3 were waited for; matrix products, arithmetic and copies ran while one was open for 1% of the time, Pallas kernels for 0%

profile of v4, /device:TPU:2, one launch (start us, length us, event | category | flops | bytes accessed | tf_op | source)
XLA Modules:
  0.0 146.0 jit_solution(18121646387406606276)
XLA Ops:
  0.6 0.0 copy-start
  0.6 0.9 copy.12
  1.5 0.7 broadcast_in_dim.9
  2.2 11.2 %all-to-all-start = ((bf16[4,20,8,128]{3,2,1,0:T(8,128)(2,1)}), bf16[4,20,8,128]{3,2,1,0:T(8,128)(2,1)S(1)}, u32[]{:S(2)}, u32[]{:S(2)}) async-start(bf16[4,20,8,128]{3,2,1,0:T(8,128)(2,1)} %broadcast_in_dim.9), calls=%async_computation | async-start | bytes 327680 | tf_op jit(solution)/shard_map/all_to_all | solution.py:31
  13.4 0.9 convert_bitcast_fusion
  14.4 12.0 %all-to-all-done = bf16[4,20,8,128]{3,2,1,0:T(8,128)(2,1)S(1)} async-done(((bf16[4,20,8,128]{3,2,1,0:T(8,128)(2,1)}), bf16[4,20,8,128]{3,2,1,0:T(8,128)(2,1)S(1)}, u32[]{:S(2)}, u32[]{:S(2)}) %all-to-all-start) | async-done | bytes 163872 | tf_op jit(solution)/shard_map/all_to_all | solution.py:31
  26.3 1.3 broadcast_in_dim.10
  27.6 5.7 %all-to-all-start.1 = ((bf16[8,4,20,8,128]{4,3,2,1,0:T(8,128)(2,1)}), bf16[8,4,20,8,128]{4,3,2,1,0:T(8,128)(2,1)S(1)}, u32[]{:S(2)}, u32[]{:S(2)}) async-start(bf16[8,4,20,8,128]{4,3,2,1,0:T(8,128)(2,1)} %broadcast_in_dim.10), calls=%async_computation.1 | async-start | bytes 2621440 | tf_op jit(solution)/shard_map/all_to_all | solution.py:31
  33.3 8.2 %collective-permute-start = (bf16[2,40,512]{2,1,0:T(8,128)(2,1)S(1)}, bf16[2,40,512]{2,1,0:T(8,128)(2,1)S(1)}, u32[]{:S(2)}, u32[]{:S(2)}) collective-permute-start(bf16[2,40,512]{2,1,0:T(8,128)(2,1)S(1)} %pad_maximum_fusion), channel_id=1, source_target_pairs={{0,64},{64,0},{1,65},{65,1},{2,66},{66,2},{3,67},{67,3},{4,68},{68... | collective-permute-start | bytes 245768 | tf_op jit(solution)/shard_map/ppermute | solution.py:35
  41.5 17.0 %collective-permute-done = bf16[2,40,512]{2,1,0:T(8,128)(2,1)S(1)} collective-permute-done((bf16[2,40,512]{2,1,0:T(8,128)(2,1)S(1)}, bf16[2,40,512]{2,1,0:T(8,128)(2,1)S(1)}, u32[]{:S(2)}, u32[]{:S(2)}) %collective-permute-start) | collective-permute-done | bytes 81952 | tf_op jit(solution)/shard_map/ppermute | solution.py:35
  58.5 0.0 all-to-all-done.1
  58.5 0.1 copy.10
  58.6 0.0 copy-done
  58.6 0.8 fusion.1
  59.5 0.1 dynamic-slice_convert_fusion
  59.5 2.3 %all-gather = bf16[640,512]{1,0:T(8,128)(2,1)S(1)} all-gather(bf16[320,512]{1,0:T(8,128)(2,1)S(1)} %dynamic-slice_convert_fusion), channel_id=2, replica_groups=mesh['y'=4,'zh'=2,'core'=2,'zf'=4,'zn'=2,'x'=4] {'core'}, dimensions={0}, use_global_device_ids=true | all-gather | bytes 983040 | tf_op jit(solution)/shard_map/all_gather | solution.py:39
  61.8 0.1 fusion.4
  61.9 11.9 %all_to_all.30 = bf16[4,80,512]{2,1,0:T(8,128)(2,1)S(1)} all-to-all(bf16[4,80,512]{2,1,0:T(8,128)(2,1)S(1)} %bitcast.53), channel_id=1, replica_groups=mesh['y'=4,'zh'=2,'core'=2,'zf'=4,'zn'=2,'x'=4] {'y'}, dimensions={0} | all-to-all | bytes 655360 | tf_op jit(solution)/shard_map/all_to_all | solution.py:60
  73.9 2.3 %collective-permute-start.1 = (bf16[80,512]{1,0:T(8,128)(2,1)S(1)}, bf16[80,512]{1,0:T(8,128)(2,1)S(1)}, u32[]{:S(2)}, u32[]{:S(2)}) collective-permute-start(bf16[80,512]{1,0:T(8,128)(2,1)S(1)} %convert_element_type.48), channel_id=1, source_target_pairs={{0,64},{64,0},{1,65},{65,1},{2,66},{66,2},{3,67},{67,3},{4,68},{68... | collective-permute-start | bytes 245768 | tf_op jit(solution)/shard_map/ppermute | solution.py:35
  76.3 12.8 %collective-permute-done.1 = bf16[80,512]{1,0:T(8,128)(2,1)S(1)} collective-permute-done((bf16[80,512]{1,0:T(8,128)(2,1)S(1)}, bf16[80,512]{1,0:T(8,128)(2,1)S(1)}, u32[]{:S(2)}, u32[]{:S(2)}) %collective-permute-start.1) | collective-permute-done | bytes 81952 | tf_op jit(solution)/shard_map/ppermute | solution.py:35
  89.1 0.0 copy-done.1
  89.1 0.0 copy-done.2
  89.1 0.8 broadcast_select_fusion.1
  89.9 11.2 %all_to_all.31 = bf16[4,80,512]{2,1,0:T(8,128)(2,1)S(1)} all-to-all(bf16[4,80,512]{2,1,0:T(8,128)(2,1)S(1)} %broadcast_in_dim.22), channel_id=1, replica_groups=mesh['y'=4,'zh'=2,'core'=2,'zf'=4,'zn'=2,'x'=4] {'y'}, dimensions={0} | all-to-all | bytes 655360 | tf_op jit(solution)/shard_map/all_to_all | solution.py:31
  101.2 2.3 %all_gather.11 = bf16[640,512]{1,0:T(8,128)(2,1)S(1)} all-gather(bf16[320,512]{1,0:T(8,128)(2,1)S(1)} %bitcast.54), channel_id=1, replica_groups=mesh['y'=4,'zh'=2,'core'=2,'zf'=4,'zn'=2,'x'=4] {'core'}, dimensions={0}, use_global_device_ids=true | all-gather | bytes 983040 | tf_op jit(solution)/shard_map/all_gather | solution.py:72
  103.4 0.9 fusion
  104.3 0.4 copy.14
  104.7 0.1 copy.11
  104.8 21.1 %all_to_all.32 = bf16[8,4,20,8,128]{4,3,2,1,0:T(8,128)(2,1)S(1)} all-to-all(bf16[8,4,20,8,128]{4,3,2,1,0:T(8,128)(2,1)S(1)} %bitcast.50), channel_id=1, replica_groups=mesh['y'=4,'zh'=2,'core'=2,'zf'=4,'zn'=2,'x'=4] {'zn','x'}, dimensions={0} | all-to-all | bytes 2621440 | tf_op jit(solution)/shard_map/all_to_all | solution.py:79
  126.0 0.2 reduce_sum.34
  126.2 19.1 %all_to_all.33 = bf16[4,20,8,128]{3,2,1,0:T(8,128)(2,1)S(1)} all-to-all(bf16[4,20,8,128]{3,2,1,0:T(8,128)(2,1)S(1)} %reduce_sum.34), channel_id=1, replica_groups=mesh['y'=4,'zh'=2,'core'=2,'zf'=4,'zn'=2,'x'=4] {'zf'}, dimensions={0} | all-to-all | bytes 327680 | tf_op jit(solution)/shard_map/all_to_all | solution.py:81
  145.3 0.6 copy.15
  (12 shorter events, 0.2 us)
Async XLA Ops:
  0.6 58.0 %copy-start = (bf16[1024,512]{1,0:T(8,128)(2,1)S(1)}, bf16[1024,512]{1,0:T(8,128)(2,1)}, u32[]{:S(2)}) copy-start(bf16[1024,512]{1,0:T(8,128)(2,1)} %param.5) | copy-start | bytes 3145732
  2.2 24.1 %all-to-all-start = ((bf16[4,20,8,128]{3,2,1,0:T(8,128)(2,1)}), bf16[4,20,8,128]{3,2,1,0:T(8,128)(2,1)S(1)}, u32[]{:S(2)}, u32[]{:S(2)}) async-start(bf16[4,20,8,128]{3,2,1,0:T(8,128)(2,1)} %broadcast_in_dim.9), calls=%async_computation | async-start | bytes 327680 | tf_op jit(solution)/shard_map/all_to_all | solution.py:31
  27.6 30.9 %all-to-all-start.1 = ((bf16[8,4,20,8,128]{4,3,2,1,0:T(8,128)(2,1)}), bf16[8,4,20,8,128]{4,3,2,1,0:T(8,128)(2,1)S(1)}, u32[]{:S(2)}, u32[]{:S(2)}) async-start(bf16[8,4,20,8,128]{4,3,2,1,0:T(8,128)(2,1)} %broadcast_in_dim.10), calls=%async_computation.1 | async-start | bytes 2621440 | tf_op jit(solution)/shard_map/all_to_all | solution.py:31
  33.3 25.2 %collective-permute-start = (bf16[2,40,512]{2,1,0:T(8,128)(2,1)S(1)}, bf16[2,40,512]{2,1,0:T(8,128)(2,1)S(1)}, u32[]{:S(2)}, u32[]{:S(2)}) collective-permute-start(bf16[2,40,512]{2,1,0:T(8,128)(2,1)S(1)} %pad_maximum_fusion), channel_id=1, source_target_pairs={{0,64},{64,0},{1,65},{65,1},{2,66},{66,2},{3,67},{67,3},{4,68},{68... | collective-permute-start | bytes 245768 | tf_op jit(solution)/shard_map/ppermute | solution.py:35
  61.8 27.3 %copy-start.1 = (f32[40,512]{1,0:T(8,128)S(1)}, f32[40,512]{1,0:T(8,128)}, u32[]{:S(2)}) copy-start(f32[40,512]{1,0:T(8,128)} %param.6) | copy-start | bytes 245764
  61.8 27.3 %copy-start.2 = (f32[40,512]{1,0:T(8,128)S(1)}, f32[40,512]{1,0:T(8,128)}, u32[]{:S(2)}) copy-start(f32[40,512]{1,0:T(8,128)} %param.7) | copy-start | bytes 245764
  73.9 15.1 %collective-permute-start.1 = (bf16[80,512]{1,0:T(8,128)(2,1)S(1)}, bf16[80,512]{1,0:T(8,128)(2,1)S(1)}, u32[]{:S(2)}, u32[]{:S(2)}) collective-permute-start(bf16[80,512]{1,0:T(8,128)(2,1)S(1)} %convert_element_type.48), channel_id=1, source_target_pairs={{0,64},{64,0},{1,65},{65,1},{2,66},{66,2},{3,67},{67,3},{4,68},{68... | collective-permute-start | bytes 245768 | tf_op jit(solution)/shard_map/ppermute | solution.py:35

commit v5 on v4

--- a/solution.py
+++ b/solution.py
@@ -45,11 +45,7 @@
     moments = jnp.stack([first_moment, second_moment]).astype(BF16)
     block = grad.reshape(rows, cols // LANES, LANES)
     block = spread(block, "zf", 4)
-    block, moments = lax.optimization_barrier((block, moments))
-    moments = swap(moments, "zh")
     block = spread(block, ("zn", "x"), 8)
-    block, moments = lax.optimization_barrier((block, moments))
-    first_other, second_other = moments[0].astype(F32), moments[1].astype(F32)
     block = block.reshape(2, 2, 2, 4, rows, cols // LANES, LANES)
     picked = block.transpose(1, 3, 0, 2, 4, 5, 6).reshape(32 * rows, cols)
 
@@ -57,6 +53,8 @@
     away = lax.dynamic_slice_in_dim(partial, 320 * (1 - core), 320).astype(BF16)
     kept = lax.dynamic_slice_in_dim(partial, 320 * core, 320)
     chip = (kept + swap_cores(away, core).astype(F32)).astype(BF16)
+    chip, moments = lax.optimization_barrier((chip, moments))
+    first_other, second_other = swap(moments, "zh").astype(F32)
     parts = lax.all_to_all(chip.reshape(4, 80, -1), "y", 0, 0, tiled=True)
     part = jnp.sum(parts.astype(F32), axis=0)
     rotated = part + swap(part.astype(BF16), "zh").astype(F32)

time: 147 us -> 140 us (0.952)
  waiting for transfers between devices: 41.8 us -> 24.2 us
  blocking collectives: 68 us -> 80.3 us
    all_to_all x1 -> x2, blocking collectives: 11.2 us -> 35.5 us  [spread(): lax.all_to_all(jnp.broadcast_to(block[None], (n,) + block.shape), axes, 0...]
    ppermute x2, waiting for transfers between devices: 29.8 us -> 9.88 us  [swap(): return lax.ppermute(value, axis, [(0, 1), (1, 0)])]
    all_to_all x1 -> x0, blocking collectives: 11.9 us -> none  [shards(): parts = lax.all_to_all(chip.reshape(4, 80, -1), 'y', 0, 0, tiled=True)]
    all_to_all x2 -> x1, starting transfers between devices: 16.8 us -> 5.44 us  [spread(): lax.all_to_all(jnp.broadcast_to(block[None], (n,) + block.shape), axes, 0...]
    ppermute x2, starting transfers between devices: 10.5 us -> 17.4 us  [swap(): return lax.ppermute(value, axis, [(0, 1), (1, 0)])]
    all_to_all x0 -> x1, starting transfers between devices: none -> 4.46 us  [shards(): parts = lax.all_to_all(chip.reshape(4, 80, -1), 'y', 0, 0, tiled=True)]
    all_to_all x2 -> x1, waiting for transfers between devices: 12 us -> 14.3 us  [spread(): lax.all_to_all(jnp.broadcast_to(block[None], (n,) + block.shape), axes, 0...]
  transfers between devices with their start and end apart: 4 -> 4, of which waited for: 3 -> 2; matrix products, arithmetic and copies ran while one was open for 1% -> 0% of each run, Pallas kernels for 0% -> 0%
where the time goes in v5:
time: 140 us
  blocking collectives  80.3 us (57%)
  starting transfers between devices  27.3 us (20%)
  waiting for transfers between devices  24.2 us (17%)
  local copies, waits for them, and re-layouts  3.51 us (3%)
  other arithmetic  1.95 us (1%)
  matrix products  1.72 us (1%)
    all_to_all x2, blocking collectives, spread(): lax.all_to_all(jnp.broadcast_to(block[None], (n,) + block.shape), axes, 0...  35.5 us
    all_to_all x1, blocking collectives, shards(): total = lax.all_to_all(total, ('zn', 'x'), 0, 0, tiled=True)  20.5 us
    all_to_all x1, blocking collectives, shards(): total = lax.all_to_all(total, 'zf', 0, 0, tiled=True)  19.8 us
    ppermute x2, starting transfers between devices, swap(): return lax.ppermute(value, axis, [(0, 1), (1, 0)])  17.4 us
    all_to_all x1, waiting for transfers between devices, spread(): lax.all_to_all(jnp.broadcast_to(block[None], (n,) + block.shape), axes, 0...  14.3 us
    ppermute x2, waiting for transfers between devices, swap(): return lax.ppermute(value, axis, [(0, 1), (1, 0)])  9.88 us
    all_to_all x1, starting transfers between devices, spread(): lax.all_to_all(jnp.broadcast_to(block[None], (n,) + block.shape), axes, 0...  5.44 us
    all_to_all x1, starting transfers between devices, shards(): parts = lax.all_to_all(chip.reshape(4, 80, -1), 'y', 0, 0, tiled=True)  4.46 us
  transfers between devices with their start and end apart: 4, of which 2 were waited for; matrix products, arithmetic and copies ran while one was open for 0% of the time, Pallas kernels for 0%

profile of v5, /device:TPU:2, one launch (start us, length us, event | category | flops | bytes accessed | tf_op | source)
XLA Modules:
  0.0 139.8 jit_solution(9600897148091857235)
XLA Ops:
  0.6 0.0 copy-start
  0.6 0.9 copy.12
  1.6 24.2 %all_to_all.30 = bf16[4,20,8,128]{3,2,1,0:T(8,128)(2,1)S(1)} all-to-all(bf16[4,20,8,128]{3,2,1,0:T(8,128)(2,1)S(1)} %broadcast_in_dim.9), channel_id=1, replica_groups=mesh['y'=4,'zh'=2,'core'=2,'zf'=4,'zn'=2,'x'=4] {'zf'}, dimensions={0} | all-to-all | bytes 327680 | tf_op jit(solution)/shard_map/all_to_all | solution.py:31
  25.8 1.3 broadcast_in_dim.10
  27.1 0.0 copy-start.1
  27.1 0.0 copy-start.2
  27.1 5.4 %all-to-all-start.1 = ((bf16[8,4,20,8,128]{4,3,2,1,0:T(8,128)(2,1)}), bf16[8,4,20,8,128]{4,3,2,1,0:T(8,128)(2,1)S(1)}, u32[]{:S(2)}, u32[]{:S(2)}) async-start(bf16[8,4,20,8,128]{4,3,2,1,0:T(8,128)(2,1)} %broadcast_in_dim.10), calls=%async_computation.1 | async-start | bytes 2621440 | tf_op jit(solution)/shard_map/all_to_all | solution.py:31
  32.5 0.0 copy-done.1
  32.5 0.0 copy-done.2
  32.6 14.3 %all-to-all-done.1 = bf16[8,4,20,8,128]{4,3,2,1,0:T(8,128)(2,1)S(1)} async-done(((bf16[8,4,20,8,128]{4,3,2,1,0:T(8,128)(2,1)}), bf16[8,4,20,8,128]{4,3,2,1,0:T(8,128)(2,1)S(1)}, u32[]{:S(2)}, u32[]{:S(2)}) %all-to-all-start.1) | async-done | bytes 1310752 | tf_op jit(solution)/shard_map/all_to_all | solution.py:31
  46.9 0.1 copy.10
  47.0 0.0 copy-done
  47.1 0.8 fusion.1
  47.9 0.1 dynamic-slice_convert_fusion
  48.0 2.3 %all-gather = bf16[640,512]{1,0:T(8,128)(2,1)S(1)} all-gather(bf16[320,512]{1,0:T(8,128)(2,1)S(1)} %dynamic-slice_convert_fusion), channel_id=2, replica_groups=mesh['y'=4,'zh'=2,'core'=2,'zf'=4,'zn'=2,'x'=4] {'core'}, dimensions={0}, use_global_device_ids=true | all-gather | bytes 983040 | tf_op jit(solution)/shard_map/all_gather | solution.py:39
  50.2 0.8 fusion.4
  51.0 4.5 %all-to-all-start.2 = ((bf16[4,80,512]{2,1,0:T(8,128)(2,1)}), bf16[4,80,512]{2,1,0:T(8,128)(2,1)S(1)}, u32[]{:S(2)}, u32[]{:S(2)}) async-start(bf16[4,80,512]{2,1,0:T(8,128)(2,1)} %bitcast.6), calls=%async_computation.2 | async-start | bytes 655360 | tf_op jit(solution)/shard_map/all_to_all | solution.py:58
  55.5 9.8 %collective-permute-start.1 = (bf16[2,40,512]{2,1,0:T(8,128)(2,1)S(1)}, bf16[2,40,512]{2,1,0:T(8,128)(2,1)S(1)}, u32[]{:S(2)}, u32[]{:S(2)}) collective-permute-start(bf16[2,40,512]{2,1,0:T(8,128)(2,1)S(1)} %pad_maximum_fusion), channel_id=1, source_target_pairs={{0,64},{64,0},{1,65},{65,1},{2,66},{66,2},{3,67},{67,3},{4,68},{68... | collective-permute-start | bytes 245768 | tf_op jit(solution)/shard_map/ppermute | solution.py:35
  65.3 0.0 all-to-all-done.2
  65.4 7.7 %collective-permute-start = (bf16[80,512]{1,0:T(8,128)(2,1)S(1)}, bf16[80,512]{1,0:T(8,128)(2,1)S(1)}, u32[]{:S(2)}, u32[]{:S(2)}) collective-permute-start(bf16[80,512]{1,0:T(8,128)(2,1)S(1)} %convert_element_type.43), channel_id=1, source_target_pairs={{0,64},{64,0},{1,65},{65,1},{2,66},{66,2},{3,67},{67,3},{4,68},{68... | collective-permute-start | bytes 245768 | tf_op jit(solution)/shard_map/ppermute | solution.py:35
  73.0 0.0 collective-permute-done.1
  73.1 9.9 %collective-permute-done = bf16[80,512]{1,0:T(8,128)(2,1)S(1)} collective-permute-done((bf16[80,512]{1,0:T(8,128)(2,1)S(1)}, bf16[80,512]{1,0:T(8,128)(2,1)S(1)}, u32[]{:S(2)}, u32[]{:S(2)}) %collective-permute-start) | collective-permute-done | bytes 81952 | tf_op jit(solution)/shard_map/ppermute | solution.py:35
  83.0 0.8 broadcast_select_fusion.1
  83.8 11.2 %all_to_all.31 = bf16[4,80,512]{2,1,0:T(8,128)(2,1)S(1)} all-to-all(bf16[4,80,512]{2,1,0:T(8,128)(2,1)S(1)} %broadcast_in_dim.22), channel_id=1, replica_groups=mesh['y'=4,'zh'=2,'core'=2,'zf'=4,'zn'=2,'x'=4] {'y'}, dimensions={0} | all-to-all | bytes 655360 | tf_op jit(solution)/shard_map/all_to_all | solution.py:31
  95.1 2.3 %all_gather.11 = bf16[640,512]{1,0:T(8,128)(2,1)S(1)} all-gather(bf16[320,512]{1,0:T(8,128)(2,1)S(1)} %bitcast.57), channel_id=1, replica_groups=mesh['y'=4,'zh'=2,'core'=2,'zf'=4,'zn'=2,'x'=4] {'core'}, dimensions={0}, use_global_device_ids=true | all-gather | bytes 983040 | tf_op jit(solution)/shard_map/all_gather | solution.py:70
  97.3 0.9 fusion
  98.2 0.4 copy.14
  98.6 0.1 copy.11
  98.7 20.5 %all_to_all.32 = bf16[8,4,20,8,128]{4,3,2,1,0:T(8,128)(2,1)S(1)} all-to-all(bf16[8,4,20,8,128]{4,3,2,1,0:T(8,128)(2,1)S(1)} %bitcast.54), channel_id=1, replica_groups=mesh['y'=4,'zh'=2,'core'=2,'zf'=4,'zn'=2,'x'=4] {'zn','x'}, dimensions={0} | all-to-all | bytes 2621440 | tf_op jit(solution)/shard_map/all_to_all | solution.py:77
  119.2 0.2 reduce_sum.34
  119.4 19.8 %all_to_all.33 = bf16[4,20,8,128]{3,2,1,0:T(8,128)(2,1)S(1)} all-to-all(bf16[4,20,8,128]{3,2,1,0:T(8,128)(2,1)S(1)} %reduce_sum.34), channel_id=1, replica_groups=mesh['y'=4,'zh'=2,'core'=2,'zf'=4,'zn'=2,'x'=4] {'zf'}, dimensions={0} | all-to-all | bytes 327680 | tf_op jit(solution)/shard_map/all_to_all | solution.py:79
  139.2 0.6 copy.15
  (13 shorter events, 0.2 us)
Async XLA Ops:
  0.6 46.4 %copy-start = (bf16[1024,512]{1,0:T(8,128)(2,1)S(1)}, bf16[1024,512]{1,0:T(8,128)(2,1)}, u32[]{:S(2)}) copy-start(bf16[1024,512]{1,0:T(8,128)(2,1)} %param.5) | copy-start | bytes 3145732
  27.1 5.4 %copy-start.1 = (f32[40,512]{1,0:T(8,128)S(1)}, f32[40,512]{1,0:T(8,128)}, u32[]{:S(2)}) copy-start(f32[40,512]{1,0:T(8,128)} %param.6) | copy-start | bytes 245764
  27.1 5.4 %copy-start.2 = (f32[40,512]{1,0:T(8,128)S(1)}, f32[40,512]{1,0:T(8,128)}, u32[]{:S(2)}) copy-start(f32[40,512]{1,0:T(8,128)} %param.7) | copy-start | bytes 245764
  27.1 19.8 %all-to-all-start.1 = ((bf16[8,4,20,8,128]{4,3,2,1,0:T(8,128)(2,1)}), bf16[8,4,20,8,128]{4,3,2,1,0:T(8,128)(2,1)S(1)}, u32[]{:S(2)}, u32[]{:S(2)}) async-start(bf16[8,4,20,8,128]{4,3,2,1,0:T(8,128)(2,1)} %broadcast_in_dim.10), calls=%async_computation.1 | async-start | bytes 2621440 | tf_op jit(solution)/shard_map/all_to_all | solution.py:31
  51.0 14.2 %all-to-all-start.2 = ((bf16[4,80,512]{2,1,0:T(8,128)(2,1)}), bf16[4,80,512]{2,1,0:T(8,128)(2,1)S(1)}, u32[]{:S(2)}, u32[]{:S(2)}) async-start(bf16[4,80,512]{2,1,0:T(8,128)(2,1)} %bitcast.6), calls=%async_computation.2 | async-start | bytes 655360 | tf_op jit(solution)/shard_map/all_to_all | solution.py:58
  55.5 17.5 %collective-permute-start.1 = (bf16[2,40,512]{2,1,0:T(8,128)(2,1)S(1)}, bf16[2,40,512]{2,1,0:T(8,128)(2,1)S(1)}, u32[]{:S(2)}, u32[]{:S(2)}) collective-permute-start(bf16[2,40,512]{2,1,0:T(8,128)(2,1)S(1)} %pad_maximum_fusion), channel_id=1, source_target_pairs={{0,64},{64,0},{1,65},{65,1},{2,66},{66,2},{3,67},{67,3},{4,68},{68... | collective-permute-start | bytes 245768 | tf_op jit(solution)/shard_map/ppermute | solution.py:35
  65.4 17.6 %collective-permute-start = (bf16[80,512]{1,0:T(8,128)(2,1)S(1)}, bf16[80,512]{1,0:T(8,128)(2,1)S(1)}, u32[]{:S(2)}, u32[]{:S(2)}) collective-permute-start(bf16[80,512]{1,0:T(8,128)(2,1)S(1)} %convert_element_type.43), channel_id=1, source_target_pairs={{0,64},{64,0},{1,65},{65,1},{2,66},{66,2},{3,67},{67,3},{4,68},{68... | collective-permute-start | bytes 245768 | tf_op jit(solution)/shard_map/ppermute | solution.py:35

commit v6 on v5

--- a/solution.py
+++ b/solution.py
@@ -42,7 +42,8 @@
 def shards(grad, basis, first_moment, second_moment):
     zh, core = lax.axis_index("zh"), lax.axis_index("core")
     rows, cols = grad.shape
-    moments = jnp.stack([first_moment, second_moment]).astype(BF16)
+    moments = swap(jnp.stack([first_moment, second_moment]).astype(BF16), "core")
+    moments = lax.ppermute(moments, ("zh", "core"), [(i, 3 - i) for i in range(4)])
     block = grad.reshape(rows, cols // LANES, LANES)
     block = spread(block, "zf", 4)
     block = spread(block, ("zn", "x"), 8)
@@ -54,7 +55,7 @@
     kept = lax.dynamic_slice_in_dim(partial, 320 * core, 320)
     chip = (kept + swap_cores(away, core).astype(F32)).astype(BF16)
     chip, moments = lax.optimization_barrier((chip, moments))
-    first_other, second_other = swap(moments, "zh").astype(F32)
+    first_other, second_other = moments.astype(F32)
     parts = lax.all_to_all(chip.reshape(4, 80, -1), "y", 0, 0, tiled=True)
     part = jnp.sum(parts.astype(F32), axis=0)
     rotated = part + swap(part.astype(BF16), "zh").astype(F32)

time: 140 us -> 144 us (1.029)
  blocking collectives: 80.3 us -> 95.5 us
  waiting for transfers between devices: 24.2 us -> 17.6 us
  starting transfers between devices: 27.3 us -> 23.4 us
    all_to_all x0 -> x1, blocking collectives: none -> 11.5 us  [shards(): parts = lax.all_to_all(chip.reshape(4, 80, -1), 'y', 0, 0, tiled=True)]
    all_to_all x1, waiting for transfers between devices: 14.3 us -> 2.84 us  [spread(): lax.all_to_all(jnp.broadcast_to(block[None], (n,) + block.shape), axes, 0...]
    ppermute x0 -> x1, starting transfers between devices: none -> 8.3 us  [shards(): lax.ppermute(moments, ('zh', 'core'), [(i, 3 - i) for i in range(4)])]
    ppermute x2, starting transfers between devices: 17.4 us -> 9.7 us  [swap(): return lax.ppermute(value, axis, [(0, 1), (1, 0)])]
    ppermute x0 -> x1, waiting for transfers between devices: none -> 5.68 us  [shards(): lax.ppermute(moments, ('zh', 'core'), [(i, 3 - i) for i in range(4)])]
    all_to_all x1 -> x0, starting transfers between devices: 4.46 us -> none  [shards(): parts = lax.all_to_all(chip.reshape(4, 80, -1), 'y', 0, 0, tiled=True)]
    all_to_all x1, blocking collectives: 20.5 us -> 23.3 us  [shards(): total = lax.all_to_all(total, ('zn', 'x'), 0, 0, tiled=True)]
    all_to_all x1, blocking collectives: 19.8 us -> 21.3 us  [shards(): total = lax.all_to_all(total, 'zf', 0, 0, tiled=True)]
  transfers between devices with their start and end apart: 4 -> 4, of which waited for: 2 -> 4; matrix products, arithmetic and copies ran while one was open for 0% -> 1% of each run, Pallas kernels for 0% -> 0%
where the time goes in v6:
time: 144 us
  blocking collectives  95.5 us (66%)
  starting transfers between devices  23.4 us (16%)
  waiting for transfers between devices  17.6 us (12%)
  local copies, waits for them, and re-layouts  3.52 us (2%)
  matrix products  1.71 us (1%)
    all_to_all x2, blocking collectives, spread(): lax.all_to_all(jnp.broadcast_to(block[None], (n,) + block.shape), axes, 0...  34.4 us
    all_to_all x1, blocking collectives, shards(): total = lax.all_to_all(total, ('zn', 'x'), 0, 0, tiled=True)  23.3 us
    all_to_all x1, blocking collectives, shards(): total = lax.all_to_all(total, 'zf', 0, 0, tiled=True)  21.3 us
    all_to_all x1, blocking collectives, shards(): parts = lax.all_to_all(chip.reshape(4, 80, -1), 'y', 0, 0, tiled=True)  11.5 us
    ppermute x2, starting transfers between devices, swap(): return lax.ppermute(value, axis, [(0, 1), (1, 0)])  9.7 us
    ppermute x2, waiting for transfers between devices, swap(): return lax.ppermute(value, axis, [(0, 1), (1, 0)])  9.03 us
    ppermute x1, starting transfers between devices, shards(): lax.ppermute(moments, ('zh', 'core'), [(i, 3 - i) for i in range(4)])  8.3 us
    ppermute x1, waiting for transfers between devices, shards(): lax.ppermute(moments, ('zh', 'core'), [(i, 3 - i) for i in range(4)])  5.68 us
  transfers between devices with their start and end apart: 4, of which 4 were waited for; matrix products, arithmetic and copies ran while one was open for 1% of the time, Pallas kernels for 0%

profile of v6, /device:TPU:2, one launch (start us, length us, event | category | flops | bytes accessed | tf_op | source)
XLA Modules:
  0.0 143.8 jit_solution(8423752693550105768)
XLA Ops:
  0.6 0.0 copy-start
  0.6 0.9 copy.12
  1.6 24.2 %all_to_all.30 = bf16[4,20,8,128]{3,2,1,0:T(8,128)(2,1)S(1)} all-to-all(bf16[4,20,8,128]{3,2,1,0:T(8,128)(2,1)S(1)} %broadcast_in_dim.9), channel_id=1, replica_groups=mesh['y'=4,'zh'=2,'core'=2,'zf'=4,'zn'=2,'x'=4] {'zf'}, dimensions={0} | all-to-all | bytes 327680 | tf_op jit(solution)/shard_map/all_to_all | solution.py:31
  25.8 1.3 broadcast_in_dim.10
  27.1 0.0 copy-start.1
  27.1 5.4 %all-to-all-start.1 = ((bf16[8,4,20,8,128]{4,3,2,1,0:T(8,128)(2,1)}), bf16[8,4,20,8,128]{4,3,2,1,0:T(8,128)(2,1)S(1)}, u32[]{:S(2)}, u32[]{:S(2)}) async-start(bf16[8,4,20,8,128]{4,3,2,1,0:T(8,128)(2,1)} %broadcast_in_dim.10), calls=%async_computation.1 | async-start | bytes 2621440 | tf_op jit(solution)/shard_map/all_to_all | solution.py:31
  32.6 0.0 copy-done.1
  32.6 0.0 copy-done.2
  32.6 1.9 %collective-permute-start = (bf16[2,40,512]{2,1,0:T(8,128)(2,1)S(1)}, bf16[2,40,512]{2,1,0:T(8,128)(2,1)S(1)}, u32[]{:S(2)}, u32[]{:S(2)}) collective-permute-start(bf16[2,40,512]{2,1,0:T(8,128)(2,1)S(1)} %pad_maximum_fusion), channel_id=1, source_target_pairs={{0,32},{32,0},{1,33},{33,1},{2,34},{34,2},{3,35},{35,3},{4,36},{36... | collective-permute-start | bytes 245768 | tf_op jit(solution)/shard_map/ppermute | solution.py:35
  34.5 1.2 collective-permute-done
  35.8 8.3 %collective-permute-start.1 = (bf16[2,40,512]{2,1,0:T(8,128)(2,1)S(1)}, bf16[2,40,512]{2,1,0:T(8,128)(2,1)S(1)}, u32[]{:S(2)}, u32[]{:S(2)}) collective-permute-start(bf16[2,40,512]{2,1,0:T(8,128)(2,1)S(1)} %collective-permute-done), channel_id=1, source_target_pairs={{0,96},{32,64},{64,32},{96,0},{1,97},{33,65},{65,33},{97,1},{2,98}... | collective-permute-start | bytes 245768 | tf_op jit(solution)/shard_map/ppermute | solution.py:46
  44.1 2.8 %all-to-all-done.1 = bf16[8,4,20,8,128]{4,3,2,1,0:T(8,128)(2,1)S(1)} async-done(((bf16[8,4,20,8,128]{4,3,2,1,0:T(8,128)(2,1)}), bf16[8,4,20,8,128]{4,3,2,1,0:T(8,128)(2,1)S(1)}, u32[]{:S(2)}, u32[]{:S(2)}) %all-to-all-start.1) | async-done | bytes 1310752 | tf_op jit(solution)/shard_map/all_to_all | solution.py:31
  46.9 0.1 copy.10
  47.1 0.0 copy-done
  47.1 0.8 fusion.1
  47.9 0.1 dynamic-slice_convert_fusion
  48.0 2.3 %all-gather = bf16[640,512]{1,0:T(8,128)(2,1)S(1)} all-gather(bf16[320,512]{1,0:T(8,128)(2,1)S(1)} %dynamic-slice_convert_fusion), channel_id=2, replica_groups=mesh['y'=4,'zh'=2,'core'=2,'zf'=4,'zn'=2,'x'=4] {'core'}, dimensions={0}, use_global_device_ids=true | all-gather | bytes 983040 | tf_op jit(solution)/shard_map/all_gather | solution.py:39
  50.2 0.1 fusion.4
  50.3 5.7 %collective-permute-done.1 = bf16[2,40,512]{2,1,0:T(8,128)(2,1)S(1)} collective-permute-done((bf16[2,40,512]{2,1,0:T(8,128)(2,1)S(1)}, bf16[2,40,512]{2,1,0:T(8,128)(2,1)S(1)}, u32[]{:S(2)}, u32[]{:S(2)}) %collective-permute-start.1) | collective-permute-done | bytes 81952 | tf_op jit(solution)/shard_map/ppermute | solution.py:46
  56.0 11.5 %all_to_all.31 = bf16[4,80,512]{2,1,0:T(8,128)(2,1)S(1)} all-to-all(bf16[4,80,512]{2,1,0:T(8,128)(2,1)S(1)} %bitcast.57), channel_id=1, replica_groups=mesh['y'=4,'zh'=2,'core'=2,'zf'=4,'zn'=2,'x'=4] {'y'}, dimensions={0} | all-to-all | bytes 655360 | tf_op jit(solution)/shard_map/all_to_all | solution.py:59
  67.6 7.8 %collective-permute-start.2 = (bf16[80,512]{1,0:T(8,128)(2,1)S(1)}, bf16[80,512]{1,0:T(8,128)(2,1)S(1)}, u32[]{:S(2)}, u32[]{:S(2)}) collective-permute-start(bf16[80,512]{1,0:T(8,128)(2,1)S(1)} %convert_element_type.43), channel_id=1, source_target_pairs={{0,64},{64,0},{1,65},{65,1},{2,66},{66,2},{3,67},{67,3},{4,68},{68... | collective-permute-start | bytes 245768 | tf_op jit(solution)/shard_map/ppermute | solution.py:35
  75.4 7.8 %collective-permute-done.2 = bf16[80,512]{1,0:T(8,128)(2,1)S(1)} collective-permute-done((bf16[80,512]{1,0:T(8,128)(2,1)S(1)}, bf16[80,512]{1,0:T(8,128)(2,1)S(1)}, u32[]{:S(2)}, u32[]{:S(2)}) %collective-permute-start.2) | collective-permute-done | bytes 81952 | tf_op jit(solution)/shard_map/ppermute | solution.py:35
  83.2 0.8 broadcast_select_fusion.1
  84.0 10.1 %all_to_all.32 = bf16[4,80,512]{2,1,0:T(8,128)(2,1)S(1)} all-to-all(bf16[4,80,512]{2,1,0:T(8,128)(2,1)S(1)} %broadcast_in_dim.22), channel_id=1, replica_groups=mesh['y'=4,'zh'=2,'core'=2,'zf'=4,'zn'=2,'x'=4] {'y'}, dimensions={0} | all-to-all | bytes 655360 | tf_op jit(solution)/shard_map/all_to_all | solution.py:31
  94.2 2.7 %all_gather.11 = bf16[640,512]{1,0:T(8,128)(2,1)S(1)} all-gather(bf16[320,512]{1,0:T(8,128)(2,1)S(1)} %bitcast.58), channel_id=1, replica_groups=mesh['y'=4,'zh'=2,'core'=2,'zf'=4,'zn'=2,'x'=4] {'core'}, dimensions={0}, use_global_device_ids=true | all-gather | bytes 983040 | tf_op jit(solution)/shard_map/all_gather | solution.py:71
  96.9 0.9 fusion
  97.8 0.4 copy.14
  98.2 0.1 copy.11
  98.3 23.3 %all_to_all.33 = bf16[8,4,20,8,128]{4,3,2,1,0:T(8,128)(2,1)S(1)} all-to-all(bf16[8,4,20,8,128]{4,3,2,1,0:T(8,128)(2,1)S(1)} %bitcast.54), channel_id=1, replica_groups=mesh['y'=4,'zh'=2,'core'=2,'zf'=4,'zn'=2,'x'=4] {'zn','x'}, dimensions={0} | all-to-all | bytes 2621440 | tf_op jit(solution)/shard_map/all_to_all | solution.py:78
  121.6 0.2 reduce_sum.34
  121.8 21.3 %all_to_all.34 = bf16[4,20,8,128]{3,2,1,0:T(8,128)(2,1)S(1)} all-to-all(bf16[4,20,8,128]{3,2,1,0:T(8,128)(2,1)S(1)} %reduce_sum.34), channel_id=1, replica_groups=mesh['y'=4,'zh'=2,'core'=2,'zf'=4,'zn'=2,'x'=4] {'zf'}, dimensions={0} | all-to-all | bytes 327680 | tf_op jit(solution)/shard_map/all_to_all | solution.py:80
  143.2 0.6 copy.15
  (14 shorter events, 0.2 us)
Async XLA Ops:
  0.6 46.4 %copy-start = (bf16[1024,512]{1,0:T(8,128)(2,1)S(1)}, bf16[1024,512]{1,0:T(8,128)(2,1)}, u32[]{:S(2)}) copy-start(bf16[1024,512]{1,0:T(8,128)(2,1)} %param.5) | copy-start | bytes 3145732
  27.1 5.4 %copy-start.1 = (f32[40,512]{1,0:T(8,128)S(1)}, f32[40,512]{1,0:T(8,128)}, u32[]{:S(2)}) copy-start(f32[40,512]{1,0:T(8,128)} %param.6) | copy-start | bytes 245764
  27.1 5.4 %copy-start.2 = (f32[40,512]{1,0:T(8,128)S(1)}, f32[40,512]{1,0:T(8,128)}, u32[]{:S(2)}) copy-start(f32[40,512]{1,0:T(8,128)} %param.7) | copy-start | bytes 245764
  27.1 19.8 %all-to-all-start.1 = ((bf16[8,4,20,8,128]{4,3,2,1,0:T(8,128)(2,1)}), bf16[8,4,20,8,128]{4,3,2,1,0:T(8,128)(2,1)S(1)}, u32[]{:S(2)}, u32[]{:S(2)}) async-start(bf16[8,4,20,8,128]{4,3,2,1,0:T(8,128)(2,1)} %broadcast_in_dim.10), calls=%async_computation.1 | async-start | bytes 2621440 | tf_op jit(solution)/shard_map/all_to_all | solution.py:31
  32.6 3.2 %collective-permute-start = (bf16[2,40,512]{2,1,0:T(8,128)(2,1)S(1)}, bf16[2,40,512]{2,1,0:T(8,128)(2,1)S(1)}, u32[]{:S(2)}, u32[]{:S(2)}) collective-permute-start(bf16[2,40,512]{2,1,0:T(8,128)(2,1)S(1)} %pad_maximum_fusion), channel_id=1, source_target_pairs={{0,32},{32,0},{1,33},{33,1},{2,34},{34,2},{3,35},{35,3},{4,36},{36... | collective-permute-start | bytes 245768 | tf_op jit(solution)/shard_map/ppermute | solution.py:35
  35.8 20.2 %collective-permute-start.1 = (bf16[2,40,512]{2,1,0:T(8,128)(2,1)S(1)}, bf16[2,40,512]{2,1,0:T(8,128)(2,1)S(1)}, u32[]{:S(2)}, u32[]{:S(2)}) collective-permute-start(bf16[2,40,512]{2,1,0:T(8,128)(2,1)S(1)} %collective-permute-done), channel_id=1, source_target_pairs={{0,96},{32,64},{64,32},{96,0},{1,97},{33,65},{65,33},{97,1},{2,98}... | collective-permute-start | bytes 245768 | tf_op jit(solution)/shard_map/ppermute | solution.py:46
  67.6 15.6 %collective-permute-start.2 = (bf16[80,512]{1,0:T(8,128)(2,1)S(1)}, bf16[80,512]{1,0:T(8,128)(2,1)S(1)}, u32[]{:S(2)}, u32[]{:S(2)}) collective-permute-start(bf16[80,512]{1,0:T(8,128)(2,1)S(1)} %convert_element_type.43), channel_id=1, source_target_pairs={{0,64},{64,0},{1,65},{65,1},{2,66},{66,2},{3,67},{67,3},{4,68},{68... | collective-permute-start | bytes 245768 | tf_op jit(solution)/shard_map/ppermute | solution.py:35

commit v7 on v5

--- a/solution.py
+++ b/solution.py
@@ -13,9 +13,9 @@
 
 F32, BF16 = jnp.float32, jnp.bfloat16
 LANES = 128
-SIZES = {"y": 4, "zh": 2, "core": 2, "zf": 4, "zn": 2, "x": 4}
+SIZES = {"y": 4, "zh": 2, "core": 2, "zf": 4, "zn": 2, "x1": 2, "x0": 2}
 GR = ("y", "zh", "core")
-GC = ("zf", "zn", "x")
+GC = ("zf", "zn", "x1", "x0")
 
 
 def adam_step(rotated, first_moment, second_moment):
@@ -40,12 +40,12 @@
 
 
 def shards(grad, basis, first_moment, second_moment):
-    zh, core = lax.axis_index("zh"), lax.axis_index("core")
+    zh, core, x0 = lax.axis_index("zh"), lax.axis_index("core"), lax.axis_index("x0")
     rows, cols = grad.shape
     moments = jnp.stack([first_moment, second_moment]).astype(BF16)
     block = grad.reshape(rows, cols // LANES, LANES)
     block = spread(block, "zf", 4)
-    block = spread(block, ("zn", "x"), 8)
+    block = spread(block, ("zn", "x1", "x0"), 8)
     block = block.reshape(2, 2, 2, 4, rows, cols // LANES, LANES)
     picked = block.transpose(1, 3, 0, 2, 4, 5, 6).reshape(32 * rows, cols)
 
@@ -53,7 +53,8 @@
     away = lax.dynamic_slice_in_dim(partial, 320 * (1 - core), 320).astype(BF16)
     kept = lax.dynamic_slice_in_dim(partial, 320 * core, 320)
     chip = (kept + swap_cores(away, core).astype(F32)).astype(BF16)
-    chip, moments = lax.optimization_barrier((chip, moments))
+    chip, moments, basis_sent = lax.optimization_barrier((chip, moments, basis))
+    basis_next = swap(basis_sent, "x0")
     first_other, second_other = swap(moments, "zh").astype(F32)
     parts = lax.all_to_all(chip.reshape(4, 80, -1), "y", 0, 0, tiled=True)
     part = jnp.sum(parts.astype(F32), axis=0)
@@ -66,15 +67,20 @@
     pair = jnp.concatenate(
         [jnp.where(first, share, share_other), jnp.where(first, share_other, share)], axis=0
     )
-    direction = spread(pair, "y", 4).reshape(320, -1)
-    direction = lax.all_gather(direction, "core", axis=0, tiled=True)
+    pair = pair.reshape(2, 2, rows, -1).transpose(1, 0, 2, 3).reshape(2, 2 * rows, -1)
+    pair = jnp.broadcast_to(pair[None], (4,) + pair.shape).reshape(8, 2 * rows, -1)
+    pair = lax.all_to_all(pair, ("y", "x0"), 0, 0, tiled=True).reshape(4, 2, 2 * rows, -1)
+    direction = lax.all_gather(pair.transpose(1, 0, 2, 3), "core").reshape(2, 2, 8 * rows, -1)
+    own = lax.dynamic_index_in_dim(direction, x0, 1, keepdims=False).reshape(16 * rows, -1)
+    away = lax.dynamic_index_in_dim(direction, 1 - x0, 1, keepdims=False).reshape(16 * rows, -1)
 
-    total = lax.dot_general(
-        direction, basis, (((1,), (1,)), ((), ())), preferred_element_type=F32
+    total = sum(
+        lax.dot_general(d, b, (((1,), (1,)), ((), ())), preferred_element_type=F32)
+        for d, b in ((own, basis), (away, basis_next))
     ).astype(BF16)
-    total = total.reshape(2, 4, 2, 2, rows, cols // LANES, LANES)
-    total = total.transpose(2, 0, 3, 1, 4, 5, 6).reshape(8, 4, rows, cols // LANES, LANES)
-    total = lax.all_to_all(total, ("zn", "x"), 0, 0, tiled=True)
+    total = total.reshape(2, 4, 2, rows, cols // LANES, LANES)
+    total = total.transpose(2, 0, 1, 3, 4, 5).reshape(4, 4, rows, cols // LANES, LANES)
+    total = lax.all_to_all(total, ("zn", "x1"), 0, 0, tiled=True)
     total = jnp.sum(total.astype(F32), axis=0).astype(BF16)
     total = lax.all_to_all(total, "zf", 0, 0, tiled=True)
     update = jnp.sum(total.astype(F32), axis=0).astype(BF16).reshape(rows, cols)

time: 140 us -> 142 us (1.014)
  blocking collectives: 80.3 us -> 62.5 us
  starting transfers between devices: 27.3 us -> 36.3 us
  waiting for transfers between devices: 24.2 us -> 32.7 us
  local copies, waits for them, and re-layouts: 3.51 us -> 5.16 us
    all_to_all x0 -> x1, waiting for transfers between devices: none -> 11.6 us  [shards(): lax.all_to_all(pair, ('y', 'x0'), 0, 0, tiled=True)]
    all_to_all x2 -> x1, blocking collectives: 35.5 us -> 24.2 us  [spread(): lax.all_to_all(jnp.broadcast_to(block[None], (n,) + block.shape), axes, 0...]
    all_to_all x0 -> x1, starting transfers between devices: none -> 5.88 us  [shards(): lax.all_to_all(pair, ('y', 'x0'), 0, 0, tiled=True)]
    all_to_all x1, blocking collectives: 20.5 us -> 15.2 us  [shards(): total = lax.all_to_all(total, ('zn', 'x1'), 0, 0, tiled=True)]
    ppermute x2 -> x3, waiting for transfers between devices: 9.88 us -> 6.78 us  [swap(): return lax.ppermute(value, axis, [(0, 1), (1, 0)])]
    ppermute x2 -> x3, starting transfers between devices: 17.4 us -> 20.5 us  [swap(): return lax.ppermute(value, axis, [(0, 1), (1, 0)])]
  transfers between devices with their start and end apart: 4 -> 6, of which waited for: 2 -> 3; matrix products, arithmetic and copies ran while one was open for 0% -> 2% of each run, Pallas kernels for 0% -> 0%
where the time goes in v7:
time: 142 us; the launch traced here: 141 us
  blocking collectives  62.5 us (44%)
  starting transfers between devices  36.3 us (26%)
  waiting for transfers between devices  32.7 us (23%)
  local copies, waits for them, and re-layouts  5.16 us (4%)
  matrix products  1.92 us (1%)
  other arithmetic  1.88 us (1%)
    all_to_all x1, blocking collectives, spread(): lax.all_to_all(jnp.broadcast_to(block[None], (n,) + block.shape), axes, 0...  24.2 us
    ppermute x3, starting transfers between devices, swap(): return lax.ppermute(value, axis, [(0, 1), (1, 0)])  20.5 us
    all_to_all x1, blocking collectives, shards(): total = lax.all_to_all(total, 'zf', 0, 0, tiled=True)  18.6 us
    all_to_all x1, blocking collectives, shards(): total = lax.all_to_all(total, ('zn', 'x1'), 0, 0, tiled=True)  15.2 us
    all_to_all x1, waiting for transfers between devices, spread(): lax.all_to_all(jnp.broadcast_to(block[None], (n,) + block.shape), axes, 0...  14.3 us
    all_to_all x1, waiting for transfers between devices, shards(): lax.all_to_all(pair, ('y', 'x0'), 0, 0, tiled=True)  11.6 us
    ppermute x3, waiting for transfers between devices, swap(): return lax.ppermute(value, axis, [(0, 1), (1, 0)])  6.78 us
    all_to_all x1, starting transfers between devices, shards(): lax.all_to_all(pair, ('y', 'x0'), 0, 0, tiled=True)  5.88 us
  transfers between devices with their start and end apart: 6, of which 3 were waited for; matrix products, arithmetic and copies ran while one was open for 2% of the time, Pallas kernels for 0%

profile of v7, /device:TPU:2, one launch (start us, length us, event | category | flops | bytes accessed | tf_op | source)
XLA Modules:
  0.0 141.4 jit_solution(907807782028887340)
XLA Ops:
  0.6 0.8 copy.20
  1.5 24.2 %all_to_all.30 = bf16[4,20,8,128]{3,2,1,0:T(8,128)(2,1)S(1)} all-to-all(bf16[4,20,8,128]{3,2,1,0:T(8,128)(2,1)S(1)} %broadcast_in_dim.21), channel_id=1, replica_groups=mesh['y'=4,'zh'=2,'core'=2,'zf'=4,'zn'=2,'x1'=2,'x0'=2] {'zf'}, dimensions={0} | all-to-all | bytes 327680 | tf_op jit(solution)/shard_map/all_to_all | solution.py:31
  25.7 1.3 broadcast_in_dim.22
  27.0 5.4 %all-to-all-start.1 = ((bf16[8,4,20,8,128]{4,3,2,1,0:T(8,128)(2,1)}), bf16[8,4,20,8,128]{4,3,2,1,0:T(8,128)(2,1)S(1)}, u32[]{:S(2)}, u32[]{:S(2)}) async-start(bf16[8,4,20,8,128]{4,3,2,1,0:T(8,128)(2,1)} %broadcast_in_dim.22), calls=%async_computation.1 | async-start | bytes 2621440 | tf_op jit(solution)/shard_map/all_to_all | solution.py:31
  32.5 14.3 %all-to-all-done.1 = bf16[8,4,20,8,128]{4,3,2,1,0:T(8,128)(2,1)S(1)} async-done(((bf16[8,4,20,8,128]{4,3,2,1,0:T(8,128)(2,1)}), bf16[8,4,20,8,128]{4,3,2,1,0:T(8,128)(2,1)S(1)}, u32[]{:S(2)}, u32[]{:S(2)}) %all-to-all-start.1) | async-done | bytes 1310752 | tf_op jit(solution)/shard_map/all_to_all | solution.py:31
  46.8 0.1 copy.15
  47.0 1.1 copy-done
  48.1 0.8 fusion.1
  48.9 0.1 dynamic-slice_convert_fusion
  49.0 2.3 %all-gather = bf16[640,512]{1,0:T(8,128)(2,1)S(1)} all-gather(bf16[320,512]{1,0:T(8,128)(2,1)S(1)} %dynamic-slice_convert_fusion), channel_id=2, replica_groups=mesh['y'=4,'zh'=2,'core'=2,'zf'=4,'zn'=2,'x1'=2,'x0'=2] {'core'}, dimensions={0}, use_global_device_ids=true | all-gather | bytes 983040 | tf_op jit(solution)/shard_map/all_gather | solution.py:39
  51.2 0.8 fusion.5
  52.1 4.5 %all-to-all-start.2 = ((bf16[4,80,512]{2,1,0:T(8,128)(2,1)}), bf16[4,80,512]{2,1,0:T(8,128)(2,1)S(1)}, u32[]{:S(2)}, u32[]{:S(2)}) async-start(bf16[4,80,512]{2,1,0:T(8,128)(2,1)} %bitcast.6), calls=%async_computation.2 | async-start | bytes 655360 | tf_op jit(solution)/shard_map/all_to_all | solution.py:59
  56.5 9.8 %collective-permute-start.1 = (bf16[2,40,512]{2,1,0:T(8,128)(2,1)S(1)}, bf16[2,40,512]{2,1,0:T(8,128)(2,1)S(1)}, u32[]{:S(2)}, u32[]{:S(2)}) collective-permute-start(bf16[2,40,512]{2,1,0:T(8,128)(2,1)S(1)} %pad_maximum_fusion), channel_id=1, source_target_pairs={{0,64},{64,0},{1,65},{65,1},{2,66},{66,2},{3,67},{67,3},{4,68},{68... | collective-permute-start | bytes 245768 | tf_op jit(solution)/shard_map/ppermute | solution.py:35
  66.4 7.7 %collective-permute-start = (bf16[80,512]{1,0:T(8,128)(2,1)S(1)}, bf16[80,512]{1,0:T(8,128)(2,1)S(1)}, u32[]{:S(2)}, u32[]{:S(2)}) collective-permute-start(bf16[80,512]{1,0:T(8,128)(2,1)S(1)} %convert_element_type.43), channel_id=1, source_target_pairs={{0,64},{64,0},{1,65},{65,1},{2,66},{66,2},{3,67},{67,3},{4,68},{68... | collective-permute-start | bytes 245768 | tf_op jit(solution)/shard_map/ppermute | solution.py:35
  74.1 3.1 %collective-permute-start.2 = (bf16[1024,512]{1,0:T(8,128)(2,1)S(1)}, bf16[1024,512]{1,0:T(8,128)(2,1)S(1)}, u32[]{:S(2)}, u32[]{:S(2)}) collective-permute-start(bf16[1024,512]{1,0:T(8,128)(2,1)S(1)} %copy-done), channel_id=1, source_target_pairs={{0,1},{1,0},{2,3},{3,2},{4,5},{5,4},{6,7},{7,6},{8,9},{9,8},{10,11... | collective-permute-start | bytes 3145736 | tf_op jit(solution)/shard_map/ppermute | solution.py:35
  77.2 6.8 %collective-permute-done = bf16[80,512]{1,0:T(8,128)(2,1)S(1)} collective-permute-done((bf16[80,512]{1,0:T(8,128)(2,1)S(1)}, bf16[80,512]{1,0:T(8,128)(2,1)S(1)}, u32[]{:S(2)}, u32[]{:S(2)}) %collective-permute-start) | collective-permute-done | bytes 81952 | tf_op jit(solution)/shard_map/ppermute | solution.py:35
  84.0 0.8 broadcast_select_fusion.1
  84.8 0.1 copy.16
  84.9 0.8 broadcast_in_dim.24
  85.7 5.9 %all-to-all-start.3 = ((bf16[8,40,512]{2,1,0:T(8,128)(2,1)}), bf16[8,40,512]{2,1,0:T(8,128)(2,1)S(1)}, u32[]{:S(2)}, u32[]{:S(2)}) async-start(bf16[8,40,512]{2,1,0:T(8,128)(2,1)} %bitcast.11), calls=%async_computation.3 | async-start | bytes 655360 | tf_op jit(solution)/shard_map/all_to_all | solution.py:72
  91.6 11.6 %all-to-all-done.3 = bf16[8,40,512]{2,1,0:T(8,128)(2,1)S(1)} async-done(((bf16[8,40,512]{2,1,0:T(8,128)(2,1)}), bf16[8,40,512]{2,1,0:T(8,128)(2,1)S(1)}, u32[]{:S(2)}, u32[]{:S(2)}) %all-to-all-start.3) | async-done | bytes 327712 | tf_op jit(solution)/shard_map/all_to_all | solution.py:72
  103.2 2.3 %all-gather.1 = bf16[4,4,40,512]{3,2,0,1:T(8,128)(2,1)S(1)} all-gather(bf16[2,4,40,512]{3,2,0,1:T(8,128)(2,1)S(1)} %bitcast.69), channel_id=3, replica_groups=mesh['y'=4,'zh'=2,'core'=2,'zf'=4,'zn'=2,'x1'=2,'x0'=2] {'core'}, dimensions={0}, use_global_device_ids=true | all-gather | bytes 983040 | tf_op jit(solution)/shard_map/all_gather | solution.py:73
  105.5 0.1 copy.18
  105.5 0.1 constant_dynamic-slice_fusion.1
  105.6 0.5 fusion.19
  106.1 0.0 collective-permute-done.2
  106.1 0.5 fusion.4
  106.7 0.1 copy.22
  106.9 15.2 %all_to_all.31 = bf16[4,4,20,8,128]{4,3,2,1,0:T(8,128)(2,1)S(1)} all-to-all(bf16[4,4,20,8,128]{4,3,2,1,0:T(8,128)(2,1)S(1)} %bitcast.65), channel_id=1, replica_groups=mesh['y'=4,'zh'=2,'core'=2,'zf'=4,'zn'=2,'x1'=2,'x0'=2] {'zn','x1'}, dimensions={0} | all-to-all | bytes 1310720 | tf_op jit(solution)/shard_map/all_to_all | solution.py:83
  122.0 0.1 reduce_sum.34
  122.2 18.6 %all_to_all.32 = bf16[4,20,8,128]{3,2,1,0:T(8,128)(2,1)S(1)} all-to-all(bf16[4,20,8,128]{3,2,1,0:T(8,128)(2,1)S(1)} %reduce_sum.34), channel_id=1, replica_groups=mesh['y'=4,'zh'=2,'core'=2,'zf'=4,'zn'=2,'x1'=2,'x0'=2] {'zf'}, dimensions={0} | all-to-all | bytes 327680 | tf_op jit(solution)/shard_map/all_to_all | solution.py:85
  140.7 0.6 copy.23
  (22 shorter events, 0.3 us)
Async XLA Ops:
  27.0 5.4 %copy-start.1 = (f32[40,512]{1,0:T(8,128)S(1)}, f32[40,512]{1,0:T(8,128)}, u32[]{:S(2)}) copy-start(f32[40,512]{1,0:T(8,128)} %param.6) | copy-start | bytes 245764
  27.0 5.4 %copy-start.2 = (f32[40,512]{1,0:T(8,128)S(1)}, f32[40,512]{1,0:T(8,128)}, u32[]{:S(2)}) copy-start(f32[40,512]{1,0:T(8,128)} %param.7) | copy-start | bytes 245764
  27.0 19.8 %all-to-all-start.1 = ((bf16[8,4,20,8,128]{4,3,2,1,0:T(8,128)(2,1)}), bf16[8,4,20,8,128]{4,3,2,1,0:T(8,128)(2,1)S(1)}, u32[]{:S(2)}, u32[]{:S(2)}) async-start(bf16[8,4,20,8,128]{4,3,2,1,0:T(8,128)(2,1)} %broadcast_in_dim.22), calls=%async_computation.1 | async-start | bytes 2621440 | tf_op jit(solution)/shard_map/all_to_all | solution.py:31
  46.8 1.2 copy-start
  52.1 14.2 %all-to-all-start.2 = ((bf16[4,80,512]{2,1,0:T(8,128)(2,1)}), bf16[4,80,512]{2,1,0:T(8,128)(2,1)S(1)}, u32[]{:S(2)}, u32[]{:S(2)}) async-start(bf16[4,80,512]{2,1,0:T(8,128)(2,1)} %bitcast.6), calls=%async_computation.2 | async-start | bytes 655360 | tf_op jit(solution)/shard_map/all_to_all | solution.py:59
  56.5 20.6 %collective-permute-start.1 = (bf16[2,40,512]{2,1,0:T(8,128)(2,1)S(1)}, bf16[2,40,512]{2,1,0:T(8,128)(2,1)S(1)}, u32[]{:S(2)}, u32[]{:S(2)}) collective-permute-start(bf16[2,40,512]{2,1,0:T(8,128)(2,1)S(1)} %pad_maximum_fusion), channel_id=1, source_target_pairs={{0,64},{64,0},{1,65},{65,1},{2,66},{66,2},{3,67},{67,3},{4,68},{68... | collective-permute-start | bytes 245768 | tf_op jit(solution)/shard_map/ppermute | solution.py:35
  66.4 17.6 %collective-permute-start = (bf16[80,512]{1,0:T(8,128)(2,1)S(1)}, bf16[80,512]{1,0:T(8,128)(2,1)S(1)}, u32[]{:S(2)}, u32[]{:S(2)}) collective-permute-start(bf16[80,512]{1,0:T(8,128)(2,1)S(1)} %convert_element_type.43), channel_id=1, source_target_pairs={{0,64},{64,0},{1,65},{65,1},{2,66},{66,2},{3,67},{67,3},{4,68},{68... | collective-permute-start | bytes 245768 | tf_op jit(solution)/shard_map/ppermute | solution.py:35
  74.1 32.0 %collective-permute-start.2 = (bf16[1024,512]{1,0:T(8,128)(2,1)S(1)}, bf16[1024,512]{1,0:T(8,128)(2,1)S(1)}, u32[]{:S(2)}, u32[]{:S(2)}) collective-permute-start(bf16[1024,512]{1,0:T(8,128)(2,1)S(1)} %copy-done), channel_id=1, source_target_pairs={{0,1},{1,0},{2,3},{3,2},{4,5},{5,4},{6,7},{7,6},{8,9},{9,8},{10,11... | collective-permute-start | bytes 3145736 | tf_op jit(solution)/shard_map/ppermute | solution.py:35
  85.7 17.5 %all-to-all-start.3 = ((bf16[8,40,512]{2,1,0:T(8,128)(2,1)}), bf16[8,40,512]{2,1,0:T(8,128)(2,1)S(1)}, u32[]{:S(2)}, u32[]{:S(2)}) async-start(bf16[8,40,512]{2,1,0:T(8,128)(2,1)} %bitcast.11), calls=%async_computation.3 | async-start | bytes 655360 | tf_op jit(solution)/shard_map/all_to_all | solution.py:72

commit v8 on v6

--- a/solution.py
+++ b/solution.py
@@ -35,15 +35,16 @@
     return lax.ppermute(value, axis, [(0, 1), (1, 0)])
 
 
-def swap_cores(value, core):
-    return lax.dynamic_index_in_dim(lax.all_gather(value, "core"), 1 - core, keepdims=False)
+def swap_gathered(value, axis):
+    return lax.dynamic_index_in_dim(
+        lax.all_gather(value, axis), 1 - lax.axis_index(axis), keepdims=False
+    )
 
 
 def shards(grad, basis, first_moment, second_moment):
     zh, core = lax.axis_index("zh"), lax.axis_index("core")
     rows, cols = grad.shape
-    moments = swap(jnp.stack([first_moment, second_moment]).astype(BF16), "core")
-    moments = lax.ppermute(moments, ("zh", "core"), [(i, 3 - i) for i in range(4)])
+    moments = swap(jnp.stack([first_moment, second_moment]).astype(BF16), "zh")
     block = grad.reshape(rows, cols // LANES, LANES)
     block = spread(block, "zf", 4)
     block = spread(block, ("zn", "x"), 8)
@@ -53,12 +54,12 @@
     partial = jnp.dot(picked, basis, preferred_element_type=F32)
     away = lax.dynamic_slice_in_dim(partial, 320 * (1 - core), 320).astype(BF16)
     kept = lax.dynamic_slice_in_dim(partial, 320 * core, 320)
-    chip = (kept + swap_cores(away, core).astype(F32)).astype(BF16)
+    chip = (kept + swap_gathered(away, "core").astype(F32)).astype(BF16)
     chip, moments = lax.optimization_barrier((chip, moments))
     first_other, second_other = moments.astype(F32)
     parts = lax.all_to_all(chip.reshape(4, 80, -1), "y", 0, 0, tiled=True)
     part = jnp.sum(parts.astype(F32), axis=0)
-    rotated = part + swap(part.astype(BF16), "zh").astype(F32)
+    rotated = part + swap_gathered(part.astype(BF16), "zh").astype(F32)
     low, high = rotated[:40], rotated[40:]
     first = zh == 0
     mine, other = jnp.where(first, low, high), jnp.where(first, high, low)

time: 144 us -> 142 us (0.986)
  starting transfers between devices: 23.4 us -> 18.5 us
  waiting for transfers between devices: 17.6 us -> 20.6 us
    all_gather x1 -> x2, blocking collectives: 2.28 us -> 18.6 us  [swap_gathered(): lax.all_gather(value, axis)]
    all_to_all x1 -> x0, blocking collectives: 11.5 us -> none  [shards(): parts = lax.all_to_all(chip.reshape(4, 80, -1), 'y', 0, 0, tiled=True)]
    ppermute x1 -> x0, starting transfers between devices: 8.3 us -> none  [shards(): lax.ppermute(moments, ('zh', 'core'), [(i, 3 - i) for i in range(4)])]
    all_to_all x1, waiting for transfers between devices: 2.84 us -> 10.5 us  [spread(): lax.all_to_all(jnp.broadcast_to(block[None], (n,) + block.shape), axes, 0...]
    all_to_all x0 -> x1, waiting for transfers between devices: none -> 7.01 us  [shards(): parts = lax.all_to_all(chip.reshape(4, 80, -1), 'y', 0, 0, tiled=True)]
    ppermute x2 -> x1, waiting for transfers between devices: 9.03 us -> 3.16 us  [swap(): return lax.ppermute(value, axis, [(0, 1), (1, 0)])]
    ppermute x1 -> x0, waiting for transfers between devices: 5.68 us -> none  [shards(): lax.ppermute(moments, ('zh', 'core'), [(i, 3 - i) for i in range(4)])]
    all_to_all x0 -> x1, starting transfers between devices: none -> 4.46 us  [shards(): parts = lax.all_to_all(chip.reshape(4, 80, -1), 'y', 0, 0, tiled=True)]
  transfers between devices with their start and end apart: 4 -> 3, of which waited for: 4 -> 3; matrix products, arithmetic and copies ran while one was open for 1% -> 1% of each run, Pallas kernels for 0% -> 0%
where the time goes in v8:
time: 142 us
  blocking collectives  94.8 us (67%)
  waiting for transfers between devices  20.6 us (15%)
  starting transfers between devices  18.5 us (13%)
  local copies, waits for them, and re-layouts  3.52 us (2%)
  other arithmetic  1.95 us (1%)
  matrix products  1.71 us (1%)
    all_to_all x2, blocking collectives, spread(): lax.all_to_all(jnp.broadcast_to(block[None], (n,) + block.shape), axes, 0...  33.7 us
    all_to_all x1, blocking collectives, shards(): total = lax.all_to_all(total, ('zn', 'x'), 0, 0, tiled=True)  21.5 us
    all_to_all x1, blocking collectives, shards(): total = lax.all_to_all(total, 'zf', 0, 0, tiled=True)  18.7 us
    all_gather x2, blocking collectives, swap_gathered(): lax.all_gather(value, axis)  18.6 us
    all_to_all x1, waiting for transfers between devices, spread(): lax.all_to_all(jnp.broadcast_to(block[None], (n,) + block.shape), axes, 0...  10.5 us
    ppermute x1, starting transfers between devices, swap(): return lax.ppermute(value, axis, [(0, 1), (1, 0)])  8.55 us
    all_to_all x1, waiting for transfers between devices, shards(): parts = lax.all_to_all(chip.reshape(4, 80, -1), 'y', 0, 0, tiled=True)  7.01 us
    all_to_all x1, starting transfers between devices, spread(): lax.all_to_all(jnp.broadcast_to(block[None], (n,) + block.shape), axes, 0...  5.44 us
  transfers between devices with their start and end apart: 3, of which 3 were waited for; matrix products, arithmetic and copies ran while one was open for 1% of the time, Pallas kernels for 0%

profile of v8, /device:TPU:2, one launch (start us, length us, event | category | flops | bytes accessed | tf_op | source)
XLA Modules:
  0.0 141.8 jit_solution(13237275456514593614)
XLA Ops:
  0.6 0.0 copy-start
  0.6 0.9 copy.12
  1.6 24.2 %all_to_all.30 = bf16[4,20,8,128]{3,2,1,0:T(8,128)(2,1)S(1)} all-to-all(bf16[4,20,8,128]{3,2,1,0:T(8,128)(2,1)S(1)} %broadcast_in_dim.9), channel_id=1, replica_groups=mesh['y'=4,'zh'=2,'core'=2,'zf'=4,'zn'=2,'x'=4] {'zf'}, dimensions={0} | all-to-all | bytes 327680 | tf_op jit(solution)/shard_map/all_to_all | solution.py:31
  25.8 1.3 broadcast_in_dim.10
  27.1 0.0 copy-start.1
  27.1 0.0 copy-start.2
  27.1 5.4 %all-to-all-start.1 = ((bf16[8,4,20,8,128]{4,3,2,1,0:T(8,128)(2,1)}), bf16[8,4,20,8,128]{4,3,2,1,0:T(8,128)(2,1)S(1)}, u32[]{:S(2)}, u32[]{:S(2)}) async-start(bf16[8,4,20,8,128]{4,3,2,1,0:T(8,128)(2,1)} %broadcast_in_dim.10), calls=%async_computation.1 | async-start | bytes 2621440 | tf_op jit(solution)/shard_map/all_to_all | solution.py:31
  32.6 0.0 copy-done.1
  32.6 0.0 copy-done.2
  32.6 8.6 %collective-permute-start = (bf16[2,40,512]{2,1,0:T(8,128)(2,1)S(1)}, bf16[2,40,512]{2,1,0:T(8,128)(2,1)S(1)}, u32[]{:S(2)}, u32[]{:S(2)}) collective-permute-start(bf16[2,40,512]{2,1,0:T(8,128)(2,1)S(1)} %pad_maximum_fusion), channel_id=1, source_target_pairs={{0,64},{64,0},{1,65},{65,1},{2,66},{66,2},{3,67},{67,3},{4,68},{68... | collective-permute-start | bytes 245768 | tf_op jit(solution)/shard_map/ppermute | solution.py:35
  41.2 10.5 %all-to-all-done.1 = bf16[8,4,20,8,128]{4,3,2,1,0:T(8,128)(2,1)S(1)} async-done(((bf16[8,4,20,8,128]{4,3,2,1,0:T(8,128)(2,1)}), bf16[8,4,20,8,128]{4,3,2,1,0:T(8,128)(2,1)S(1)}, u32[]{:S(2)}, u32[]{:S(2)}) %all-to-all-start.1) | async-done | bytes 1310752 | tf_op jit(solution)/shard_map/all_to_all | solution.py:31
  51.6 0.1 copy.10
  51.8 0.0 copy-done
  51.8 0.8 fusion.1
  52.6 0.1 dynamic-slice_convert_fusion
  52.7 2.3 %all-gather = bf16[640,512]{1,0:T(8,128)(2,1)S(1)} all-gather(bf16[320,512]{1,0:T(8,128)(2,1)S(1)} %dynamic-slice_convert_fusion), channel_id=2, replica_groups=mesh['y'=4,'zh'=2,'core'=2,'zf'=4,'zn'=2,'x'=4] {'core'}, dimensions={0}, use_global_device_ids=true | all-gather | bytes 983040 | tf_op jit(solution)/shard_map/all_gather | solution.py:40
  54.9 0.8 fusion.4
  55.8 3.2 %collective-permute-done = bf16[2,40,512]{2,1,0:T(8,128)(2,1)S(1)} collective-permute-done((bf16[2,40,512]{2,1,0:T(8,128)(2,1)S(1)}, bf16[2,40,512]{2,1,0:T(8,128)(2,1)S(1)}, u32[]{:S(2)}, u32[]{:S(2)}) %collective-permute-start) | collective-permute-done | bytes 81952 | tf_op jit(solution)/shard_map/ppermute | solution.py:35
  58.9 4.5 %all-to-all-start.2 = ((bf16[4,80,512]{2,1,0:T(8,128)(2,1)}), bf16[4,80,512]{2,1,0:T(8,128)(2,1)S(1)}, u32[]{:S(2)}, u32[]{:S(2)}) async-start(bf16[4,80,512]{2,1,0:T(8,128)(2,1)} %bitcast.6), calls=%async_computation.2 | async-start | bytes 655360 | tf_op jit(solution)/shard_map/all_to_all | solution.py:60
  63.4 7.0 %all-to-all-done.2 = bf16[4,80,512]{2,1,0:T(8,128)(2,1)S(1)} async-done(((bf16[4,80,512]{2,1,0:T(8,128)(2,1)}), bf16[4,80,512]{2,1,0:T(8,128)(2,1)S(1)}, u32[]{:S(2)}, u32[]{:S(2)}) %all-to-all-start.2) | async-done | bytes 327712 | tf_op jit(solution)/shard_map/all_to_all | solution.py:60
  70.5 16.3 %all-gather.1 = bf16[160,512]{1,0:T(8,128)(2,1)S(1)} all-gather(bf16[80,512]{1,0:T(8,128)(2,1)S(1)} %convert_element_type.56), channel_id=3, replica_groups=mesh['y'=4,'zh'=2,'core'=2,'zf'=4,'zn'=2,'x'=4] {'zh'}, dimensions={0}, use_global_device_ids=true | all-gather | bytes 245760 | tf_op jit(solution)/shard_map/all_gather | solution.py:40
  86.8 0.8 broadcast_select_fusion.1
  87.6 9.4 %all_to_all.31 = bf16[4,80,512]{2,1,0:T(8,128)(2,1)S(1)} all-to-all(bf16[4,80,512]{2,1,0:T(8,128)(2,1)S(1)} %broadcast_in_dim.22), channel_id=1, replica_groups=mesh['y'=4,'zh'=2,'core'=2,'zf'=4,'zn'=2,'x'=4] {'y'}, dimensions={0} | all-to-all | bytes 655360 | tf_op jit(solution)/shard_map/all_to_all | solution.py:31
  97.0 2.3 %all_gather.16 = bf16[640,512]{1,0:T(8,128)(2,1)S(1)} all-gather(bf16[320,512]{1,0:T(8,128)(2,1)S(1)} %bitcast.61), channel_id=1, replica_groups=mesh['y'=4,'zh'=2,'core'=2,'zf'=4,'zn'=2,'x'=4] {'core'}, dimensions={0}, use_global_device_ids=true | all-gather | bytes 983040 | tf_op jit(solution)/shard_map/all_gather | solution.py:72
  99.3 0.9 fusion
  100.2 0.4 copy.14
  100.6 0.1 copy.11
  100.7 21.5 %all_to_all.32 = bf16[8,4,20,8,128]{4,3,2,1,0:T(8,128)(2,1)S(1)} all-to-all(bf16[8,4,20,8,128]{4,3,2,1,0:T(8,128)(2,1)S(1)} %bitcast.58), channel_id=1, replica_groups=mesh['y'=4,'zh'=2,'core'=2,'zf'=4,'zn'=2,'x'=4] {'zn','x'}, dimensions={0} | all-to-all | bytes 2621440 | tf_op jit(solution)/shard_map/all_to_all | solution.py:79
  122.2 0.2 reduce_sum.34
  122.4 18.7 %all_to_all.33 = bf16[4,20,8,128]{3,2,1,0:T(8,128)(2,1)S(1)} all-to-all(bf16[4,20,8,128]{3,2,1,0:T(8,128)(2,1)S(1)} %reduce_sum.34), channel_id=1, replica_groups=mesh['y'=4,'zh'=2,'core'=2,'zf'=4,'zn'=2,'x'=4] {'zf'}, dimensions={0} | all-to-all | bytes 327680 | tf_op jit(solution)/shard_map/all_to_all | solution.py:81
  141.2 0.6 copy.15
  (13 shorter events, 0.2 us)
Async XLA Ops:
  0.6 51.1 %copy-start = (bf16[1024,512]{1,0:T(8,128)(2,1)S(1)}, bf16[1024,512]{1,0:T(8,128)(2,1)}, u32[]{:S(2)}) copy-start(bf16[1024,512]{1,0:T(8,128)(2,1)} %param.5) | copy-start | bytes 3145732
  27.1 5.4 %copy-start.1 = (f32[40,512]{1,0:T(8,128)S(1)}, f32[40,512]{1,0:T(8,128)}, u32[]{:S(2)}) copy-start(f32[40,512]{1,0:T(8,128)} %param.6) | copy-start | bytes 245764
  27.1 5.4 %copy-start.2 = (f32[40,512]{1,0:T(8,128)S(1)}, f32[40,512]{1,0:T(8,128)}, u32[]{:S(2)}) copy-start(f32[40,512]{1,0:T(8,128)} %param.7) | copy-start | bytes 245764
  27.1 24.5 %all-to-all-start.1 = ((bf16[8,4,20,8,128]{4,3,2,1,0:T(8,128)(2,1)}), bf16[8,4,20,8,128]{4,3,2,1,0:T(8,128)(2,1)S(1)}, u32[]{:S(2)}, u32[]{:S(2)}) async-start(bf16[8,4,20,8,128]{4,3,2,1,0:T(8,128)(2,1)} %broadcast_in_dim.10), calls=%async_computation.1 | async-start | bytes 2621440 | tf_op jit(solution)/shard_map/all_to_all | solution.py:31
  32.6 26.3 %collective-permute-start = (bf16[2,40,512]{2,1,0:T(8,128)(2,1)S(1)}, bf16[2,40,512]{2,1,0:T(8,128)(2,1)S(1)}, u32[]{:S(2)}, u32[]{:S(2)}) collective-permute-start(bf16[2,40,512]{2,1,0:T(8,128)(2,1)S(1)} %pad_maximum_fusion), channel_id=1, source_target_pairs={{0,64},{64,0},{1,65},{65,1},{2,66},{66,2},{3,67},{67,3},{4,68},{68... | collective-permute-start | bytes 245768 | tf_op jit(solution)/shard_map/ppermute | solution.py:35
  58.9 11.5 %all-to-all-start.2 = ((bf16[4,80,512]{2,1,0:T(8,128)(2,1)}), bf16[4,80,512]{2,1,0:T(8,128)(2,1)S(1)}, u32[]{:S(2)}, u32[]{:S(2)}) async-start(bf16[4,80,512]{2,1,0:T(8,128)(2,1)} %bitcast.6), calls=%async_computation.2 | async-start | bytes 655360 | tf_op jit(solution)/shard_map/all_to_all | solution.py:60

commit v9 on v8

--- a/solution.py
+++ b/solution.py
@@ -44,7 +44,7 @@
 def shards(grad, basis, first_moment, second_moment):
     zh, core = lax.axis_index("zh"), lax.axis_index("core")
     rows, cols = grad.shape
-    moments = swap(jnp.stack([first_moment, second_moment]).astype(BF16), "zh")
+    first_other = swap(first_moment.astype(BF16), "zh")
     block = grad.reshape(rows, cols // LANES, LANES)
     block = spread(block, "zf", 4)
     block = spread(block, ("zn", "x"), 8)
@@ -55,8 +55,9 @@
     away = lax.dynamic_slice_in_dim(partial, 320 * (1 - core), 320).astype(BF16)
     kept = lax.dynamic_slice_in_dim(partial, 320 * core, 320)
     chip = (kept + swap_gathered(away, "core").astype(F32)).astype(BF16)
-    chip, moments = lax.optimization_barrier((chip, moments))
-    first_other, second_other = moments.astype(F32)
+    chip, first_other, second_sent = lax.optimization_barrier((chip, first_other, second_moment))
+    second_other = swap(second_sent.astype(BF16), "zh").astype(F32)
+    first_other = first_other.astype(F32)
     parts = lax.all_to_all(chip.reshape(4, 80, -1), "y", 0, 0, tiled=True)
     part = jnp.sum(parts.astype(F32), axis=0)
     rotated = part + swap_gathered(part.astype(BF16), "zh").astype(F32)

time: 142 us -> 141 us (level)
  waiting for transfers between devices: 20.6 us -> 11.9 us
  starting transfers between devices: 18.5 us -> 24.2 us
    all_to_all x1, waiting for transfers between devices: 7.01 us -> 1.3 us  [shards(): parts = lax.all_to_all(chip.reshape(4, 80, -1), 'y', 0, 0, tiled=True)]
    ppermute x1 -> x2, starting transfers between devices: 8.55 us -> 14.3 us  [swap(): return lax.ppermute(value, axis, [(0, 1), (1, 0)])]
    all_to_all x1, waiting for transfers between devices: 10.5 us -> 6.99 us  [spread(): lax.all_to_all(jnp.broadcast_to(block[None], (n,) + block.shape), axes, 0...]
    all_to_all x2, blocking collectives: 33.7 us -> 36.5 us  [spread(): lax.all_to_all(jnp.broadcast_to(block[None], (n,) + block.shape), axes, 0...]
    all_to_all x1, blocking collectives: 18.7 us -> 16.1 us  [shards(): total = lax.all_to_all(total, 'zf', 0, 0, tiled=True)]
    all_to_all x1, blocking collectives: 21.5 us -> 23.2 us  [shards(): total = lax.all_to_all(total, ('zn', 'x'), 0, 0, tiled=True)]
    ppermute x1 -> x2, waiting for transfers between devices: 3.16 us -> 3.65 us  [swap(): return lax.ppermute(value, axis, [(0, 1), (1, 0)])]
  transfers between devices with their start and end apart: 3 -> 4, of which waited for: 3 -> 3; matrix products, arithmetic and copies ran while one was open for 1% -> 1% of each run, Pallas kernels for 0% -> 0%
where the time goes in v9:
time: 141 us; the launch traced here: 140 us
  blocking collectives  96.2 us (68%)
  starting transfers between devices  24.2 us (17%)
  waiting for transfers between devices  11.9 us (8%)
  local copies, waits for them, and re-layouts  3.52 us (2%)
  other arithmetic  1.93 us (1%)
  matrix products  1.71 us (1%)
    all_to_all x2, blocking collectives, spread(): lax.all_to_all(jnp.broadcast_to(block[None], (n,) + block.shape), axes, 0...  36.5 us
    all_to_all x1, blocking collectives, shards(): total = lax.all_to_all(total, ('zn', 'x'), 0, 0, tiled=True)  23.2 us
    all_gather x2, blocking collectives, swap_gathered(): lax.all_gather(value, axis)  18.2 us
    all_to_all x1, blocking collectives, shards(): total = lax.all_to_all(total, 'zf', 0, 0, tiled=True)  16.1 us
    ppermute x2, starting transfers between devices, swap(): return lax.ppermute(value, axis, [(0, 1), (1, 0)])  14.3 us
    all_to_all x1, waiting for transfers between devices, spread(): lax.all_to_all(jnp.broadcast_to(block[None], (n,) + block.shape), axes, 0...  6.99 us
    all_to_all x1, starting transfers between devices, spread(): lax.all_to_all(jnp.broadcast_to(block[None], (n,) + block.shape), axes, 0...  5.44 us
    all_to_all x1, starting transfers between devices, shards(): parts = lax.all_to_all(chip.reshape(4, 80, -1), 'y', 0, 0, tiled=True)  4.46 us
  transfers between devices with their start and end apart: 4, of which 3 were waited for; matrix products, arithmetic and copies ran while one was open for 1% of the time, Pallas kernels for 0%

profile of v9, /device:TPU:2, one launch (start us, length us, event | category | flops | bytes accessed | tf_op | source)
XLA Modules:
  0.0 140.2 jit_solution(4636304597600985872)
XLA Ops:
  0.6 0.0 copy-start
  0.6 0.9 copy.12
  1.6 24.2 %all_to_all.30 = bf16[4,20,8,128]{3,2,1,0:T(8,128)(2,1)S(1)} all-to-all(bf16[4,20,8,128]{3,2,1,0:T(8,128)(2,1)S(1)} %broadcast_in_dim.9), channel_id=1, replica_groups=mesh['y'=4,'zh'=2,'core'=2,'zf'=4,'zn'=2,'x'=4] {'zf'}, dimensions={0} | all-to-all | bytes 327680 | tf_op jit(solution)/shard_map/all_to_all | solution.py:31
  25.8 1.3 broadcast_in_dim.10
  27.1 5.4 %all-to-all-start.1 = ((bf16[8,4,20,8,128]{4,3,2,1,0:T(8,128)(2,1)}), bf16[8,4,20,8,128]{4,3,2,1,0:T(8,128)(2,1)S(1)}, u32[]{:S(2)}, u32[]{:S(2)}) async-start(bf16[8,4,20,8,128]{4,3,2,1,0:T(8,128)(2,1)} %broadcast_in_dim.10), calls=%async_computation.1 | async-start | bytes 2621440 | tf_op jit(solution)/shard_map/all_to_all | solution.py:31
  32.6 0.0 copy-done.1
  32.6 8.6 %collective-permute-start = (bf16[40,512]{1,0:T(8,128)(2,1)S(1)}, bf16[40,512]{1,0:T(8,128)(2,1)S(1)}, u32[]{:S(2)}, u32[]{:S(2)}) collective-permute-start(bf16[40,512]{1,0:T(8,128)(2,1)S(1)} %convert_element_type.63), channel_id=1, source_target_pairs={{0,64},{64,0},{1,65},{65,1},{2,66},{66,2},{3,67},{67,3},{4,68},{68... | collective-permute-start | bytes 122888 | tf_op jit(solution)/shard_map/ppermute | solution.py:35
  41.1 7.0 %all-to-all-done.1 = bf16[8,4,20,8,128]{4,3,2,1,0:T(8,128)(2,1)S(1)} async-done(((bf16[8,4,20,8,128]{4,3,2,1,0:T(8,128)(2,1)}), bf16[8,4,20,8,128]{4,3,2,1,0:T(8,128)(2,1)S(1)}, u32[]{:S(2)}, u32[]{:S(2)}) %all-to-all-start.1) | async-done | bytes 1310752 | tf_op jit(solution)/shard_map/all_to_all | solution.py:31
  48.1 0.1 copy.10
  48.3 0.0 copy-done
  48.3 0.8 fusion.1
  49.1 0.1 dynamic-slice_convert_fusion
  49.2 0.0 copy-start.2
  49.2 2.4 %all-gather = bf16[640,512]{1,0:T(8,128)(2,1)S(1)} all-gather(bf16[320,512]{1,0:T(8,128)(2,1)S(1)} %dynamic-slice_convert_fusion), channel_id=2, replica_groups=mesh['y'=4,'zh'=2,'core'=2,'zf'=4,'zn'=2,'x'=4] {'core'}, dimensions={0}, use_global_device_ids=true | all-gather | bytes 983040 | tf_op jit(solution)/shard_map/all_gather | solution.py:40
  51.6 0.8 fusion.4
  52.4 3.6 %collective-permute-done = bf16[40,512]{1,0:T(8,128)(2,1)S(1)} collective-permute-done((bf16[40,512]{1,0:T(8,128)(2,1)S(1)}, bf16[40,512]{1,0:T(8,128)(2,1)S(1)}, u32[]{:S(2)}, u32[]{:S(2)}) %collective-permute-start) | collective-permute-done | bytes 40992 | tf_op jit(solution)/shard_map/ppermute | solution.py:35
  56.0 4.5 %all-to-all-start.2 = ((bf16[4,80,512]{2,1,0:T(8,128)(2,1)}), bf16[4,80,512]{2,1,0:T(8,128)(2,1)S(1)}, u32[]{:S(2)}, u32[]{:S(2)}) async-start(bf16[4,80,512]{2,1,0:T(8,128)(2,1)} %bitcast.4), calls=%async_computation.2 | async-start | bytes 655360 | tf_op jit(solution)/shard_map/all_to_all | solution.py:61
  60.5 0.0 copy-done.2
  60.5 5.7 %collective-permute-start.1 = (bf16[40,512]{1,0:T(8,128)(2,1)S(1)}, bf16[40,512]{1,0:T(8,128)(2,1)S(1)}, u32[]{:S(2)}, u32[]{:S(2)}) collective-permute-start(bf16[40,512]{1,0:T(8,128)(2,1)S(1)} %convert_element_type.71), channel_id=1, source_target_pairs={{0,64},{64,0},{1,65},{65,1},{2,66},{66,2},{3,67},{67,3},{4,68},{68... | collective-permute-start | bytes 122888 | tf_op jit(solution)/shard_map/ppermute | solution.py:35
  66.2 1.3 all-to-all-done.2
  67.6 15.8 %all-gather.1 = bf16[160,512]{1,0:T(8,128)(2,1)S(1)} all-gather(bf16[80,512]{1,0:T(8,128)(2,1)S(1)} %convert_element_type.65), channel_id=3, replica_groups=mesh['y'=4,'zh'=2,'core'=2,'zf'=4,'zn'=2,'x'=4] {'zh'}, dimensions={0}, use_global_device_ids=true | all-gather | bytes 245760 | tf_op jit(solution)/shard_map/all_gather | solution.py:40
  83.4 0.0 collective-permute-done.1
  83.4 0.8 broadcast_select_fusion.1
  84.3 12.2 %all_to_all.31 = bf16[4,80,512]{2,1,0:T(8,128)(2,1)S(1)} all-to-all(bf16[4,80,512]{2,1,0:T(8,128)(2,1)S(1)} %broadcast_in_dim.22), channel_id=1, replica_groups=mesh['y'=4,'zh'=2,'core'=2,'zf'=4,'zn'=2,'x'=4] {'y'}, dimensions={0} | all-to-all | bytes 655360 | tf_op jit(solution)/shard_map/all_to_all | solution.py:31
  96.5 2.3 %all_gather.16 = bf16[640,512]{1,0:T(8,128)(2,1)S(1)} all-gather(bf16[320,512]{1,0:T(8,128)(2,1)S(1)} %bitcast.39), channel_id=1, replica_groups=mesh['y'=4,'zh'=2,'core'=2,'zf'=4,'zn'=2,'x'=4] {'core'}, dimensions={0}, use_global_device_ids=true | all-gather | bytes 983040 | tf_op jit(solution)/shard_map/all_gather | solution.py:73
  98.7 0.9 fusion
  99.6 0.4 copy.14
  100.0 0.1 copy.11
  100.1 23.2 %all_to_all.32 = bf16[8,4,20,8,128]{4,3,2,1,0:T(8,128)(2,1)S(1)} all-to-all(bf16[8,4,20,8,128]{4,3,2,1,0:T(8,128)(2,1)S(1)} %bitcast.36), channel_id=1, replica_groups=mesh['y'=4,'zh'=2,'core'=2,'zf'=4,'zn'=2,'x'=4] {'zn','x'}, dimensions={0} | all-to-all | bytes 2621440 | tf_op jit(solution)/shard_map/all_to_all | solution.py:80
  123.3 0.2 reduce_sum.34
  123.5 16.1 %all_to_all.33 = bf16[4,20,8,128]{3,2,1,0:T(8,128)(2,1)S(1)} all-to-all(bf16[4,20,8,128]{3,2,1,0:T(8,128)(2,1)S(1)} %reduce_sum.34), channel_id=1, replica_groups=mesh['y'=4,'zh'=2,'core'=2,'zf'=4,'zn'=2,'x'=4] {'zf'}, dimensions={0} | all-to-all | bytes 327680 | tf_op jit(solution)/shard_map/all_to_all | solution.py:82
  139.6 0.6 copy.15
  (13 shorter events, 0.2 us)
Async XLA Ops:
  0.6 47.6 %copy-start = (bf16[1024,512]{1,0:T(8,128)(2,1)S(1)}, bf16[1024,512]{1,0:T(8,128)(2,1)}, u32[]{:S(2)}) copy-start(bf16[1024,512]{1,0:T(8,128)(2,1)} %param.5) | copy-start | bytes 3145732
  27.1 5.4 %copy-start.1 = (f32[40,512]{1,0:T(8,128)S(1)}, f32[40,512]{1,0:T(8,128)}, u32[]{:S(2)}) copy-start(f32[40,512]{1,0:T(8,128)} %param.6) | copy-start | bytes 245764
  27.1 21.0 %all-to-all-start.1 = ((bf16[8,4,20,8,128]{4,3,2,1,0:T(8,128)(2,1)}), bf16[8,4,20,8,128]{4,3,2,1,0:T(8,128)(2,1)S(1)}, u32[]{:S(2)}, u32[]{:S(2)}) async-start(bf16[8,4,20,8,128]{4,3,2,1,0:T(8,128)(2,1)} %broadcast_in_dim.10), calls=%async_computation.1 | async-start | bytes 2621440 | tf_op jit(solution)/shard_map/all_to_all | solution.py:31
  32.6 23.5 %collective-permute-start = (bf16[40,512]{1,0:T(8,128)(2,1)S(1)}, bf16[40,512]{1,0:T(8,128)(2,1)S(1)}, u32[]{:S(2)}, u32[]{:S(2)}) collective-permute-start(bf16[40,512]{1,0:T(8,128)(2,1)S(1)} %convert_element_type.63), channel_id=1, source_target_pairs={{0,64},{64,0},{1,65},{65,1},{2,66},{66,2},{3,67},{67,3},{4,68},{68... | collective-permute-start | bytes 122888 | tf_op jit(solution)/shard_map/ppermute | solution.py:35
  49.2 11.3 %copy-start.2 = (f32[40,512]{1,0:T(8,128)S(1)}, f32[40,512]{1,0:T(8,128)}, u32[]{:S(2)}) copy-start(f32[40,512]{1,0:T(8,128)} %param.7) | copy-start | bytes 245764
  56.0 11.5 %all-to-all-start.2 = ((bf16[4,80,512]{2,1,0:T(8,128)(2,1)}), bf16[4,80,512]{2,1,0:T(8,128)(2,1)S(1)}, u32[]{:S(2)}, u32[]{:S(2)}) async-start(bf16[4,80,512]{2,1,0:T(8,128)(2,1)} %bitcast.4), calls=%async_computation.2 | async-start | bytes 655360 | tf_op jit(solution)/shard_map/all_to_all | solution.py:61
  60.5 22.9 %collective-permute-start.1 = (bf16[40,512]{1,0:T(8,128)(2,1)S(1)}, bf16[40,512]{1,0:T(8,128)(2,1)S(1)}, u32[]{:S(2)}, u32[]{:S(2)}) collective-permute-start(bf16[40,512]{1,0:T(8,128)(2,1)S(1)} %convert_element_type.71), channel_id=1, source_target_pairs={{0,64},{64,0},{1,65},{65,1},{2,66},{66,2},{3,67},{67,3},{4,68},{68... | collective-permute-start | bytes 122888 | tf_op jit(solution)/shard_map/ppermute | solution.py:35

commit v10 on v8

--- a/solution.py
+++ b/solution.py
@@ -42,22 +42,19 @@
 
 
 def shards(grad, basis, first_moment, second_moment):
-    zh, core = lax.axis_index("zh"), lax.axis_index("core")
+    zh = lax.axis_index("zh")
     rows, cols = grad.shape
-    moments = swap(jnp.stack([first_moment, second_moment]).astype(BF16), "zh")
     block = grad.reshape(rows, cols // LANES, LANES)
     block = spread(block, "zf", 4)
     block = spread(block, ("zn", "x"), 8)
     block = block.reshape(2, 2, 2, 4, rows, cols // LANES, LANES)
-    picked = block.transpose(1, 3, 0, 2, 4, 5, 6).reshape(32 * rows, cols)
+    picked = block.transpose(3, 1, 0, 2, 4, 5, 6).reshape(32 * rows, cols)
 
-    partial = jnp.dot(picked, basis, preferred_element_type=F32)
-    away = lax.dynamic_slice_in_dim(partial, 320 * (1 - core), 320).astype(BF16)
-    kept = lax.dynamic_slice_in_dim(partial, 320 * core, 320)
-    chip = (kept + swap_gathered(away, "core").astype(F32)).astype(BF16)
-    chip, moments = lax.optimization_barrier((chip, moments))
-    first_other, second_other = moments.astype(F32)
-    parts = lax.all_to_all(chip.reshape(4, 80, -1), "y", 0, 0, tiled=True)
+    partial = jnp.dot(picked, basis, preferred_element_type=F32).astype(BF16)
+    partial, *sent = lax.optimization_barrier((partial, first_moment, second_moment))
+    moments = swap(jnp.stack(sent).astype(BF16), "zh")
+    first_other, second_other = moments[0].astype(F32), moments[1].astype(F32)
+    parts = lax.all_to_all(partial.reshape(8, 80, -1), ("y", "core"), 0, 0, tiled=True)
     part = jnp.sum(parts.astype(F32), axis=0)
     rotated = part + swap_gathered(part.astype(BF16), "zh").astype(F32)
     low, high = rotated[:40], rotated[40:]

time: 142 us -> 139 us (0.979)
  blocking collectives: 94.8 us -> 115 us
  waiting for transfers between devices: 20.6 us -> 1.91 us
  starting transfers between devices: 18.5 us -> 14.4 us
    all_to_all x2 -> x3, blocking collectives: 33.7 us -> 54 us  [spread(): lax.all_to_all(jnp.broadcast_to(block[None], (n,) + block.shape), axes, 0...]
    all_to_all x2 -> x1, waiting for transfers between devices: 17.5 us -> 1.91 us  [shards(): lax.all_to_all(partial.reshape(8, 80, -1), ('y', 'core'), 0, 0, tiled=True)]
    all_to_all x2 -> x1, starting transfers between devices: 9.9 us -> 4.6 us  [shards(): lax.all_to_all(partial.reshape(8, 80, -1), ('y', 'core'), 0, 0, tiled=True)]
    all_gather x2 -> x1, blocking collectives: 18.6 us -> 13.9 us  [swap_gathered(): lax.all_gather(value, axis)]
    all_to_all x1, blocking collectives: 21.5 us -> 25.3 us  [shards(): total = lax.all_to_all(total, ('zn', 'x'), 0, 0, tiled=True)]
    ppermute x1, waiting for transfers between devices: 3.16 us -> 0.01 us  [swap(): return lax.ppermute(value, axis, [(0, 1), (1, 0)])]
  transfers between devices with their start and end apart: 3 -> 2, of which waited for: 3 -> 1; matrix products, arithmetic and copies ran while one was open for 1% -> 0% of each run, Pallas kernels for 0% -> 0%
where the time goes in v10:
time: 139 us; the launch traced here: 138 us
  blocking collectives  115 us (83%)
  starting transfers between devices  14.4 us (10%)
  matrix products  2.55 us (2%)
  local copies, waits for them, and re-layouts  2.41 us (2%)
  waiting for transfers between devices  1.91 us (1%)
    all_to_all x3, blocking collectives, spread(): lax.all_to_all(jnp.broadcast_to(block[None], (n,) + block.shape), axes, 0...  54 us
    all_to_all x1, blocking collectives, shards(): total = lax.all_to_all(total, ('zn', 'x'), 0, 0, tiled=True)  25.3 us
    all_to_all x1, blocking collectives, shards(): total = lax.all_to_all(total, 'zf', 0, 0, tiled=True)  19.8 us
    all_gather x1, blocking collectives, swap_gathered(): lax.all_gather(value, axis)  13.9 us
    ppermute x1, starting transfers between devices, swap(): return lax.ppermute(value, axis, [(0, 1), (1, 0)])  9.78 us
    all_to_all x1, starting transfers between devices, shards(): lax.all_to_all(partial.reshape(8, 80, -1), ('y', 'core'), 0, 0, tiled=True)  4.6 us
  transfers between devices with their start and end apart: 2, of which 1 were waited for; matrix products, arithmetic and copies ran while one was open for 0% of the time, Pallas kernels for 0%

profile of v10, /device:TPU:2, one launch (start us, length us, event | category | flops | bytes accessed | tf_op | source)
XLA Modules:
  0.0 138.5 jit_solution(4615288624912214919)
XLA Ops:
  0.6 0.0 copy-start
  0.6 0.9 copy.12
  1.6 24.2 %all_to_all.30 = bf16[4,20,8,128]{3,2,1,0:T(8,128)(2,1)S(1)} all-to-all(bf16[4,20,8,128]{3,2,1,0:T(8,128)(2,1)S(1)} %broadcast_in_dim.9), channel_id=1, replica_groups=mesh['y'=4,'zh'=2,'core'=2,'zf'=4,'zn'=2,'x'=4] {'zf'}, dimensions={0} | all-to-all | bytes 327680 | tf_op jit(solution)/shard_map/all_to_all | solution.py:31
  25.8 0.2 broadcast_in_dim.10
  26.0 19.7 %all_to_all.31 = bf16[8,4,20,8,128]{4,3,2,1,0:T(8,128)(2,1)S(1)} all-to-all(bf16[8,4,20,8,128]{4,3,2,1,0:T(8,128)(2,1)S(1)} %broadcast_in_dim.10), channel_id=1, replica_groups=mesh['y'=4,'zh'=2,'core'=2,'zf'=4,'zn'=2,'x'=4] {'zn','x'}, dimensions={0} | all-to-all | bytes 2621440 | tf_op jit(solution)/shard_map/all_to_all | solution.py:31
  45.7 0.1 copy.10
  45.9 0.0 copy-done
  45.9 1.7 %convolution_convert_fusion.1 = bf16[640,512]{1,0:T(8,128)(2,1)} fusion(bf16[1024,512]{1,0:T(8,128)(2,1)S(1)} %copy-done, bf16[80,8,8,128]{3,2,1,0:T(8,128)(2,1)S(1)} %bitcast.51), kind=kOutput, calls=%fused_computation.2 | convolution fusion | flops 671416320 | bytes 3014656 | tf_op jit(solution)/shard_map/dot_general | solution.py:53
  47.5 0.0 copy-start.1
  47.5 0.0 copy-start.2
  47.5 4.6 %all-to-all-start.2 = ((bf16[8,80,512]{2,1,0:T(8,128)(2,1)}), bf16[8,80,512]{2,1,0:T(8,128)(2,1)S(1)}, u32[]{:S(2)}, u32[]{:S(2)}) async-start(bf16[8,80,512]{2,1,0:T(8,128)(2,1)} %bitcast.2), calls=%async_computation.2 | async-start | bytes 1310720 | tf_op jit(solution)/shard_map/all_to_all | solution.py:57
  52.2 0.0 copy-done.1
  52.2 0.0 copy-done.2
  52.2 9.8 %collective-permute-start = (bf16[2,40,512]{2,1,0:T(8,128)(2,1)S(1)}, bf16[2,40,512]{2,1,0:T(8,128)(2,1)S(1)}, u32[]{:S(2)}, u32[]{:S(2)}) collective-permute-start(bf16[2,40,512]{2,1,0:T(8,128)(2,1)S(1)} %pad_maximum_fusion), channel_id=1, source_target_pairs={{0,64},{64,0},{1,65},{65,1},{2,66},{66,2},{3,67},{67,3},{4,68},{68... | collective-permute-start | bytes 245768 | tf_op jit(solution)/shard_map/ppermute | solution.py:35
  62.0 1.9 %all-to-all-done.2 = bf16[8,80,512]{2,1,0:T(8,128)(2,1)S(1)} async-done(((bf16[8,80,512]{2,1,0:T(8,128)(2,1)}), bf16[8,80,512]{2,1,0:T(8,128)(2,1)S(1)}, u32[]{:S(2)}, u32[]{:S(2)}) %all-to-all-start.2) | async-done | bytes 655392 | tf_op jit(solution)/shard_map/all_to_all | solution.py:57
  63.9 0.1 convert_reduce_fusion
  64.0 13.9 %all-gather = bf16[160,512]{1,0:T(8,128)(2,1)S(1)} all-gather(bf16[80,512]{1,0:T(8,128)(2,1)S(1)} %convert_element_type.49), channel_id=2, replica_groups=mesh['y'=4,'zh'=2,'core'=2,'zf'=4,'zn'=2,'x'=4] {'zh'}, dimensions={0}, use_global_device_ids=true | all-gather | bytes 245760 | tf_op jit(solution)/shard_map/all_gather | solution.py:40
  77.9 0.0 collective-permute-done
  77.9 0.8 broadcast_select_fusion.1
  78.7 10.0 %all_to_all.32 = bf16[4,80,512]{2,1,0:T(8,128)(2,1)S(1)} all-to-all(bf16[4,80,512]{2,1,0:T(8,128)(2,1)S(1)} %broadcast_in_dim.22), channel_id=1, replica_groups=mesh['y'=4,'zh'=2,'core'=2,'zf'=4,'zn'=2,'x'=4] {'y'}, dimensions={0} | all-to-all | bytes 655360 | tf_op jit(solution)/shard_map/all_to_all | solution.py:31
  88.8 2.3 %all_gather.8 = bf16[640,512]{1,0:T(8,128)(2,1)S(1)} all-gather(bf16[320,512]{1,0:T(8,128)(2,1)S(1)} %bitcast.52), channel_id=1, replica_groups=mesh['y'=4,'zh'=2,'core'=2,'zf'=4,'zn'=2,'x'=4] {'core'}, dimensions={0}, use_global_device_ids=true | all-gather | bytes 983040 | tf_op jit(solution)/shard_map/all_gather | solution.py:69
  91.0 0.9 fusion
  91.9 0.4 copy.14
  92.3 0.1 copy.11
  92.4 25.3 %all_to_all.33 = bf16[8,4,20,8,128]{4,3,2,1,0:T(8,128)(2,1)S(1)} all-to-all(bf16[8,4,20,8,128]{4,3,2,1,0:T(8,128)(2,1)S(1)} %bitcast.50), channel_id=1, replica_groups=mesh['y'=4,'zh'=2,'core'=2,'zf'=4,'zn'=2,'x'=4] {'zn','x'}, dimensions={0} | all-to-all | bytes 2621440 | tf_op jit(solution)/shard_map/all_to_all | solution.py:76
  117.8 0.2 reduce_sum.34
  118.0 19.8 %all_to_all.34 = bf16[4,20,8,128]{3,2,1,0:T(8,128)(2,1)S(1)} all-to-all(bf16[4,20,8,128]{3,2,1,0:T(8,128)(2,1)S(1)} %reduce_sum.34), channel_id=1, replica_groups=mesh['y'=4,'zh'=2,'core'=2,'zf'=4,'zn'=2,'x'=4] {'zf'}, dimensions={0} | all-to-all | bytes 327680 | tf_op jit(solution)/shard_map/all_to_all | solution.py:78
  137.8 0.6 copy.15
  (11 shorter events, 0.2 us)
Async XLA Ops:
  0.6 45.2 %copy-start = (bf16[1024,512]{1,0:T(8,128)(2,1)S(1)}, bf16[1024,512]{1,0:T(8,128)(2,1)}, u32[]{:S(2)}) copy-start(bf16[1024,512]{1,0:T(8,128)(2,1)} %param.5) | copy-start | bytes 3145732
  47.5 4.6 %copy-start.1 = (f32[40,512]{1,0:T(8,128)S(1)}, f32[40,512]{1,0:T(8,128)}, u32[]{:S(2)}) copy-start(f32[40,512]{1,0:T(8,128)} %param.6) | copy-start | bytes 245764
  47.5 4.6 %copy-start.2 = (f32[40,512]{1,0:T(8,128)S(1)}, f32[40,512]{1,0:T(8,128)}, u32[]{:S(2)}) copy-start(f32[40,512]{1,0:T(8,128)} %param.7) | copy-start | bytes 245764
  47.5 16.4 %all-to-all-start.2 = ((bf16[8,80,512]{2,1,0:T(8,128)(2,1)}), bf16[8,80,512]{2,1,0:T(8,128)(2,1)S(1)}, u32[]{:S(2)}, u32[]{:S(2)}) async-start(bf16[8,80,512]{2,1,0:T(8,128)(2,1)} %bitcast.2), calls=%async_computation.2 | async-start | bytes 1310720 | tf_op jit(solution)/shard_map/all_to_all | solution.py:57
  52.2 25.7 %collective-permute-start = (bf16[2,40,512]{2,1,0:T(8,128)(2,1)S(1)}, bf16[2,40,512]{2,1,0:T(8,128)(2,1)S(1)}, u32[]{:S(2)}, u32[]{:S(2)}) collective-permute-start(bf16[2,40,512]{2,1,0:T(8,128)(2,1)S(1)} %pad_maximum_fusion), channel_id=1, source_target_pairs={{0,64},{64,0},{1,65},{65,1},{2,66},{66,2},{3,67},{67,3},{4,68},{68... | collective-permute-start | bytes 245768 | tf_op jit(solution)/shard_map/ppermute | solution.py:35

commit v11 on v7

--- a/solution.py
+++ b/solution.py
@@ -35,30 +35,29 @@
     return lax.ppermute(value, axis, [(0, 1), (1, 0)])
 
 
-def swap_cores(value, core):
-    return lax.dynamic_index_in_dim(lax.all_gather(value, "core"), 1 - core, keepdims=False)
+def swap_gathered(value, axis):
+    return lax.dynamic_index_in_dim(
+        lax.all_gather(value, axis), 1 - lax.axis_index(axis), keepdims=False
+    )
 
 
 def shards(grad, basis, first_moment, second_moment):
-    zh, core, x0 = lax.axis_index("zh"), lax.axis_index("core"), lax.axis_index("x0")
+    zh, x0 = lax.axis_index("zh"), lax.axis_index("x0")
     rows, cols = grad.shape
-    moments = jnp.stack([first_moment, second_moment]).astype(BF16)
     block = grad.reshape(rows, cols // LANES, LANES)
     block = spread(block, "zf", 4)
     block = spread(block, ("zn", "x1", "x0"), 8)
     block = block.reshape(2, 2, 2, 4, rows, cols // LANES, LANES)
-    picked = block.transpose(1, 3, 0, 2, 4, 5, 6).reshape(32 * rows, cols)
+    picked = block.transpose(3, 1, 0, 2, 4, 5, 6).reshape(32 * rows, cols)
 
-    partial = jnp.dot(picked, basis, preferred_element_type=F32)
-    away = lax.dynamic_slice_in_dim(partial, 320 * (1 - core), 320).astype(BF16)
-    kept = lax.dynamic_slice_in_dim(partial, 320 * core, 320)
-    chip = (kept + swap_cores(away, core).astype(F32)).astype(BF16)
-    chip, moments, basis_sent = lax.optimization_barrier((chip, moments, basis))
-    basis_next = swap(basis_sent, "x0")
-    first_other, second_other = swap(moments, "zh").astype(F32)
-    parts = lax.all_to_all(chip.reshape(4, 80, -1), "y", 0, 0, tiled=True)
+    partial = jnp.dot(picked, basis, preferred_element_type=F32).astype(BF16)
+    partial, *sent = lax.optimization_barrier((partial, first_moment, second_moment))
+    basis_next = swap(basis, "x0")
+    moments = swap(jnp.stack(sent).astype(BF16), "zh")
+    first_other, second_other = moments[0].astype(F32), moments[1].astype(F32)
+    parts = lax.all_to_all(partial.reshape(8, 80, -1), ("y", "core"), 0, 0, tiled=True)
     part = jnp.sum(parts.astype(F32), axis=0)
-    rotated = part + swap(part.astype(BF16), "zh").astype(F32)
+    rotated = part + swap_gathered(part.astype(BF16), "zh").astype(F32)
     low, high = rotated[:40], rotated[40:]
     first = zh == 0
     mine, other = jnp.where(first, low, high), jnp.where(first, high, low)

time: 142 us -> 135 us (0.951)
  blocking collectives: 62.5 us -> 93.5 us
  waiting for transfers between devices: 32.7 us -> 6.48 us
  starting transfers between devices: 36.3 us -> 25.8 us
    all_to_all x1 -> x2, blocking collectives: 24.2 us -> 43.9 us  [spread(): lax.all_to_all(jnp.broadcast_to(block[None], (n,) + block.shape), axes, 0...]
    all_to_all x2 -> x1, waiting for transfers between devices: 14.3 us -> 0.01 us  [shards(): lax.all_to_all(partial.reshape(8, 80, -1), ('y', 'core'), 0, 0, tiled=True)]
    all_gather x1, blocking collectives: 2.28 us -> 14.3 us  [swap_gathered(): lax.all_gather(value, axis)]
    ppermute x3 -> x2, starting transfers between devices: 20.5 us -> 13.5 us  [swap(): return lax.ppermute(value, axis, [(0, 1), (1, 0)])]
    ppermute x3 -> x2, waiting for transfers between devices: 6.78 us -> 0.01 us  [swap(): return lax.ppermute(value, axis, [(0, 1), (1, 0)])]
    all_to_all x2 -> x1, starting transfers between devices: 9.89 us -> 4.61 us  [shards(): lax.all_to_all(partial.reshape(8, 80, -1), ('y', 'core'), 0, 0, tiled=True)]
    all_to_all x1, waiting for transfers between devices: 11.6 us -> 6.47 us  [shards(): lax.all_to_all(pair, ('y', 'x0'), 0, 0, tiled=True)]
    all_to_all x1, starting transfers between devices: 5.88 us -> 7.68 us  [shards(): lax.all_to_all(pair, ('y', 'x0'), 0, 0, tiled=True)]
  transfers between devices with their start and end apart: 6 -> 4, of which waited for: 3 -> 1; matrix products, arithmetic and copies ran while one was open for 2% -> 2% of each run, Pallas kernels for 0% -> 0%
where the time goes in v11:
time: 135 us; the launch traced here: 134 us
  blocking collectives  93.5 us (69%)
  starting transfers between devices  25.8 us (19%)
  waiting for transfers between devices  6.48 us (5%)
  local copies, waits for them, and re-layouts  4.01 us (3%)
  matrix products  2.75 us (2%)
    all_to_all x2, blocking collectives, spread(): lax.all_to_all(jnp.broadcast_to(block[None], (n,) + block.shape), axes, 0...  43.9 us
    all_to_all x1, blocking collectives, shards(): total = lax.all_to_all(total, 'zf', 0, 0, tiled=True)  18.6 us
    all_to_all x1, blocking collectives, shards(): total = lax.all_to_all(total, ('zn', 'x1'), 0, 0, tiled=True)  14.4 us
    all_gather x1, blocking collectives, swap_gathered(): lax.all_gather(value, axis)  14.3 us
    ppermute x2, starting transfers between devices, swap(): return lax.ppermute(value, axis, [(0, 1), (1, 0)])  13.5 us
    all_to_all x1, starting transfers between devices, shards(): lax.all_to_all(pair, ('y', 'x0'), 0, 0, tiled=True)  7.68 us
    all_to_all x1, waiting for transfers between devices, shards(): lax.all_to_all(pair, ('y', 'x0'), 0, 0, tiled=True)  6.47 us
    all_to_all x1, starting transfers between devices, shards(): lax.all_to_all(partial.reshape(8, 80, -1), ('y', 'core'), 0, 0, tiled=True)  4.61 us
  transfers between devices with their start and end apart: 4, of which 1 were waited for; matrix products, arithmetic and copies ran while one was open for 2% of the time, Pallas kernels for 0%

profile of v11, /device:TPU:2, one launch (start us, length us, event | category | flops | bytes accessed | tf_op | source)
XLA Modules:
  0.0 134.4 jit_solution(7102061266559935467)
XLA Ops:
  0.6 0.8 copy.20
  1.5 24.2 %all_to_all.30 = bf16[4,20,8,128]{3,2,1,0:T(8,128)(2,1)S(1)} all-to-all(bf16[4,20,8,128]{3,2,1,0:T(8,128)(2,1)S(1)} %broadcast_in_dim.21), channel_id=1, replica_groups=mesh['y'=4,'zh'=2,'core'=2,'zf'=4,'zn'=2,'x1'=2,'x0'=2] {'zf'}, dimensions={0} | all-to-all | bytes 327680 | tf_op jit(solution)/shard_map/all_to_all | solution.py:31
  25.7 0.2 broadcast_in_dim.22
  25.9 19.7 %all_to_all.31 = bf16[8,4,20,8,128]{4,3,2,1,0:T(8,128)(2,1)S(1)} all-to-all(bf16[8,4,20,8,128]{4,3,2,1,0:T(8,128)(2,1)S(1)} %broadcast_in_dim.22), channel_id=1, replica_groups=mesh['y'=4,'zh'=2,'core'=2,'zf'=4,'zn'=2,'x1'=2,'x0'=2] {'zn','x1','x0'}, dimensions={0} | all-to-all | bytes 2621440 | tf_op jit(solution)/shard_map/all_to_all | solution.py:31
  45.6 0.1 copy.15
  45.8 1.1 copy-done
  46.8 1.7 %convolution_convert_fusion = bf16[640,512]{1,0:T(8,128)(2,1)} fusion(bf16[1024,512]{1,0:T(8,128)(2,1)S(1)} %copy-done, bf16[80,8,8,128]{3,2,1,0:T(8,128)(2,1)S(1)} %bitcast.62), kind=kOutput, calls=%fused_computation.2 | convolution fusion | flops 671416320 | bytes 3014656 | tf_op jit(solution)/shard_map/dot_general | solution.py:53
  48.5 4.6 %all-to-all-start.2 = ((bf16[8,80,512]{2,1,0:T(8,128)(2,1)}), bf16[8,80,512]{2,1,0:T(8,128)(2,1)S(1)}, u32[]{:S(2)}, u32[]{:S(2)}) async-start(bf16[8,80,512]{2,1,0:T(8,128)(2,1)} %bitcast.2), calls=%async_computation.2 | async-start | bytes 1310720 | tf_op jit(solution)/shard_map/all_to_all | solution.py:58
  53.1 3.7 %collective-permute-start.1 = (bf16[1024,512]{1,0:T(8,128)(2,1)S(1)}, bf16[1024,512]{1,0:T(8,128)(2,1)S(1)}, u32[]{:S(2)}, u32[]{:S(2)}) collective-permute-start(bf16[1024,512]{1,0:T(8,128)(2,1)S(1)} %copy-done), channel_id=1, source_target_pairs={{0,1},{1,0},{2,3},{3,2},{4,5},{5,4},{6,7},{7,6},{8,9},{9,8},{10,11... | collective-permute-start | bytes 3145736 | tf_op jit(solution)/shard_map/ppermute | solution.py:35
  56.9 0.0 copy-done.1
  56.9 0.0 copy-done.2
  56.9 9.8 %collective-permute-start = (bf16[2,40,512]{2,1,0:T(8,128)(2,1)S(1)}, bf16[2,40,512]{2,1,0:T(8,128)(2,1)S(1)}, u32[]{:S(2)}, u32[]{:S(2)}) collective-permute-start(bf16[2,40,512]{2,1,0:T(8,128)(2,1)S(1)} %pad_maximum_fusion), channel_id=1, source_target_pairs={{0,64},{64,0},{1,65},{65,1},{2,66},{66,2},{3,67},{67,3},{4,68},{68... | collective-permute-start | bytes 245768 | tf_op jit(solution)/shard_map/ppermute | solution.py:35
  66.7 0.0 all-to-all-done.2
  66.7 0.1 convert_reduce_fusion
  66.8 14.3 %all-gather = bf16[160,512]{1,0:T(8,128)(2,1)S(1)} all-gather(bf16[80,512]{1,0:T(8,128)(2,1)S(1)} %convert_element_type.49), channel_id=2, replica_groups=mesh['y'=4,'zh'=2,'core'=2,'zf'=4,'zn'=2,'x1'=2,'x0'=2] {'zh'}, dimensions={0}, use_global_device_ids=true | all-gather | bytes 245760 | tf_op jit(solution)/shard_map/all_gather | solution.py:40
  81.1 0.0 collective-permute-done
  81.1 0.8 broadcast_select_fusion.1
  81.9 0.1 copy.16
  82.0 0.7 broadcast_in_dim.24
  82.8 7.7 %all-to-all-start.3 = ((bf16[8,40,512]{2,1,0:T(8,128)(2,1)}), bf16[8,40,512]{2,1,0:T(8,128)(2,1)S(1)}, u32[]{:S(2)}, u32[]{:S(2)}) async-start(bf16[8,40,512]{2,1,0:T(8,128)(2,1)} %bitcast.11), calls=%async_computation.3 | async-start | bytes 655360 | tf_op jit(solution)/shard_map/all_to_all | solution.py:71
  90.5 6.5 %all-to-all-done.3 = bf16[8,40,512]{2,1,0:T(8,128)(2,1)S(1)} async-done(((bf16[8,40,512]{2,1,0:T(8,128)(2,1)}), bf16[8,40,512]{2,1,0:T(8,128)(2,1)S(1)}, u32[]{:S(2)}, u32[]{:S(2)}) %all-to-all-start.3) | async-done | bytes 327712 | tf_op jit(solution)/shard_map/all_to_all | solution.py:71
  96.9 2.3 %all-gather.1 = bf16[4,4,40,512]{3,2,0,1:T(8,128)(2,1)S(1)} all-gather(bf16[2,4,40,512]{3,2,0,1:T(8,128)(2,1)S(1)} %bitcast.64), channel_id=3, replica_groups=mesh['y'=4,'zh'=2,'core'=2,'zf'=4,'zn'=2,'x1'=2,'x0'=2] {'core'}, dimensions={0}, use_global_device_ids=true | all-gather | bytes 983040 | tf_op jit(solution)/shard_map/all_gather | solution.py:72
  99.2 0.1 copy.18
  99.3 0.1 constant_dynamic-slice_fusion
  99.3 0.5 fusion.14
  99.9 0.0 collective-permute-done.1
  99.9 0.5 fusion.3
  100.4 0.1 copy.22
  100.6 14.4 %all_to_all.32 = bf16[4,4,20,8,128]{4,3,2,1,0:T(8,128)(2,1)S(1)} all-to-all(bf16[4,4,20,8,128]{4,3,2,1,0:T(8,128)(2,1)S(1)} %bitcast.61), channel_id=1, replica_groups=mesh['y'=4,'zh'=2,'core'=2,'zf'=4,'zn'=2,'x1'=2,'x0'=2] {'zn','x1'}, dimensions={0} | all-to-all | bytes 1310720 | tf_op jit(solution)/shard_map/all_to_all | solution.py:82
  115.0 0.1 reduce_sum.34
  115.1 18.6 %all_to_all.33 = bf16[4,20,8,128]{3,2,1,0:T(8,128)(2,1)S(1)} all-to-all(bf16[4,20,8,128]{3,2,1,0:T(8,128)(2,1)S(1)} %reduce_sum.34), channel_id=1, replica_groups=mesh['y'=4,'zh'=2,'core'=2,'zf'=4,'zn'=2,'x1'=2,'x0'=2] {'zf'}, dimensions={0} | all-to-all | bytes 327680 | tf_op jit(solution)/shard_map/all_to_all | solution.py:84
  133.8 0.6 copy.23
  (16 shorter events, 0.2 us)
Async XLA Ops:
  45.6 1.2 copy-start
  48.5 8.3 %copy-start.1 = (f32[40,512]{1,0:T(8,128)S(1)}, f32[40,512]{1,0:T(8,128)}, u32[]{:S(2)}) copy-start(f32[40,512]{1,0:T(8,128)} %param.6) | copy-start | bytes 245764
  48.5 8.3 %copy-start.2 = (f32[40,512]{1,0:T(8,128)S(1)}, f32[40,512]{1,0:T(8,128)}, u32[]{:S(2)}) copy-start(f32[40,512]{1,0:T(8,128)} %param.7) | copy-start | bytes 245764
  48.5 18.2 %all-to-all-start.2 = ((bf16[8,80,512]{2,1,0:T(8,128)(2,1)}), bf16[8,80,512]{2,1,0:T(8,128)(2,1)S(1)}, u32[]{:S(2)}, u32[]{:S(2)}) async-start(bf16[8,80,512]{2,1,0:T(8,128)(2,1)} %bitcast.2), calls=%async_computation.2 | async-start | bytes 1310720 | tf_op jit(solution)/shard_map/all_to_all | solution.py:58
  53.1 46.7 %collective-permute-start.1 = (bf16[1024,512]{1,0:T(8,128)(2,1)S(1)}, bf16[1024,512]{1,0:T(8,128)(2,1)S(1)}, u32[]{:S(2)}, u32[]{:S(2)}) collective-permute-start(bf16[1024,512]{1,0:T(8,128)(2,1)S(1)} %copy-done), channel_id=1, source_target_pairs={{0,1},{1,0},{2,3},{3,2},{4,5},{5,4},{6,7},{7,6},{8,9},{9,8},{10,11... | collective-permute-start | bytes 3145736 | tf_op jit(solution)/shard_map/ppermute | solution.py:35
  56.9 24.2 %collective-permute-start = (bf16[2,40,512]{2,1,0:T(8,128)(2,1)S(1)}, bf16[2,40,512]{2,1,0:T(8,128)(2,1)S(1)}, u32[]{:S(2)}, u32[]{:S(2)}) collective-permute-start(bf16[2,40,512]{2,1,0:T(8,128)(2,1)S(1)} %pad_maximum_fusion), channel_id=1, source_target_pairs={{0,64},{64,0},{1,65},{65,1},{2,66},{66,2},{3,67},{67,3},{4,68},{68... | collective-permute-start | bytes 245768 | tf_op jit(solution)/shard_map/ppermute | solution.py:35
  82.8 14.2 %all-to-all-start.3 = ((bf16[8,40,512]{2,1,0:T(8,128)(2,1)}), bf16[8,40,512]{2,1,0:T(8,128)(2,1)S(1)}, u32[]{:S(2)}, u32[]{:S(2)}) async-start(bf16[8,40,512]{2,1,0:T(8,128)(2,1)} %bitcast.11), calls=%async_computation.3 | async-start | bytes 655360 | tf_op jit(solution)/shard_map/all_to_all | solution.py:71

commit v12 on v11

--- a/solution.py
+++ b/solution.py
@@ -67,11 +67,11 @@
         [jnp.where(first, share, share_other), jnp.where(first, share_other, share)], axis=0
     )
     pair = pair.reshape(2, 2, rows, -1).transpose(1, 0, 2, 3).reshape(2, 2 * rows, -1)
-    pair = jnp.broadcast_to(pair[None], (4,) + pair.shape).reshape(8, 2 * rows, -1)
-    pair = lax.all_to_all(pair, ("y", "x0"), 0, 0, tiled=True).reshape(4, 2, 2 * rows, -1)
-    direction = lax.all_gather(pair.transpose(1, 0, 2, 3), "core").reshape(2, 2, 8 * rows, -1)
-    own = lax.dynamic_index_in_dim(direction, x0, 1, keepdims=False).reshape(16 * rows, -1)
-    away = lax.dynamic_index_in_dim(direction, 1 - x0, 1, keepdims=False).reshape(16 * rows, -1)
+    kept = lax.dynamic_index_in_dim(pair, x0, 0, keepdims=False)
+    lent = lax.dynamic_index_in_dim(pair, 1 - x0, 0, keepdims=False)
+    pair = spread(jnp.stack([kept, swap_gathered(lent, "x0")]), "y", 4)
+    direction = lax.all_gather(pair.transpose(1, 0, 2, 3), "core")
+    own, away = direction[:, 0].reshape(16 * rows, -1), direction[:, 1].reshape(16 * rows, -1)
 
     total = sum(
         lax.dot_general(d, b, (((1,), (1,)), ((), ())), preferred_element_type=F32)

time: 135 us -> 138 us (1.022)
  blocking collectives: 93.5 us -> 111 us
  starting transfers between devices: 25.8 us -> 18.1 us
  waiting for transfers between devices: 6.48 us -> 0.01 us
    all_to_all x2 -> x3, blocking collectives: 43.9 us -> 57 us  [spread(): lax.all_to_all(jnp.broadcast_to(block[None], (n,) + block.shape), axes, 0...]
    all_to_all x1 -> x0, starting transfers between devices: 7.68 us -> none  [shards(): lax.all_to_all(pair, ('y', 'x0'), 0, 0, tiled=True)]
    all_to_all x1 -> x0, waiting for transfers between devices: 6.47 us -> none  [shards(): lax.all_to_all(pair, ('y', 'x0'), 0, 0, tiled=True)]
    all_gather x1 -> x2, blocking collectives: 14.3 us -> 18.9 us  [swap_gathered(): lax.all_gather(value, axis)]
  transfers between devices with their start and end apart: 4 -> 3, of which waited for: 1 -> 0; matrix products, arithmetic and copies ran while one was open for 2% -> 2% of each run, Pallas kernels for 0% -> 0%
where the time goes in v12:
time: 138 us; the launch traced here: 137 us
  blocking collectives  111 us (80%)
  starting transfers between devices  18.1 us (13%)
  local copies, waits for them, and re-layouts  3.51 us (3%)
  matrix products  2.75 us (2%)
    all_to_all x3, blocking collectives, spread(): lax.all_to_all(jnp.broadcast_to(block[None], (n,) + block.shape), axes, 0...  57 us
    all_gather x2, blocking collectives, swap_gathered(): lax.all_gather(value, axis)  18.9 us
    all_to_all x1, blocking collectives, shards(): total = lax.all_to_all(total, 'zf', 0, 0, tiled=True)  18.4 us
    all_to_all x1, blocking collectives, shards(): total = lax.all_to_all(total, ('zn', 'x1'), 0, 0, tiled=True)  14.4 us
    ppermute x2, starting transfers between devices, swap(): return lax.ppermute(value, axis, [(0, 1), (1, 0)])  13.5 us
    all_to_all x1, starting transfers between devices, shards(): lax.all_to_all(partial.reshape(8, 80, -1), ('y', 'core'), 0, 0, tiled=True)  4.61 us
  transfers between devices with their start and end apart: 3, of which 0 were waited for; matrix products, arithmetic and copies ran while one was open for 2% of the time, Pallas kernels for 0%

profile of v12, /device:TPU:2, one launch (start us, length us, event | category | flops | bytes accessed | tf_op | source)
XLA Modules:
  0.0 137.5 jit_solution(3848925225031636138)
XLA Ops:
  0.6 0.8 copy.29
  1.5 24.2 %all_to_all.30 = bf16[4,20,8,128]{3,2,1,0:T(8,128)(2,1)S(1)} all-to-all(bf16[4,20,8,128]{3,2,1,0:T(8,128)(2,1)S(1)} %broadcast_in_dim.9), channel_id=1, replica_groups=mesh['y'=4,'zh'=2,'core'=2,'zf'=4,'zn'=2,'x1'=2,'x0'=2] {'zf'}, dimensions={0} | all-to-all | bytes 327680 | tf_op jit(solution)/shard_map/all_to_all | solution.py:31
  25.7 0.2 broadcast_in_dim.10
  25.9 19.7 %all_to_all.31 = bf16[8,4,20,8,128]{4,3,2,1,0:T(8,128)(2,1)S(1)} all-to-all(bf16[8,4,20,8,128]{4,3,2,1,0:T(8,128)(2,1)S(1)} %broadcast_in_dim.10), channel_id=1, replica_groups=mesh['y'=4,'zh'=2,'core'=2,'zf'=4,'zn'=2,'x1'=2,'x0'=2] {'zn','x1','x0'}, dimensions={0} | all-to-all | bytes 2621440 | tf_op jit(solution)/shard_map/all_to_all | solution.py:31
  45.6 0.1 copy.21
  45.8 1.1 copy-done
  46.8 1.7 %convolution_convert_fusion = bf16[640,512]{1,0:T(8,128)(2,1)} fusion(bf16[1024,512]{1,0:T(8,128)(2,1)S(1)} %copy-done, bf16[80,8,8,128]{3,2,1,0:T(8,128)(2,1)S(1)} %bitcast.60), kind=kOutput, calls=%fused_computation.2 | convolution fusion | flops 671416320 | bytes 3014656 | tf_op jit(solution)/shard_map/dot_general | solution.py:53
  48.5 4.6 %all-to-all-start.2 = ((bf16[8,80,512]{2,1,0:T(8,128)(2,1)}), bf16[8,80,512]{2,1,0:T(8,128)(2,1)S(1)}, u32[]{:S(2)}, u32[]{:S(2)}) async-start(bf16[8,80,512]{2,1,0:T(8,128)(2,1)} %bitcast.2), calls=%async_computation.2 | async-start | bytes 1310720 | tf_op jit(solution)/shard_map/all_to_all | solution.py:58
  53.1 3.7 %collective-permute-start.1 = (bf16[1024,512]{1,0:T(8,128)(2,1)S(1)}, bf16[1024,512]{1,0:T(8,128)(2,1)S(1)}, u32[]{:S(2)}, u32[]{:S(2)}) collective-permute-start(bf16[1024,512]{1,0:T(8,128)(2,1)S(1)} %copy-done), channel_id=1, source_target_pairs={{0,1},{1,0},{2,3},{3,2},{4,5},{5,4},{6,7},{7,6},{8,9},{9,8},{10,11... | collective-permute-start | bytes 3145736 | tf_op jit(solution)/shard_map/ppermute | solution.py:35
  56.9 0.0 copy-done.1
  56.9 0.0 copy-done.2
  56.9 9.8 %collective-permute-start = (bf16[2,40,512]{2,1,0:T(8,128)(2,1)S(1)}, bf16[2,40,512]{2,1,0:T(8,128)(2,1)S(1)}, u32[]{:S(2)}, u32[]{:S(2)}) collective-permute-start(bf16[2,40,512]{2,1,0:T(8,128)(2,1)S(1)} %pad_maximum_fusion), channel_id=1, source_target_pairs={{0,64},{64,0},{1,65},{65,1},{2,66},{66,2},{3,67},{67,3},{4,68},{68... | collective-permute-start | bytes 245768 | tf_op jit(solution)/shard_map/ppermute | solution.py:35
  66.7 0.0 all-to-all-done.2
  66.7 0.1 convert_reduce_fusion
  66.8 14.3 %all-gather = bf16[160,512]{1,0:T(8,128)(2,1)S(1)} all-gather(bf16[80,512]{1,0:T(8,128)(2,1)S(1)} %convert_element_type.49), channel_id=2, replica_groups=mesh['y'=4,'zh'=2,'core'=2,'zf'=4,'zn'=2,'x1'=2,'x0'=2] {'zh'}, dimensions={0}, use_global_device_ids=true | all-gather | bytes 245760 | tf_op jit(solution)/shard_map/all_gather | solution.py:40
  81.1 0.0 collective-permute-done
  81.1 0.8 broadcast_select_fusion.1
  81.9 0.1 copy.22
  82.0 0.2 constant_dynamic-slice_fusion.2
  82.2 4.7 %all_gather.15 = bf16[2,40,512]{2,1,0:T(8,128)(2,1)S(1)} all-gather(bf16[1,40,512]{2,1,0:T(8,128)(2,1)S(1)} %copy.23), channel_id=1, replica_groups=mesh['y'=4,'zh'=2,'core'=2,'zf'=4,'zn'=2,'x1'=2,'x0'=2] {'x0'}, dimensions={0}, use_global_device_ids=true | all-gather | bytes 122880 | tf_op jit(solution)/shard_map/all_gather | solution.py:40
  86.9 0.1 copy.28
  87.0 0.2 pad_maximum_fusion.2
  87.2 13.0 %all_to_all.32 = bf16[4,2,40,512]{3,2,1,0:T(8,128)(2,1)S(1)} all-to-all(bf16[4,2,40,512]{3,2,1,0:T(8,128)(2,1)S(1)} %broadcast_in_dim.22), channel_id=1, replica_groups=mesh['y'=4,'zh'=2,'core'=2,'zf'=4,'zn'=2,'x1'=2,'x0'=2] {'y'}, dimensions={0} | all-to-all | bytes 655360 | tf_op jit(solution)/shard_map/all_to_all | solution.py:31
  100.3 2.3 %all-gather.1 = bf16[4,4,40,512]{3,2,1,0:T(8,128)(2,1)S(1)} all-gather(bf16[2,4,40,512]{3,2,1,0:T(8,128)(2,1)S(1)} %copy.26), channel_id=3, replica_groups=mesh['y'=4,'zh'=2,'core'=2,'zf'=4,'zn'=2,'x1'=2,'x0'=2] {'core'}, dimensions={0}, use_global_device_ids=true | all-gather | bytes 983040 | tf_op jit(solution)/shard_map/all_gather | solution.py:73
  102.6 0.5 fusion.15
  103.2 0.0 collective-permute-done.1
  103.2 0.5 fusion.3
  103.7 0.1 copy.31
  103.9 14.4 %all_to_all.33 = bf16[4,4,20,8,128]{4,3,2,1,0:T(8,128)(2,1)S(1)} all-to-all(bf16[4,4,20,8,128]{4,3,2,1,0:T(8,128)(2,1)S(1)} %bitcast.58), channel_id=1, replica_groups=mesh['y'=4,'zh'=2,'core'=2,'zf'=4,'zn'=2,'x1'=2,'x0'=2] {'zn','x1'}, dimensions={0} | all-to-all | bytes 1310720 | tf_op jit(solution)/shard_map/all_to_all | solution.py:82
  118.3 0.1 reduce_sum.34
  118.5 18.4 %all_to_all.34 = bf16[4,20,8,128]{3,2,1,0:T(8,128)(2,1)S(1)} all-to-all(bf16[4,20,8,128]{3,2,1,0:T(8,128)(2,1)S(1)} %reduce_sum.34), channel_id=1, replica_groups=mesh['y'=4,'zh'=2,'core'=2,'zf'=4,'zn'=2,'x1'=2,'x0'=2] {'zf'}, dimensions={0} | all-to-all | bytes 327680 | tf_op jit(solution)/shard_map/all_to_all | solution.py:84
  136.9 0.6 copy.32
  (21 shorter events, 0.3 us)
Async XLA Ops:
  45.6 1.2 copy-start
  48.5 8.3 %copy-start.1 = (f32[40,512]{1,0:T(8,128)S(1)}, f32[40,512]{1,0:T(8,128)}, u32[]{:S(2)}) copy-start(f32[40,512]{1,0:T(8,128)} %param.6) | copy-start | bytes 245764
  48.5 8.3 %copy-start.2 = (f32[40,512]{1,0:T(8,128)S(1)}, f32[40,512]{1,0:T(8,128)}, u32[]{:S(2)}) copy-start(f32[40,512]{1,0:T(8,128)} %param.7) | copy-start | bytes 245764
  48.5 18.2 %all-to-all-start.2 = ((bf16[8,80,512]{2,1,0:T(8,128)(2,1)}), bf16[8,80,512]{2,1,0:T(8,128)(2,1)S(1)}, u32[]{:S(2)}, u32[]{:S(2)}) async-start(bf16[8,80,512]{2,1,0:T(8,128)(2,1)} %bitcast.2), calls=%async_computation.2 | async-start | bytes 1310720 | tf_op jit(solution)/shard_map/all_to_all | solution.py:58
  53.1 50.0 %collective-permute-start.1 = (bf16[1024,512]{1,0:T(8,128)(2,1)S(1)}, bf16[1024,512]{1,0:T(8,128)(2,1)S(1)}, u32[]{:S(2)}, u32[]{:S(2)}) collective-permute-start(bf16[1024,512]{1,0:T(8,128)(2,1)S(1)} %copy-done), channel_id=1, source_target_pairs={{0,1},{1,0},{2,3},{3,2},{4,5},{5,4},{6,7},{7,6},{8,9},{9,8},{10,11... | collective-permute-start | bytes 3145736 | tf_op jit(solution)/shard_map/ppermute | solution.py:35
  56.9 24.2 %collective-permute-start = (bf16[2,40,512]{2,1,0:T(8,128)(2,1)S(1)}, bf16[2,40,512]{2,1,0:T(8,128)(2,1)S(1)}, u32[]{:S(2)}, u32[]{:S(2)}) collective-permute-start(bf16[2,40,512]{2,1,0:T(8,128)(2,1)S(1)} %pad_maximum_fusion), channel_id=1, source_target_pairs={{0,64},{64,0},{1,65},{65,1},{2,66},{66,2},{3,67},{67,3},{4,68},{68... | collective-permute-start | bytes 245768 | tf_op jit(solution)/shard_map/ppermute | solution.py:35

commit v13 on v11

--- a/solution.py
+++ b/solution.py
@@ -67,11 +67,17 @@
         [jnp.where(first, share, share_other), jnp.where(first, share_other, share)], axis=0
     )
     pair = pair.reshape(2, 2, rows, -1).transpose(1, 0, 2, 3).reshape(2, 2 * rows, -1)
+    near, far = x0, 1 - x0
+    pair, near, far = lax.optimization_barrier((pair, near, far))
     pair = jnp.broadcast_to(pair[None], (4,) + pair.shape).reshape(8, 2 * rows, -1)
     pair = lax.all_to_all(pair, ("y", "x0"), 0, 0, tiled=True).reshape(4, 2, 2 * rows, -1)
     direction = lax.all_gather(pair.transpose(1, 0, 2, 3), "core").reshape(2, 2, 8 * rows, -1)
-    own = lax.dynamic_index_in_dim(direction, x0, 1, keepdims=False).reshape(16 * rows, -1)
-    away = lax.dynamic_index_in_dim(direction, 1 - x0, 1, keepdims=False).reshape(16 * rows, -1)
+    own, away = (
+        lax.dynamic_index_in_dim(
+            direction, i, 1, keepdims=False, allow_negative_indices=False
+        ).reshape(16 * rows, -1)
+        for i in (near, far)
+    )
 
     total = sum(
         lax.dot_general(d, b, (((1,), (1,)), ((), ())), preferred_element_type=F32)

time: 135 us -> 134 us (level)
  blocking collectives: 93.5 us -> 107 us
  starting transfers between devices: 25.8 us -> 18.1 us
  waiting for transfers between devices: 6.48 us -> 0.01 us
    all_to_all x0 -> x1, blocking collectives: none -> 13.9 us  [shards(): lax.all_to_all(pair, ('y', 'x0'), 0, 0, tiled=True)]
    all_to_all x1 -> x0, starting transfers between devices: 7.68 us -> none  [shards(): lax.all_to_all(pair, ('y', 'x0'), 0, 0, tiled=True)]
    all_to_all x1 -> x0, waiting for transfers between devices: 6.47 us -> none  [shards(): lax.all_to_all(pair, ('y', 'x0'), 0, 0, tiled=True)]
  transfers between devices with their start and end apart: 4 -> 3, of which waited for: 1 -> 0; matrix products, arithmetic and copies ran while one was open for 2% -> 1% of each run, Pallas kernels for 0% -> 0%
where the time goes in v13:
time: 134 us; the launch traced here: 133 us
  blocking collectives  107 us (80%)
  starting transfers between devices  18.1 us (14%)
  local copies, waits for them, and re-layouts  3.29 us (2%)
  matrix products  2.76 us (2%)
    all_to_all x2, blocking collectives, spread(): lax.all_to_all(jnp.broadcast_to(block[None], (n,) + block.shape), axes, 0...  43.9 us
    all_to_all x1, blocking collectives, shards(): total = lax.all_to_all(total, 'zf', 0, 0, tiled=True)  18.4 us
    all_to_all x1, blocking collectives, shards(): total = lax.all_to_all(total, ('zn', 'x1'), 0, 0, tiled=True)  14.4 us
    all_gather x1, blocking collectives, swap_gathered(): lax.all_gather(value, axis)  14.3 us
    all_to_all x1, blocking collectives, shards(): lax.all_to_all(pair, ('y', 'x0'), 0, 0, tiled=True)  13.9 us
    ppermute x2, starting transfers between devices, swap(): return lax.ppermute(value, axis, [(0, 1), (1, 0)])  13.5 us
    all_to_all x1, starting transfers between devices, shards(): lax.all_to_all(partial.reshape(8, 80, -1), ('y', 'core'), 0, 0, tiled=True)  4.61 us
  transfers between devices with their start and end apart: 3, of which 0 were waited for; matrix products, arithmetic and copies ran while one was open for 1% of the time, Pallas kernels for 0%

profile of v13, /device:TPU:2, one launch (start us, length us, event | category | flops | bytes accessed | tf_op | source)
XLA Modules:
  0.0 133.3 jit_solution(18217850843620404341)
XLA Ops:
  0.6 0.8 copy.20
  1.5 24.2 %all_to_all.30 = bf16[4,20,8,128]{3,2,1,0:T(8,128)(2,1)S(1)} all-to-all(bf16[4,20,8,128]{3,2,1,0:T(8,128)(2,1)S(1)} %broadcast_in_dim.9), channel_id=1, replica_groups=mesh['y'=4,'zh'=2,'core'=2,'zf'=4,'zn'=2,'x1'=2,'x0'=2] {'zf'}, dimensions={0} | all-to-all | bytes 327680 | tf_op jit(solution)/shard_map/all_to_all | solution.py:31
  25.7 0.2 broadcast_in_dim.10
  25.9 19.7 %all_to_all.31 = bf16[8,4,20,8,128]{4,3,2,1,0:T(8,128)(2,1)S(1)} all-to-all(bf16[8,4,20,8,128]{4,3,2,1,0:T(8,128)(2,1)S(1)} %broadcast_in_dim.10), channel_id=1, replica_groups=mesh['y'=4,'zh'=2,'core'=2,'zf'=4,'zn'=2,'x1'=2,'x0'=2] {'zn','x1','x0'}, dimensions={0} | all-to-all | bytes 2621440 | tf_op jit(solution)/shard_map/all_to_all | solution.py:31
  45.6 0.0 copy-start
  45.6 0.1 copy.15
  45.8 1.1 copy-done
  46.8 1.7 %convolution_convert_fusion = bf16[640,512]{1,0:T(8,128)(2,1)} fusion(bf16[1024,512]{1,0:T(8,128)(2,1)S(1)} %copy-done, bf16[80,8,8,128]{3,2,1,0:T(8,128)(2,1)S(1)} %bitcast.62), kind=kOutput, calls=%fused_computation.2 | convolution fusion | flops 671416320 | bytes 3014656 | tf_op jit(solution)/shard_map/dot_general | solution.py:53
  48.5 0.0 copy-start.1
  48.5 4.6 %all-to-all-start.2 = ((bf16[8,80,512]{2,1,0:T(8,128)(2,1)}), bf16[8,80,512]{2,1,0:T(8,128)(2,1)S(1)}, u32[]{:S(2)}, u32[]{:S(2)}) async-start(bf16[8,80,512]{2,1,0:T(8,128)(2,1)} %bitcast.2), calls=%async_computation.2 | async-start | bytes 1310720 | tf_op jit(solution)/shard_map/all_to_all | solution.py:58
  53.1 3.7 %collective-permute-start.1 = (bf16[1024,512]{1,0:T(8,128)(2,1)S(1)}, bf16[1024,512]{1,0:T(8,128)(2,1)S(1)}, u32[]{:S(2)}, u32[]{:S(2)}) collective-permute-start(bf16[1024,512]{1,0:T(8,128)(2,1)S(1)} %copy-done), channel_id=1, source_target_pairs={{0,1},{1,0},{2,3},{3,2},{4,5},{5,4},{6,7},{7,6},{8,9},{9,8},{10,11... | collective-permute-start | bytes 3145736 | tf_op jit(solution)/shard_map/ppermute | solution.py:35
  56.9 0.0 copy-done.1
  56.9 0.0 copy-done.2
  56.9 9.8 %collective-permute-start = (bf16[2,40,512]{2,1,0:T(8,128)(2,1)S(1)}, bf16[2,40,512]{2,1,0:T(8,128)(2,1)S(1)}, u32[]{:S(2)}, u32[]{:S(2)}) collective-permute-start(bf16[2,40,512]{2,1,0:T(8,128)(2,1)S(1)} %pad_maximum_fusion), channel_id=1, source_target_pairs={{0,64},{64,0},{1,65},{65,1},{2,66},{66,2},{3,67},{67,3},{4,68},{68... | collective-permute-start | bytes 245768 | tf_op jit(solution)/shard_map/ppermute | solution.py:35
  66.7 0.0 all-to-all-done.2
  66.7 0.1 convert_reduce_fusion
  66.8 14.3 %all-gather = bf16[160,512]{1,0:T(8,128)(2,1)S(1)} all-gather(bf16[80,512]{1,0:T(8,128)(2,1)S(1)} %convert_element_type.49), channel_id=2, replica_groups=mesh['y'=4,'zh'=2,'core'=2,'zf'=4,'zn'=2,'x1'=2,'x0'=2] {'zh'}, dimensions={0}, use_global_device_ids=true | all-gather | bytes 245760 | tf_op jit(solution)/shard_map/all_gather | solution.py:40
  81.1 0.0 collective-permute-done
  81.1 0.8 broadcast_select_fusion.1
  82.0 0.1 copy.16
  82.1 13.9 %all_to_all.32 = bf16[8,40,512]{2,1,0:T(8,128)(2,1)S(1)} all-to-all(bf16[8,40,512]{2,1,0:T(8,128)(2,1)S(1)} %bitcast.64), channel_id=1, replica_groups=mesh['y'=4,'zh'=2,'core'=2,'zf'=4,'zn'=2,'x1'=2,'x0'=2] {'y','x0'}, dimensions={0} | all-to-all | bytes 655360 | tf_op jit(solution)/shard_map/all_to_all | solution.py:73
  96.0 2.3 %all-gather.1 = bf16[4,4,40,512]{3,2,0,1:T(8,128)(2,1)S(1)} all-gather(bf16[2,4,40,512]{3,2,0,1:T(8,128)(2,1)S(1)} %bitcast.65), channel_id=3, replica_groups=mesh['y'=4,'zh'=2,'core'=2,'zf'=4,'zn'=2,'x1'=2,'x0'=2] {'core'}, dimensions={0}, use_global_device_ids=true | all-gather | bytes 983040 | tf_op jit(solution)/shard_map/all_gather | solution.py:74
  98.3 0.1 copy.18
  98.3 0.1 constant_dynamic-slice_fusion
  98.4 0.5 fusion.14
  98.9 0.0 collective-permute-done.1
  99.0 0.5 fusion.3
  99.5 0.1 copy.22
  99.7 14.4 %all_to_all.33 = bf16[4,4,20,8,128]{4,3,2,1,0:T(8,128)(2,1)S(1)} all-to-all(bf16[4,4,20,8,128]{4,3,2,1,0:T(8,128)(2,1)S(1)} %bitcast.61), channel_id=1, replica_groups=mesh['y'=4,'zh'=2,'core'=2,'zf'=4,'zn'=2,'x1'=2,'x0'=2] {'zn','x1'}, dimensions={0} | all-to-all | bytes 1310720 | tf_op jit(solution)/shard_map/all_to_all | solution.py:88
  114.1 0.1 reduce_sum.34
  114.2 18.4 %all_to_all.34 = bf16[4,20,8,128]{3,2,1,0:T(8,128)(2,1)S(1)} all-to-all(bf16[4,20,8,128]{3,2,1,0:T(8,128)(2,1)S(1)} %reduce_sum.34), channel_id=1, replica_groups=mesh['y'=4,'zh'=2,'core'=2,'zf'=4,'zn'=2,'x1'=2,'x0'=2] {'zf'}, dimensions={0} | all-to-all | bytes 327680 | tf_op jit(solution)/shard_map/all_to_all | solution.py:90
  132.6 0.6 copy.23
  (15 shorter events, 0.2 us)
Async XLA Ops:
  45.6 1.2 copy-start
  48.5 8.3 %copy-start.1 = (f32[40,512]{1,0:T(8,128)S(1)}, f32[40,512]{1,0:T(8,128)}, u32[]{:S(2)}) copy-start(f32[40,512]{1,0:T(8,128)} %param.6) | copy-start | bytes 245764
  48.5 8.3 %copy-start.2 = (f32[40,512]{1,0:T(8,128)S(1)}, f32[40,512]{1,0:T(8,128)}, u32[]{:S(2)}) copy-start(f32[40,512]{1,0:T(8,128)} %param.7) | copy-start | bytes 245764
  48.5 18.2 %all-to-all-start.2 = ((bf16[8,80,512]{2,1,0:T(8,128)(2,1)}), bf16[8,80,512]{2,1,0:T(8,128)(2,1)S(1)}, u32[]{:S(2)}, u32[]{:S(2)}) async-start(bf16[8,80,512]{2,1,0:T(8,128)(2,1)} %bitcast.2), calls=%async_computation.2 | async-start | bytes 1310720 | tf_op jit(solution)/shard_map/all_to_all | solution.py:58
  53.1 45.8 %collective-permute-start.1 = (bf16[1024,512]{1,0:T(8,128)(2,1)S(1)}, bf16[1024,512]{1,0:T(8,128)(2,1)S(1)}, u32[]{:S(2)}, u32[]{:S(2)}) collective-permute-start(bf16[1024,512]{1,0:T(8,128)(2,1)S(1)} %copy-done), channel_id=1, source_target_pairs={{0,1},{1,0},{2,3},{3,2},{4,5},{5,4},{6,7},{7,6},{8,9},{9,8},{10,11... | collective-permute-start | bytes 3145736 | tf_op jit(solution)/shard_map/ppermute | solution.py:35
  56.9 24.2 %collective-permute-start = (bf16[2,40,512]{2,1,0:T(8,128)(2,1)S(1)}, bf16[2,40,512]{2,1,0:T(8,128)(2,1)S(1)}, u32[]{:S(2)}, u32[]{:S(2)}) collective-permute-start(bf16[2,40,512]{2,1,0:T(8,128)(2,1)S(1)} %pad_maximum_fusion), channel_id=1, source_target_pairs={{0,64},{64,0},{1,65},{65,1},{2,66},{66,2},{3,67},{67,3},{4,68},{68... | collective-permute-start | bytes 245768 | tf_op jit(solution)/shard_map/ppermute | solution.py:35

commit v14 on v13

--- a/solution.py
+++ b/solution.py
@@ -69,9 +69,9 @@
     pair = pair.reshape(2, 2, rows, -1).transpose(1, 0, 2, 3).reshape(2, 2 * rows, -1)
     near, far = x0, 1 - x0
     pair, near, far = lax.optimization_barrier((pair, near, far))
-    pair = jnp.broadcast_to(pair[None], (4,) + pair.shape).reshape(8, 2 * rows, -1)
-    pair = lax.all_to_all(pair, ("y", "x0"), 0, 0, tiled=True).reshape(4, 2, 2 * rows, -1)
-    direction = lax.all_gather(pair.transpose(1, 0, 2, 3), "core").reshape(2, 2, 8 * rows, -1)
+    pair = jnp.broadcast_to(pair[:, None], (2, 4, 2 * rows, pair.shape[-1]))
+    pair = lax.all_to_all(pair.reshape(8, 2 * rows, -1), ("x0", "y"), 0, 0, tiled=True)
+    direction = lax.all_gather(pair.reshape(2, 8 * rows, -1), "core")
     own, away = (
         lax.dynamic_index_in_dim(
             direction, i, 1, keepdims=False, allow_negative_indices=False

time: 134 us -> 134 us (level)
  the two profiles are of different devices: /device:TPU:2 before, /device:TPU:8 now
where the time goes in v14:
time: 134 us; the launch traced here: 133 us
  blocking collectives  108 us (81%)
  starting transfers between devices  16.9 us (13%)
  local copies, waits for them, and re-layouts  3.23 us (2%)
  matrix products  2.76 us (2%)
    all_to_all x2, blocking collectives, spread(): lax.all_to_all(jnp.broadcast_to(block[None], (n,) + block.shape), axes, 0...  45.2 us
    all_to_all x1, blocking collectives, shards(): total = lax.all_to_all(total, 'zf', 0, 0, tiled=True)  18.5 us
    all_to_all x1, blocking collectives, shards(): total = lax.all_to_all(total, ('zn', 'x1'), 0, 0, tiled=True)  14.4 us
    all_to_all x1, blocking collectives, shards(): lax.all_to_all(pair.reshape(8, 2 * rows, -1), ('x0', 'y'), 0, 0, tiled=True)  13.9 us
    all_gather x1, blocking collectives, swap_gathered(): lax.all_gather(value, axis)  13.9 us
    ppermute x2, starting transfers between devices, swap(): return lax.ppermute(value, axis, [(0, 1), (1, 0)])  11.9 us
    all_to_all x1, starting transfers between devices, shards(): lax.all_to_all(partial.reshape(8, 80, -1), ('y', 'core'), 0, 0, tiled=True)  5.05 us
  transfers between devices with their start and end apart: 3, of which 0 were waited for; matrix products, arithmetic and copies ran while one was open for 1% of the time, Pallas kernels for 0%

profile of v14, /device:TPU:8, one launch (start us, length us, event | category | flops | bytes accessed | tf_op | source)
XLA Modules:
  0.0 133.1 jit_solution(11651189764427665942)
XLA Ops:
  0.6 0.8 copy.22
  1.5 24.2 %all_to_all.30 = bf16[4,20,8,128]{3,2,1,0:T(8,128)(2,1)S(1)} all-to-all(bf16[4,20,8,128]{3,2,1,0:T(8,128)(2,1)S(1)} %broadcast_in_dim.9), channel_id=1, replica_groups=mesh['y'=4,'zh'=2,'core'=2,'zf'=4,'zn'=2,'x1'=2,'x0'=2] {'zf'}, dimensions={0} | all-to-all | bytes 327680 | tf_op jit(solution)/shard_map/all_to_all | solution.py:31
  25.7 0.2 broadcast_in_dim.10
  25.9 21.0 %all_to_all.31 = bf16[8,4,20,8,128]{4,3,2,1,0:T(8,128)(2,1)S(1)} all-to-all(bf16[8,4,20,8,128]{4,3,2,1,0:T(8,128)(2,1)S(1)} %broadcast_in_dim.10), channel_id=1, replica_groups=mesh['y'=4,'zh'=2,'core'=2,'zf'=4,'zn'=2,'x1'=2,'x0'=2] {'zn','x1','x0'}, dimensions={0} | all-to-all | bytes 2621440 | tf_op jit(solution)/shard_map/all_to_all | solution.py:31
  46.9 0.0 copy-start
  46.9 0.1 copy.18
  47.0 1.1 copy-done
  48.1 1.7 %convolution_convert_fusion = bf16[640,512]{1,0:T(8,128)(2,1)} fusion(bf16[1024,512]{1,0:T(8,128)(2,1)S(1)} %copy-done, bf16[80,8,8,128]{3,2,1,0:T(8,128)(2,1)S(1)} %bitcast.58), kind=kOutput, calls=%fused_computation.2 | convolution fusion | flops 671416320 | bytes 3014656 | tf_op jit(solution)/shard_map/dot_general | solution.py:53
  49.8 0.0 copy-start.1
  49.8 0.0 copy-start.2
  49.8 5.0 %all-to-all-start.2 = ((bf16[8,80,512]{2,1,0:T(8,128)(2,1)}), bf16[8,80,512]{2,1,0:T(8,128)(2,1)S(1)}, u32[]{:S(2)}, u32[]{:S(2)}) async-start(bf16[8,80,512]{2,1,0:T(8,128)(2,1)} %bitcast.2), calls=%async_computation.2 | async-start | bytes 1310720 | tf_op jit(solution)/shard_map/all_to_all | solution.py:58
  54.9 2.1 %collective-permute-start.1 = (bf16[1024,512]{1,0:T(8,128)(2,1)S(1)}, bf16[1024,512]{1,0:T(8,128)(2,1)S(1)}, u32[]{:S(2)}, u32[]{:S(2)}) collective-permute-start(bf16[1024,512]{1,0:T(8,128)(2,1)S(1)} %copy-done), channel_id=1, source_target_pairs={{0,1},{1,0},{2,3},{3,2},{4,5},{5,4},{6,7},{7,6},{8,9},{9,8},{10,11... | collective-permute-start | bytes 3145736 | tf_op jit(solution)/shard_map/ppermute | solution.py:35
  57.0 0.0 copy-done.1
  57.0 0.0 copy-done.2
  57.0 9.8 %collective-permute-start = (bf16[2,40,512]{2,1,0:T(8,128)(2,1)S(1)}, bf16[2,40,512]{2,1,0:T(8,128)(2,1)S(1)}, u32[]{:S(2)}, u32[]{:S(2)}) collective-permute-start(bf16[2,40,512]{2,1,0:T(8,128)(2,1)S(1)} %pad_maximum_fusion), channel_id=1, source_target_pairs={{0,64},{64,0},{1,65},{65,1},{2,66},{66,2},{3,67},{67,3},{4,68},{68... | collective-permute-start | bytes 245768 | tf_op jit(solution)/shard_map/ppermute | solution.py:35
  66.8 0.0 all-to-all-done.2
  66.8 0.1 convert_reduce_fusion
  67.0 13.9 %all-gather = bf16[160,512]{1,0:T(8,128)(2,1)S(1)} all-gather(bf16[80,512]{1,0:T(8,128)(2,1)S(1)} %convert_element_type.49), channel_id=2, replica_groups=mesh['y'=4,'zh'=2,'core'=2,'zf'=4,'zn'=2,'x1'=2,'x0'=2] {'zh'}, dimensions={0}, use_global_device_ids=true | all-gather | bytes 245760 | tf_op jit(solution)/shard_map/all_gather | solution.py:40
  80.9 0.0 collective-permute-done
  80.9 0.8 broadcast_select_fusion.1
  81.7 0.1 copy.19
  81.8 13.9 %all_to_all.32 = bf16[8,40,512]{2,1,0:T(8,128)(2,1)S(1)} all-to-all(bf16[8,40,512]{2,1,0:T(8,128)(2,1)S(1)} %bitcast.60), channel_id=1, replica_groups=mesh['y'=4,'zh'=2,'core'=2,'zf'=4,'zn'=2,'x1'=2,'x0'=2] {'x0','y'}, dimensions={0} | all-to-all | bytes 655360 | tf_op jit(solution)/shard_map/all_to_all | solution.py:73
  95.8 2.3 %all_gather.8 = bf16[2,2,160,512]{3,2,1,0:T(8,128)(2,1)S(1)} all-gather(bf16[1,2,160,512]{3,2,1,0:T(8,128)(2,1)S(1)} %bitcast.61), channel_id=1, replica_groups=mesh['y'=4,'zh'=2,'core'=2,'zf'=4,'zn'=2,'x1'=2,'x0'=2] {'core'}, dimensions={0}, use_global_device_ids=true | all-gather | bytes 983040 | tf_op jit(solution)/shard_map/all_gather | solution.py:74
  98.1 0.5 fusion.14
  98.6 0.0 collective-permute-done.1
  98.6 0.5 fusion.3
  99.2 0.1 copy.24
  99.4 14.4 %all_to_all.33 = bf16[4,4,20,8,128]{4,3,2,1,0:T(8,128)(2,1)S(1)} all-to-all(bf16[4,4,20,8,128]{4,3,2,1,0:T(8,128)(2,1)S(1)} %bitcast.57), channel_id=1, replica_groups=mesh['y'=4,'zh'=2,'core'=2,'zf'=4,'zn'=2,'x1'=2,'x0'=2] {'zn','x1'}, dimensions={0} | all-to-all | bytes 1310720 | tf_op jit(solution)/shard_map/all_to_all | solution.py:88
  113.8 0.1 reduce_sum.34
  113.9 18.5 %all_to_all.34 = bf16[4,20,8,128]{3,2,1,0:T(8,128)(2,1)S(1)} all-to-all(bf16[4,20,8,128]{3,2,1,0:T(8,128)(2,1)S(1)} %reduce_sum.34), channel_id=1, replica_groups=mesh['y'=4,'zh'=2,'core'=2,'zf'=4,'zn'=2,'x1'=2,'x0'=2] {'zf'}, dimensions={0} | all-to-all | bytes 327680 | tf_op jit(solution)/shard_map/all_to_all | solution.py:90
  132.5 0.6 copy.25
  (15 shorter events, 0.3 us)
Async XLA Ops:
  46.9 1.2 copy-start
  49.8 7.2 %copy-start.1 = (f32[40,512]{1,0:T(8,128)S(1)}, f32[40,512]{1,0:T(8,128)}, u32[]{:S(2)}) copy-start(f32[40,512]{1,0:T(8,128)} %param.6) | copy-start | bytes 245764
  49.8 7.2 %copy-start.2 = (f32[40,512]{1,0:T(8,128)S(1)}, f32[40,512]{1,0:T(8,128)}, u32[]{:S(2)}) copy-start(f32[40,512]{1,0:T(8,128)} %param.7) | copy-start | bytes 245764
  49.8 17.0 %all-to-all-start.2 = ((bf16[8,80,512]{2,1,0:T(8,128)(2,1)}), bf16[8,80,512]{2,1,0:T(8,128)(2,1)S(1)}, u32[]{:S(2)}, u32[]{:S(2)}) async-start(bf16[8,80,512]{2,1,0:T(8,128)(2,1)} %bitcast.2), calls=%async_computation.2 | async-start | bytes 1310720 | tf_op jit(solution)/shard_map/all_to_all | solution.py:58
  54.9 43.8 %collective-permute-start.1 = (bf16[1024,512]{1,0:T(8,128)(2,1)S(1)}, bf16[1024,512]{1,0:T(8,128)(2,1)S(1)}, u32[]{:S(2)}, u32[]{:S(2)}) collective-permute-start(bf16[1024,512]{1,0:T(8,128)(2,1)S(1)} %copy-done), channel_id=1, source_target_pairs={{0,1},{1,0},{2,3},{3,2},{4,5},{5,4},{6,7},{7,6},{8,9},{9,8},{10,11... | collective-permute-start | bytes 3145736 | tf_op jit(solution)/shard_map/ppermute | solution.py:35
  57.0 23.8 %collective-permute-start = (bf16[2,40,512]{2,1,0:T(8,128)(2,1)S(1)}, bf16[2,40,512]{2,1,0:T(8,128)(2,1)S(1)}, u32[]{:S(2)}, u32[]{:S(2)}) collective-permute-start(bf16[2,40,512]{2,1,0:T(8,128)(2,1)S(1)} %pad_maximum_fusion), channel_id=1, source_target_pairs={{0,64},{64,0},{1,65},{65,1},{2,66},{66,2},{3,67},{67,3},{4,68},{68... | collective-permute-start | bytes 245768 | tf_op jit(solution)/shard_map/ppermute | solution.py:35

commit v15 on v14

--- a/solution.py
+++ b/solution.py
@@ -46,11 +46,10 @@
     rows, cols = grad.shape
     block = grad.reshape(rows, cols // LANES, LANES)
     block = spread(block, "zf", 4)
-    block = spread(block, ("zn", "x1", "x0"), 8)
-    block = block.reshape(2, 2, 2, 4, rows, cols // LANES, LANES)
-    picked = block.transpose(3, 1, 0, 2, 4, 5, 6).reshape(32 * rows, cols)
-
-    partial = jnp.dot(picked, basis, preferred_element_type=F32).astype(BF16)
+    block = spread(block.reshape(4 * rows, cols), ("zn", "x1", "x0"), 8)
+    partial = jnp.dot(block.reshape(32 * rows, cols), basis, preferred_element_type=F32)
+    partial = partial.astype(BF16).reshape(2, 2, 2, 4, rows, -1)
+    partial = partial.transpose(3, 1, 0, 2, 4, 5).reshape(32 * rows, -1)
     partial, *sent = lax.optimization_barrier((partial, first_moment, second_moment))
     basis_next = swap(basis, "x0")
     moments = swap(jnp.stack(sent).astype(BF16), "zh")

time: 134 us -> 133 us (level)
  no operation moved by 1% of the time
where the time goes in v15:
time: 133 us; the launch traced here: 132 us
  blocking collectives  108 us (81%)
  starting transfers between devices  16.8 us (13%)
  local copies, waits for them, and re-layouts  3.18 us (2%)
  matrix products  1.92 us (1%)
    all_to_all x2, blocking collectives, spread(): lax.all_to_all(jnp.broadcast_to(block[None], (n,) + block.shape), axes, 0...  45.3 us
    all_to_all x1, blocking collectives, shards(): total = lax.all_to_all(total, 'zf', 0, 0, tiled=True)  18.5 us
    all_to_all x1, blocking collectives, shards(): total = lax.all_to_all(total, ('zn', 'x1'), 0, 0, tiled=True)  14.4 us
    all_to_all x1, blocking collectives, shards(): lax.all_to_all(pair.reshape(8, 2 * rows, -1), ('x0', 'y'), 0, 0, tiled=True)  13.9 us
    all_gather x1, blocking collectives, swap_gathered(): lax.all_gather(value, axis)  13.9 us
    ppermute x2, starting transfers between devices, swap(): return lax.ppermute(value, axis, [(0, 1), (1, 0)])  11.9 us
    all_to_all x1, starting transfers between devices, shards(): lax.all_to_all(partial.reshape(8, 80, -1), ('y', 'core'), 0, 0, tiled=True)  4.92 us
  transfers between devices with their start and end apart: 3, of which 0 were waited for; matrix products, arithmetic and copies ran while one was open for 1% of the time, Pallas kernels for 0%

profile of v15, /device:TPU:8, one launch (start us, length us, event | category | flops | bytes accessed | tf_op | source)
XLA Modules:
  0.0 132.2 jit_solution(11332885417121606413)
XLA Ops:
  0.6 0.8 copy.19
  1.5 24.2 %all_to_all.30 = bf16[4,20,8,128]{3,2,1,0:T(8,128)(2,1)S(1)} all-to-all(bf16[4,20,8,128]{3,2,1,0:T(8,128)(2,1)S(1)} %broadcast_in_dim.21), channel_id=1, replica_groups=mesh['y'=4,'zh'=2,'core'=2,'zf'=4,'zn'=2,'x1'=2,'x0'=2] {'zf'}, dimensions={0} | all-to-all | bytes 327680 | tf_op jit(solution)/shard_map/all_to_all | solution.py:31
  25.8 0.1 broadcast_in_dim.23
  25.9 0.0 copy-start
  25.9 21.1 %all_to_all.31 = bf16[8,80,1024]{2,1,0:T(8,128)(2,1)S(1)} all-to-all(bf16[8,80,1024]{2,1,0:T(8,128)(2,1)S(1)} %broadcast_in_dim.23), channel_id=1, replica_groups=mesh['y'=4,'zh'=2,'core'=2,'zf'=4,'zn'=2,'x1'=2,'x0'=2] {'zn','x1','x0'}, dimensions={0} | all-to-all | bytes 2621440 | tf_op jit(solution)/shard_map/all_to_all | solution.py:31
  47.0 0.8 convolution_convert_fusion
  47.9 0.1 reshape.64
  48.0 0.1 copy.15
  48.1 0.0 copy-start.1
  48.1 0.0 copy-start.2
  48.1 1.0 reshape.65
  49.1 4.9 %all-to-all-start.2 = ((bf16[8,80,512]{2,1,0:T(8,128)(2,1)}), bf16[8,80,512]{2,1,0:T(8,128)(2,1)S(1)}, u32[]{:S(2)}, u32[]{:S(2)}) async-start(bf16[8,80,512]{2,1,0:T(8,128)(2,1)} %bitcast.2), calls=%async_computation.2 | async-start | bytes 1310720 | tf_op jit(solution)/shard_map/all_to_all | solution.py:57
  54.0 2.1 %collective-permute-start.1 = (bf16[1024,512]{1,0:T(8,128)(2,1)S(1)}, bf16[1024,512]{1,0:T(8,128)(2,1)S(1)}, u32[]{:S(2)}, u32[]{:S(2)}) collective-permute-start(bf16[1024,512]{1,0:T(8,128)(2,1)S(1)} %copy-done), channel_id=1, source_target_pairs={{0,1},{1,0},{2,3},{3,2},{4,5},{5,4},{6,7},{7,6},{8,9},{9,8},{10,11... | collective-permute-start | bytes 3145736 | tf_op jit(solution)/shard_map/ppermute | solution.py:35
  56.1 0.0 copy-done.1
  56.1 0.0 copy-done.2
  56.2 9.8 %collective-permute-start = (bf16[2,40,512]{2,1,0:T(8,128)(2,1)S(1)}, bf16[2,40,512]{2,1,0:T(8,128)(2,1)S(1)}, u32[]{:S(2)}, u32[]{:S(2)}) collective-permute-start(bf16[2,40,512]{2,1,0:T(8,128)(2,1)S(1)} %pad_maximum_fusion), channel_id=1, source_target_pairs={{0,64},{64,0},{1,65},{65,1},{2,66},{66,2},{3,67},{67,3},{4,68},{68... | collective-permute-start | bytes 245768 | tf_op jit(solution)/shard_map/ppermute | solution.py:35
  66.0 0.0 all-to-all-done.2
  66.0 0.1 convert_reduce_fusion
  66.1 13.9 %all-gather = bf16[160,512]{1,0:T(8,128)(2,1)S(1)} all-gather(bf16[80,512]{1,0:T(8,128)(2,1)S(1)} %convert_element_type.49), channel_id=2, replica_groups=mesh['y'=4,'zh'=2,'core'=2,'zf'=4,'zn'=2,'x1'=2,'x0'=2] {'zh'}, dimensions={0}, use_global_device_ids=true | all-gather | bytes 245760 | tf_op jit(solution)/shard_map/all_gather | solution.py:40
  80.0 0.0 collective-permute-done
  80.0 0.8 broadcast_select_fusion.1
  80.9 0.1 copy.16
  81.0 13.9 %all_to_all.32 = bf16[8,40,512]{2,1,0:T(8,128)(2,1)S(1)} all-to-all(bf16[8,40,512]{2,1,0:T(8,128)(2,1)S(1)} %bitcast.60), channel_id=1, replica_groups=mesh['y'=4,'zh'=2,'core'=2,'zf'=4,'zn'=2,'x1'=2,'x0'=2] {'x0','y'}, dimensions={0} | all-to-all | bytes 655360 | tf_op jit(solution)/shard_map/all_to_all | solution.py:72
  94.9 2.3 %all_gather.8 = bf16[2,2,160,512]{3,2,1,0:T(8,128)(2,1)S(1)} all-gather(bf16[1,2,160,512]{3,2,1,0:T(8,128)(2,1)S(1)} %bitcast.61), channel_id=1, replica_groups=mesh['y'=4,'zh'=2,'core'=2,'zf'=4,'zn'=2,'x1'=2,'x0'=2] {'core'}, dimensions={0}, use_global_device_ids=true | all-gather | bytes 983040 | tf_op jit(solution)/shard_map/all_gather | solution.py:73
  97.2 0.5 fusion.12
  97.8 0.0 collective-permute-done.1
  97.8 0.5 fusion.1
  98.3 0.1 copy.21
  98.5 14.4 %all_to_all.33 = bf16[4,4,20,8,128]{4,3,2,1,0:T(8,128)(2,1)S(1)} all-to-all(bf16[4,4,20,8,128]{4,3,2,1,0:T(8,128)(2,1)S(1)} %bitcast.57), channel_id=1, replica_groups=mesh['y'=4,'zh'=2,'core'=2,'zf'=4,'zn'=2,'x1'=2,'x0'=2] {'zn','x1'}, dimensions={0} | all-to-all | bytes 1310720 | tf_op jit(solution)/shard_map/all_to_all | solution.py:87
  112.9 0.1 reduce_sum.34
  113.0 18.5 %all_to_all.34 = bf16[4,20,8,128]{3,2,1,0:T(8,128)(2,1)S(1)} all-to-all(bf16[4,20,8,128]{3,2,1,0:T(8,128)(2,1)S(1)} %reduce_sum.34), channel_id=1, replica_groups=mesh['y'=4,'zh'=2,'core'=2,'zf'=4,'zn'=2,'x1'=2,'x0'=2] {'zf'}, dimensions={0} | all-to-all | bytes 327680 | tf_op jit(solution)/shard_map/all_to_all | solution.py:89
  131.6 0.6 copy.22
  (17 shorter events, 0.3 us)
Async XLA Ops:
  25.9 21.1 %copy-start = (bf16[1024,512]{1,0:T(8,128)(2,1)S(1)}, bf16[1024,512]{1,0:T(8,128)(2,1)}, u32[]{:S(2)}) copy-start(bf16[1024,512]{1,0:T(8,128)(2,1)} %param.5) | copy-start | bytes 3145732
  48.1 8.0 %copy-start.1 = (f32[40,512]{1,0:T(8,128)S(1)}, f32[40,512]{1,0:T(8,128)}, u32[]{:S(2)}) copy-start(f32[40,512]{1,0:T(8,128)} %param.6) | copy-start | bytes 245764
  48.1 8.0 %copy-start.2 = (f32[40,512]{1,0:T(8,128)S(1)}, f32[40,512]{1,0:T(8,128)}, u32[]{:S(2)}) copy-start(f32[40,512]{1,0:T(8,128)} %param.7) | copy-start | bytes 245764
  49.1 16.9 %all-to-all-start.2 = ((bf16[8,80,512]{2,1,0:T(8,128)(2,1)}), bf16[8,80,512]{2,1,0:T(8,128)(2,1)S(1)}, u32[]{:S(2)}, u32[]{:S(2)}) async-start(bf16[8,80,512]{2,1,0:T(8,128)(2,1)} %bitcast.2), calls=%async_computation.2 | async-start | bytes 1310720 | tf_op jit(solution)/shard_map/all_to_all | solution.py:57
  54.0 43.8 %collective-permute-start.1 = (bf16[1024,512]{1,0:T(8,128)(2,1)S(1)}, bf16[1024,512]{1,0:T(8,128)(2,1)S(1)}, u32[]{:S(2)}, u32[]{:S(2)}) collective-permute-start(bf16[1024,512]{1,0:T(8,128)(2,1)S(1)} %copy-done), channel_id=1, source_target_pairs={{0,1},{1,0},{2,3},{3,2},{4,5},{5,4},{6,7},{7,6},{8,9},{9,8},{10,11... | collective-permute-start | bytes 3145736 | tf_op jit(solution)/shard_map/ppermute | solution.py:35
  56.2 23.8 %collective-permute-start = (bf16[2,40,512]{2,1,0:T(8,128)(2,1)S(1)}, bf16[2,40,512]{2,1,0:T(8,128)(2,1)S(1)}, u32[]{:S(2)}, u32[]{:S(2)}) collective-permute-start(bf16[2,40,512]{2,1,0:T(8,128)(2,1)S(1)} %pad_maximum_fusion), channel_id=1, source_target_pairs={{0,64},{64,0},{1,65},{65,1},{2,66},{66,2},{3,67},{67,3},{4,68},{68... | collective-permute-start | bytes 245768 | tf_op jit(solution)/shard_map/ppermute | solution.py:35

commit v16 on v15

--- a/solution.py
+++ b/solution.py
@@ -48,8 +48,8 @@
     block = spread(block, "zf", 4)
     block = spread(block.reshape(4 * rows, cols), ("zn", "x1", "x0"), 8)
     partial = jnp.dot(block.reshape(32 * rows, cols), basis, preferred_element_type=F32)
-    partial = partial.astype(BF16).reshape(2, 2, 2, 4, rows, -1)
-    partial = partial.transpose(3, 1, 0, 2, 4, 5).reshape(32 * rows, -1)
+    partial = partial.reshape(2, 2, 2, 4, rows, -1)
+    partial = partial.transpose(3, 1, 0, 2, 4, 5).reshape(32 * rows, -1).astype(BF16)
     partial, *sent = lax.optimization_barrier((partial, first_moment, second_moment))
     basis_next = swap(basis, "x0")
     moments = swap(jnp.stack(sent).astype(BF16), "zh")

time: 133 us -> 134 us (level)
  matrix products: 1.92 us -> 3.3 us
    dot_general x1, matrix products: 0.84 us -> 2.22 us  [shards(): jnp.dot(block.reshape(32 * rows, cols), basis, preferred_element_type=F32)]
where the time goes in v16:
time: 134 us
  blocking collectives  108 us (81%)
  starting transfers between devices  16.8 us (13%)
  local copies, waits for them, and re-layouts  3.34 us (2%)
  matrix products  3.3 us (2%)
    all_to_all x2, blocking collectives, spread(): lax.all_to_all(jnp.broadcast_to(block[None], (n,) + block.shape), axes, 0...  45.2 us
    all_to_all x1, blocking collectives, shards(): total = lax.all_to_all(total, 'zf', 0, 0, tiled=True)  18.5 us
    all_to_all x1, blocking collectives, shards(): total = lax.all_to_all(total, ('zn', 'x1'), 0, 0, tiled=True)  14.4 us
    all_to_all x1, blocking collectives, shards(): lax.all_to_all(pair.reshape(8, 2 * rows, -1), ('x0', 'y'), 0, 0, tiled=True)  14 us
    all_gather x1, blocking collectives, swap_gathered(): lax.all_gather(value, axis)  13.9 us
    ppermute x2, starting transfers between devices, swap(): return lax.ppermute(value, axis, [(0, 1), (1, 0)])  11.9 us
    all_to_all x1, starting transfers between devices, shards(): lax.all_to_all(partial.reshape(8, 80, -1), ('y', 'core'), 0, 0, tiled=True)  4.92 us
  transfers between devices with their start and end apart: 3, of which 0 were waited for; matrix products, arithmetic and copies ran while one was open for 1% of the time, Pallas kernels for 0%

profile of v16, /device:TPU:8, one launch (start us, length us, event | category | flops | bytes accessed | tf_op | source)
XLA Modules:
  0.0 133.6 jit_solution(877057149012506401)
XLA Ops:
  0.6 0.8 copy.26
  1.5 24.2 %all_to_all.30 = bf16[4,20,8,128]{3,2,1,0:T(8,128)(2,1)S(1)} all-to-all(bf16[4,20,8,128]{3,2,1,0:T(8,128)(2,1)S(1)} %broadcast_in_dim.21), channel_id=1, replica_groups=mesh['y'=4,'zh'=2,'core'=2,'zf'=4,'zn'=2,'x1'=2,'x0'=2] {'zf'}, dimensions={0} | all-to-all | bytes 327680 | tf_op jit(solution)/shard_map/all_to_all | solution.py:31
  25.8 0.1 broadcast_in_dim.23
  25.9 21.0 %all_to_all.31 = bf16[8,80,1024]{2,1,0:T(8,128)(2,1)S(1)} all-to-all(bf16[8,80,1024]{2,1,0:T(8,128)(2,1)S(1)} %broadcast_in_dim.23), channel_id=1, replica_groups=mesh['y'=4,'zh'=2,'core'=2,'zf'=4,'zn'=2,'x1'=2,'x0'=2] {'zn','x1','x0'}, dimensions={0} | all-to-all | bytes 2621440 | tf_op jit(solution)/shard_map/all_to_all | solution.py:31
  46.9 0.3 reshape.72
  47.2 2.2 %fusion.1 = bf16[4,2,2,2,20,512]{5,4,0,3,1,2:T(8,128)(2,1)S(1)} fusion(bf16[2,2,2,4,20,1024]{5,4,3,2,1,0:T(8,128)(2,1)S(1)} %reshape.72, bf16[1024,512]{1,0:T(8,128)(2,1)} %param.5), kind=kOutput, calls=%fused_computation.4 | convolution fusion | flops 671416320 | bytes 3014656 | tf_op jit(solution)/shard_map/dot_general | solution.py:50
  49.4 0.1 copy.20
  49.5 0.0 copy-start
  49.5 0.0 copy-start.1
  49.5 0.0 copy-start.2
  49.5 1.0 convert_element_type.55
  50.5 4.9 %all-to-all-start.2 = ((bf16[8,80,512]{2,1,0:T(8,128)(2,1)}), bf16[8,80,512]{2,1,0:T(8,128)(2,1)S(1)}, u32[]{:S(2)}, u32[]{:S(2)}) async-start(bf16[8,80,512]{2,1,0:T(8,128)(2,1)} %bitcast.3), calls=%async_computation.2 | async-start | bytes 1310720 | tf_op jit(solution)/shard_map/all_to_all | solution.py:57
  55.4 0.0 copy-done
  55.4 2.1 %collective-permute-start.1 = (bf16[1024,512]{1,0:T(8,128)(2,1)S(1)}, bf16[1024,512]{1,0:T(8,128)(2,1)S(1)}, u32[]{:S(2)}, u32[]{:S(2)}) collective-permute-start(bf16[1024,512]{1,0:T(8,128)(2,1)S(1)} %copy-done), channel_id=1, source_target_pairs={{0,1},{1,0},{2,3},{3,2},{4,5},{5,4},{6,7},{7,6},{8,9},{9,8},{10,11... | collective-permute-start | bytes 3145736 | tf_op jit(solution)/shard_map/ppermute | solution.py:35
  57.6 0.0 copy-done.1
  57.6 9.8 %collective-permute-start = (bf16[2,40,512]{2,1,0:T(8,128)(2,1)S(1)}, bf16[2,40,512]{2,1,0:T(8,128)(2,1)S(1)}, u32[]{:S(2)}, u32[]{:S(2)}) collective-permute-start(bf16[2,40,512]{2,1,0:T(8,128)(2,1)S(1)} %pad_maximum_fusion), channel_id=1, source_target_pairs={{0,64},{64,0},{1,65},{65,1},{2,66},{66,2},{3,67},{67,3},{4,68},{68... | collective-permute-start | bytes 245768 | tf_op jit(solution)/shard_map/ppermute | solution.py:35
  67.4 0.0 all-to-all-done.2
  67.4 0.1 convert_reduce_fusion
  67.5 13.9 %all-gather = bf16[160,512]{1,0:T(8,128)(2,1)S(1)} all-gather(bf16[80,512]{1,0:T(8,128)(2,1)S(1)} %convert_element_type.57), channel_id=2, replica_groups=mesh['y'=4,'zh'=2,'core'=2,'zf'=4,'zn'=2,'x1'=2,'x0'=2] {'zh'}, dimensions={0}, use_global_device_ids=true | all-gather | bytes 245760 | tf_op jit(solution)/shard_map/all_gather | solution.py:40
  81.4 0.0 collective-permute-done
  81.4 0.8 broadcast_select_fusion.1
  82.3 0.1 copy.21
  82.4 14.0 %all_to_all.32 = bf16[8,40,512]{2,1,0:T(8,128)(2,1)S(1)} all-to-all(bf16[8,40,512]{2,1,0:T(8,128)(2,1)S(1)} %bitcast.62), channel_id=1, replica_groups=mesh['y'=4,'zh'=2,'core'=2,'zf'=4,'zn'=2,'x1'=2,'x0'=2] {'x0','y'}, dimensions={0} | all-to-all | bytes 655360 | tf_op jit(solution)/shard_map/all_to_all | solution.py:72
  96.4 2.3 %all_gather.8 = bf16[2,2,160,512]{3,2,1,0:T(8,128)(2,1)S(1)} all-gather(bf16[1,2,160,512]{3,2,1,0:T(8,128)(2,1)S(1)} %bitcast.63), channel_id=1, replica_groups=mesh['y'=4,'zh'=2,'core'=2,'zf'=4,'zn'=2,'x1'=2,'x0'=2] {'core'}, dimensions={0}, use_global_device_ids=true | all-gather | bytes 983040 | tf_op jit(solution)/shard_map/all_gather | solution.py:73
  98.7 0.5 fusion.14
  99.2 0.0 collective-permute-done.1
  99.2 0.5 fusion.2
  99.8 0.1 copy.28
  100.0 14.4 %all_to_all.33 = bf16[4,4,20,8,128]{4,3,2,1,0:T(8,128)(2,1)S(1)} all-to-all(bf16[4,4,20,8,128]{4,3,2,1,0:T(8,128)(2,1)S(1)} %bitcast.60), channel_id=1, replica_groups=mesh['y'=4,'zh'=2,'core'=2,'zf'=4,'zn'=2,'x1'=2,'x0'=2] {'zn','x1'}, dimensions={0} | all-to-all | bytes 1310720 | tf_op jit(solution)/shard_map/all_to_all | solution.py:87
  114.4 0.1 reduce_sum.34
  114.5 18.5 %all_to_all.34 = bf16[4,20,8,128]{3,2,1,0:T(8,128)(2,1)S(1)} all-to-all(bf16[4,20,8,128]{3,2,1,0:T(8,128)(2,1)S(1)} %reduce_sum.34), channel_id=1, replica_groups=mesh['y'=4,'zh'=2,'core'=2,'zf'=4,'zn'=2,'x1'=2,'x0'=2] {'zf'}, dimensions={0} | all-to-all | bytes 327680 | tf_op jit(solution)/shard_map/all_to_all | solution.py:89
  133.0 0.6 copy.29
  (17 shorter events, 0.3 us)
Async XLA Ops:
  49.5 5.9 %copy-start = (bf16[1024,512]{1,0:T(8,128)(2,1)S(1)}, bf16[1024,512]{1,0:T(8,128)(2,1)}, u32[]{:S(2)}) copy-start(bf16[1024,512]{1,0:T(8,128)(2,1)} %param.5) | copy-start | bytes 3145732
  49.5 8.0 %copy-start.1 = (f32[40,512]{1,0:T(8,128)S(1)}, f32[40,512]{1,0:T(8,128)}, u32[]{:S(2)}) copy-start(f32[40,512]{1,0:T(8,128)} %param.6) | copy-start | bytes 245764
  49.5 8.0 %copy-start.2 = (f32[40,512]{1,0:T(8,128)S(1)}, f32[40,512]{1,0:T(8,128)}, u32[]{:S(2)}) copy-start(f32[40,512]{1,0:T(8,128)} %param.7) | copy-start | bytes 245764
  50.5 16.9 %all-to-all-start.2 = ((bf16[8,80,512]{2,1,0:T(8,128)(2,1)}), bf16[8,80,512]{2,1,0:T(8,128)(2,1)S(1)}, u32[]{:S(2)}, u32[]{:S(2)}) async-start(bf16[8,80,512]{2,1,0:T(8,128)(2,1)} %bitcast.3), calls=%async_computation.2 | async-start | bytes 1310720 | tf_op jit(solution)/shard_map/all_to_all | solution.py:57
  55.4 43.8 %collective-permute-start.1 = (bf16[1024,512]{1,0:T(8,128)(2,1)S(1)}, bf16[1024,512]{1,0:T(8,128)(2,1)S(1)}, u32[]{:S(2)}, u32[]{:S(2)}) collective-permute-start(bf16[1024,512]{1,0:T(8,128)(2,1)S(1)} %copy-done), channel_id=1, source_target_pairs={{0,1},{1,0},{2,3},{3,2},{4,5},{5,4},{6,7},{7,6},{8,9},{9,8},{10,11... | collective-permute-start | bytes 3145736 | tf_op jit(solution)/shard_map/ppermute | solution.py:35
  57.6 23.8 %collective-permute-start = (bf16[2,40,512]{2,1,0:T(8,128)(2,1)S(1)}, bf16[2,40,512]{2,1,0:T(8,128)(2,1)S(1)}, u32[]{:S(2)}, u32[]{:S(2)}) collective-permute-start(bf16[2,40,512]{2,1,0:T(8,128)(2,1)S(1)} %pad_maximum_fusion), channel_id=1, source_target_pairs={{0,64},{64,0},{1,65},{65,1},{2,66},{66,2},{3,67},{67,3},{4,68},{68... | collective-permute-start | bytes 245768 | tf_op jit(solution)/shard_map/ppermute | solution.py:35
